TPU v7x, 32 devices: a whole 2x2x4 slice. The times are simulated.
32 devices in a mesh: node: 8 (over z, y), head: 4 (over x, core).
Axes of the slice: x: 2, y: 2, z: 4, core: 2. Of those that a mesh axis runs over, the one named last changes fastest.
Arguments:
- features: bfloat16 [16384, 256], P(('node', 'head')), may hold values from -40 to 40
- in_weight: bfloat16 [256, 768], replicated, may hold values from -0.6 to 0.6
- out_weight: bfloat16 [256, 256], replicated, may hold values from -0.375 to 0.375
- cotangent: bfloat16 [16384, 256], P(('node', 'head')), may hold values from -6 to 6
- key_slots: int32 [128, 12], P('node'), may hold values from 0 to 31, as said below
- block_count: int32 [128], P('node'), may hold values from 1 to 12
- wanted: int32 [8, 8, 2], P('node'), may hold values from 0 to 15
Outputs:
- output: bfloat16 [16384, 256], P(('node', 'head'))
- feature_grad: bfloat16 [16384, 256], P(('node', 'head'))
- in_weight_grad: float32 [256, 768], P(None, 'head')
- out_weight_grad: float32 [256, 256], P('head')
Inputs may be any that keep to these rules, and one draw needn't show every extreme that they name: `key_slots`: slot 0 of a query block names the block itself; the slots of one query block are distinct.
All inputs are finite; a program needn't handle non-finite values.
Results may differ from a plain program's by a relative error of at most 0.02.
The roundings to bfloat16 on the way count: a program that leaves them out, or rounds other values in their place, can miss the bound.
Values may be sent and summed in bfloat16 or wider, within the bound.
No kernel may reach another device: no remote copies, remote signals or barrier semaphores. Data moves between devices by JAX's collectives and lax.ppermute only.
A program may use at most 128 MiB of HBM per device.

v0:
```python
import functools
import math

import jax
import jax.numpy as jnp
from jax import lax
from jax.experimental import pallas as pl
from jax.experimental.pallas import tpu as pltpu
from jax.sharding import PartitionSpec as P

HEADS = 4
HD = 64
BLOCK = 128
BLK = 16
PER = 12
CAP = 2
D = 256
PAIRS = BLK // 2
SCALE = HD ** (-0.5)
SCALE_LOG2E = SCALE * math.log2(math.e)
BF16 = jnp.bfloat16
F32 = jnp.float32
MIB = 1 << 20
LAST = (((1,), (1,)), ((), ()))


def dot(a, b):
    return jnp.dot(a, b, preferred_element_type=F32)


def dot_last(a, b):
    return lax.dot_general(a, b, LAST, preferred_element_type=F32)


def span(start, size):
    return pl.ds(pl.multiple_of(start, size), size)


def smem():
    return pl.BlockSpec(memory_space=pltpu.SMEM)


def vmem():
    return pl.BlockSpec(memory_space=pltpu.VMEM)


def hbm():
    return pl.BlockSpec(memory_space=pltpu.HBM)


def call(kernel, name, outs, in_specs, limit, flops=0, scratch=(), out_specs=None):
    return pl.pallas_call(
        kernel,
        name=name,
        out_shape=tuple(jax.ShapeDtypeStruct(shape, kind) for shape, kind in outs),
        in_specs=in_specs,
        out_specs=tuple(out_specs or [vmem() for _ in outs]),
        scratch_shapes=scratch,
        compiler_params=pltpu.CompilerParams(vmem_limit_bytes=limit),
        cost_estimate=pl.CostEstimate(flops=flops, bytes_accessed=4 * MIB, transcendentals=0),
    )


def top_shift(count):
    return count.bit_length() - 3


def group_of(node, shift):
    return (node >> shift) & 3


def split(value, group, piece_refs):
    size = value.shape[0] // 4
    for g in range(4):
        for m in range(4):

            @pl.when((group ^ m) == g)
            def _():
                piece_refs[m][...] = value[g * size : (g + 1) * size, :].astype(piece_refs[m].dtype)


def split_kernel(shift, place_ref, value_ref, *piece_refs):
    split(value_ref[...], group_of(place_ref[1], shift), piece_refs)


def join(piece_refs, group, g):
    value = piece_refs[0][...]
    for m in range(1, 4):
        value = jnp.where((group ^ m) == g, piece_refs[m][...], value)
    return value


def join_kernel(shift, place_ref, p0, p1, p2, p3, out_ref):
    group = group_of(place_ref[1], shift)
    out_ref[...] = jnp.concatenate([join((p0, p1, p2, p3), group, g) for g in range(4)], axis=0)


def sum_kernel(factor, *refs):
    refs, out_ref = refs[:4], refs[-1]
    values = [ref[...].astype(F32) for ref in refs]
    out_ref[...] = ((values[0] + values[1]) + (values[2] + values[3])) * factor


def result_kernel(shift, place_ref, l0, l1, l2, l3, after_ref, in_ref, out_ref):
    group = group_of(place_ref[1], shift)
    for m, piece_ref in enumerate((l0, l1, l2, l3)):
        at = group ^ m

        @pl.when(at == 0)
        def _():
            out_ref[...] = piece_ref[...].astype(F32)

        @pl.when(at > 0)
        def _():
            in_ref[span((at - 1) * HD, HD), :] = piece_ref[...].astype(F32)


def pair_kernel(own_ref, across_ref, *refs):
    out_ref = refs[-1]
    rows = own_ref.shape[0]
    out_ref[:rows, :] = own_ref[...]
    out_ref[rows:, :] = across_ref[...]


def parts_of(pair_ref, other_ref):
    rows = pair_ref.shape[0] // 2
    return (pair_ref.at[:rows], other_ref.at[:rows], pair_ref.at[rows:], other_ref.at[rows:])


def issue_order(count):
    near, far = list(range(1, count // 2)), list(range(count // 2, count))
    return [0] + far[:2] + near + far[2:]


def by_mask(refs):
    order = issue_order(len(refs))
    return [refs[order.index(m)] for m in range(len(refs))]


def project_kernel(count, place_ref, wanted_ref, pair_ref, other_ref, in_from, *refs):
    qz_ref, kv_ref, refs = refs[0], refs[1], refs[2:]
    out_refs, (wide_ref, in_ref, sem) = refs[:count], refs[count:]
    in_copy = pltpu.make_async_copy(in_from, in_ref, sem)
    in_copy.start()
    x_refs = parts_of(pair_ref, other_ref)
    head, node = place_ref[0], place_ref[1]
    rows = x_refs[0].shape[0]
    in_copy.wait()
    wide_ref[:, HD:BLOCK] = jnp.zeros((D, HD), BF16)
    for g in range(HEADS):

        @pl.when(head == g)
        def _():
            at = g * 3 * HD
            wide_ref[:, :HD] = in_ref[:, at : at + HD]
            wide_ref[:, BLOCK:] = in_ref[:, at + HD : at + 3 * HD]

    for part in range(4):
        at = span((head ^ part) * rows, rows)
        y = dot(x_refs[part][...], wide_ref[...]).astype(BF16)
        qz_ref[at, :] = y[:, :BLOCK]
        kv_ref[at, :] = y[:, BLOCK:]
    for m in range(count):
        for c in range(CAP):
            block = wanted_ref[node ^ m, 0, c]
            out_refs[m][c] = kv_ref[span(block * BLOCK, BLOCK), :]


def prepare_kernel(place_ref, slot_ref, count_ref, pair_ref, other_ref, kv_ref, after_ref, xt_ref, kvt_ref):
    head = place_ref[0]
    rows = pair_ref.shape[0] // 2
    for part, x_ref in enumerate(parts_of(pair_ref, other_ref)):
        xt_ref[:, span((head ^ part) * rows, rows)] = x_ref[...].T
    for i in range(BLK):
        kvt_ref[i] = kv_ref[i * BLOCK : (i + 1) * BLOCK, :].T


def forward_kernel(count, place_ref, slot_ref, count_ref, qz_ref, kv_ref, kvt_ref, *refs):
    in_refs, refs = by_mask(refs[:count]), refs[count:]
    att_ref, attt_ref, table_ref, tablet_ref, top_ref, inv_ref, refs = *refs[:6], refs[6:]
    even_ref, odd_ref = refs
    node = place_ref[1]
    for i in range(BLK):
        table_ref[i] = kv_ref[i * BLOCK : (i + 1) * BLOCK, :]
        tablet_ref[i] = kvt_ref[i]
    for m in range(count):
        for c in range(CAP):
            block = in_refs[m][c]
            at = BLK + (node ^ m) * CAP + c
            table_ref[at] = block
            tablet_ref[at] = block.T

    def slots_of(i):
        return [slot_ref[i, j] for j in range(PER)]

    def score(i, raw_ref):
        live = count_ref[i]
        keys = jnp.concatenate([table_ref[s] for s in slots_of(i)], axis=0)
        raw = dot_last(keys, qz_ref[span(i * BLOCK, BLOCK), :])
        top = None
        for j in range(PER):
            here = jnp.where(j < live, raw[j * BLOCK : (j + 1) * BLOCK], -1e30)
            raw_ref[j * BLOCK : (j + 1) * BLOCK, :] = here
            here = here.reshape(BLOCK // 8, 8, BLOCK)
            highest = jnp.max(here, axis=0)
            top = highest if top is None else jnp.maximum(top, highest)
        return jnp.max(top, axis=0, keepdims=True)

    def attend(i, raw_ref, top):
        total = None
        for j in range(PER):
            here = slice(j * BLOCK, (j + 1) * BLOCK)
            raised = jnp.exp2((raw_ref[here, :] - top) * SCALE_LOG2E)
            raw_ref[here, :] = raised
            part = jnp.sum(raised.reshape(BLOCK // 8, 8, BLOCK), axis=0)
            total = part if total is None else total + part
        inverse = 1.0 / jnp.sum(total, axis=0, keepdims=True)
        values = jnp.concatenate([tablet_ref[s, HD:, :] for s in slots_of(i)], axis=1)
        result = dot(values, (raw_ref[...] * inverse).astype(BF16))
        attt_ref[:, span(i * BLOCK, BLOCK)] = result.astype(BF16)
        top_ref[i] = jnp.broadcast_to(top, (8, BLOCK))
        inv_ref[i] = jnp.broadcast_to(inverse, (8, BLOCK))
        return result

    def pair(t, even_top):
        odd_top = score(2 * t + 1, odd_ref)
        first = attend(2 * t, even_ref, even_top)
        even_top = score(jnp.minimum(2 * t + 2, BLK - 1), even_ref)
        second = attend(2 * t + 1, odd_ref, odd_top)
        both = jnp.concatenate([first, second], axis=0)
        att_ref[span(t * BLOCK, BLOCK), :] = both.T.astype(BF16)
        return even_top

    lax.fori_loop(0, PAIRS, pair, score(0, even_ref))


def middle_kernel(
    place_ref, x_pair, x_other, c_pair, c_other, a_pair, a_other, attt_ref, w_ref,
    out_ref, grad_out, gz_ref, dots_ref, owg_ref, wide_ref, pad_ref, grad_ref, sem,
):
    head = place_ref[0]
    rows = grad_ref.shape[0]
    grad_copy = pltpu.make_async_copy(grad_ref, grad_out, sem)
    own_w = w_ref[span(head * HD, HD), :]
    wide_ref[...] = jnp.zeros_like(wide_ref)
    for part in range(4):
        piece = w_ref[span((head ^ part) * HD, HD), :]
        at = (2 * part) * HD
        wide_ref[at : at + HD, :D] = piece
        wide_ref[at + HD : at + 2 * HD, D:] = piece
    pad_ref[:HD, :] = jnp.zeros((HD, D), BF16)
    pad_ref[HD:, :] = own_w
    a_refs = parts_of(a_pair, a_other)
    owg = jnp.zeros((HD, D), F32)
    pairs = rows // (2 * BLOCK)
    for part, (x_ref, c_ref) in enumerate(zip(parts_of(x_pair, x_other), parts_of(c_pair, c_other))):
        group = head ^ part
        at = span(group * (rows // 2), rows // 2)
        lhs = jnp.concatenate([a[at, :] for a in a_refs], axis=1)
        product = dot(lhs, wide_ref[...])
        lows = []
        for i in range(2 * pairs):
            local = slice(i * BLOCK, (i + 1) * BLOCK)
            pair, half = i // 2, i % 2
            summed = x_ref[local, :].astype(F32) + product[
                pair * BLOCK : (pair + 1) * BLOCK, half * D : (half + 1) * D
            ]
            inverse = lax.rsqrt(jnp.mean(summed * summed, axis=-1, keepdims=True) + 1e-06)
            normed = summed * inverse
            upstream = c_ref[local, :].astype(F32)
            grad = (upstream - normed * jnp.mean(upstream * normed, axis=-1, keepdims=True)) * inverse
            lows.append(grad.astype(BF16))
            if part == 0:
                out_ref[local, :] = normed.astype(BF16)
                grad_ref[local, :] = grad
        if part == 0:
            grad_copy.start()
        low = jnp.concatenate(lows, axis=0)
        at = span(group * rows, rows)
        gz_ref[at, :] = dot_last(low, pad_ref[...]).astype(BF16)
        turned = dot_last(own_w, low).astype(BF16).astype(F32)
        attended = attt_ref[:, at]
        sums = jnp.sum(turned * attended.astype(F32), axis=0, keepdims=True)
        for i in range(2 * pairs):
            dots_ref[group * (2 * pairs) + i] = jnp.broadcast_to(
                sums[:, i * BLOCK : (i + 1) * BLOCK], (8, BLOCK)
            )
        owg += dot(attended, low)
    owg_ref[...] = owg
    grad_copy.wait()


def backward_kernel(
    count, place_ref, slot_ref, count_ref, qz_ref, gz_ref, table_ref, tablet_ref, top_ref, inv_ref, dots_ref, *refs
):
    own_ref, dqt_ref, refs = refs[0], refs[1], refs[2:]
    dq_refs, leave_refs = refs[:4], refs[4 : 4 + count]
    acc_ref, dq_ref, even_ref, odd_ref = refs[4 + count :]
    head, node = place_ref[0], place_ref[1]
    acc_ref[...] = jnp.zeros_like(acc_ref)

    def slots_of(i):
        return [slot_ref[i, j] for j in range(PER)]

    def rows_of(i):
        at = span(i * BLOCK, BLOCK)
        return jnp.concatenate([qz_ref[at, :], gz_ref[at, :]], axis=0)

    def score(i, both_ref):
        keys = jnp.concatenate([table_ref[s] for s in slots_of(i)], axis=0)
        both_ref[...] = dot_last(keys, rows_of(i))

    def spread(i, both_ref):
        slots = slots_of(i)
        live = count_ref[i]
        top = top_ref[i, :1, :]
        inverse = inv_ref[i, :1, :]
        dots = dots_ref[i, :1, :]
        weights, grads = [], []
        for j in range(PER):
            here = slice(j * BLOCK, (j + 1) * BLOCK)
            weight = jnp.exp2((both_ref[here, :BLOCK] - top) * SCALE_LOG2E) * inverse
            weight = jnp.where(j < live, weight, 0.0)
            weights.append(weight.astype(BF16))
            grads.append((weight * (both_ref[here, BLOCK:] - dots) * SCALE).astype(BF16))
        score_grad = jnp.concatenate(grads, axis=0)
        low = jnp.concatenate(weights, axis=0)
        pair_grads = dot(jnp.concatenate([score_grad, low], axis=1), rows_of(i))
        for j in range(PER):
            acc_ref[slots[j]] += pair_grads[j * BLOCK : (j + 1) * BLOCK]
        turned = jnp.concatenate([tablet_ref[s, :HD, :] for s in slots], axis=1)
        result = dot(turned, score_grad)
        dqt_ref[:, span(i * BLOCK, BLOCK)] = result.astype(BF16)
        return result

    score(0, even_ref)

    @pl.loop(0, PAIRS)
    def _(t):
        score(2 * t + 1, odd_ref)
        first = spread(2 * t, even_ref)
        score(jnp.minimum(2 * t + 2, BLK - 1), even_ref)
        second = spread(2 * t + 1, odd_ref)
        both = jnp.concatenate([first, second], axis=0)
        dq_ref[span(t * BLOCK, BLOCK), :] = both.T.astype(BF16)

    own_ref[...] = acc_ref[:BLK]
    for m in range(count):
        for c in range(CAP):
            leave_refs[m][c] = acc_ref[BLK + (node ^ m) * CAP + c].astype(BF16)
    for part in range(4):
        size = dq_refs[part].shape[0]
        dq_refs[part][...] = dq_ref[span((head ^ part) * size, size), :]


def query_weight_kernel(place_ref, dqt_ref, pair_ref, other_ref, in_ref, out_ref, wkv_ref, wq_ref, k_ref, q_ref):
    head = place_ref[0]
    rows = pair_ref.shape[0] // 2
    total = jnp.zeros((HD, D), F32)
    for part, x_ref in enumerate(parts_of(pair_ref, other_ref)):
        total += dot(dqt_ref[:, span((head ^ part) * rows, rows)], x_ref[...])
    out_ref[...] = total
    blank = jnp.zeros((D, HD), BF16)
    for g in range(HEADS):
        at = g * 3 * HD
        query = in_ref[:, at : at + HD]
        k_ref[g] = in_ref[:, at + HD : at + 3 * HD]
        q_ref[g, :D] = jnp.concatenate([query, blank], axis=1)
        q_ref[g, D:] = jnp.concatenate([blank, query], axis=1)
    for part in range(4):
        lanes = slice(part * BLOCK, (part + 1) * BLOCK)
        wkv_ref[:, lanes] = k_ref[head ^ part]
        wq_ref[:, lanes] = q_ref[head ^ part]


def collect_kernel(count, place_ref, wanted_ref, own_ref, *refs):
    back_refs, dq_refs, refs = by_mask(refs[:count]), refs[count : count + 4], refs[count + 4 :]
    xt_ref, owg_ref, qwg_ref, refs = *refs[:3], refs[3:]
    send_refs, piece_refs, sum_ref = refs[:4], refs[4:8], refs[8]
    head, node = place_ref[0], place_ref[1]
    sum_ref[...] = own_ref[...]
    for m in range(count):
        for c in range(CAP):
            sum_ref[wanted_ref[node ^ m, 0, c]] += back_refs[m][c].astype(F32)
    for part in range(4):
        rows = 2 * dq_refs[part].shape[0]
        first = (head ^ part) * (rows // BLOCK)
        for i in range(rows // BLOCK):
            send_refs[part][i * BLOCK : (i + 1) * BLOCK, :] = sum_ref[first + i].astype(BF16)
        send_refs[part][rows:, :] = dq_refs[part][...]
    total = jnp.zeros((D, BLOCK), F32)
    for part in range(4):
        rows = 2 * dq_refs[part].shape[0]
        total += dot(xt_ref[:, span((head ^ part) * rows, rows)], send_refs[part][:rows, :])
    every = jnp.concatenate([owg_ref[...], qwg_ref[...], total.T], axis=0)
    split(every, group_of(node, top_shift(count)), piece_refs)


def finish_kernel(grad_from, s0, s3, s2, s1, wq_ref, wkv_ref, out_ref, done_ref, grad_ref, sem):
    done_ref[...] = jnp.zeros_like(done_ref)
    grad_copy = pltpu.make_async_copy(grad_from, grad_ref, sem)
    grad_copy.start()
    rows = out_ref.shape[0]
    s_refs = (s0, s1, s2, s3)
    kv = jnp.concatenate([s[:rows, :] for s in s_refs], axis=1)
    base = dot_last(kv, wkv_ref[...])
    lhs = jnp.concatenate([s[rows:, :] for s in s_refs], axis=1)
    product = dot_last(lhs, wq_ref[...])
    grad_copy.wait()
    for i in range(rows // BLOCK):
        at = slice(i * BLOCK, (i + 1) * BLOCK)
        pack = slice(i // 2 * BLOCK, (i // 2 + 1) * BLOCK)
        half = i % 2
        out_ref[at, :] = (
            grad_ref[at, :] + base[at] + product[pack, half * D : (half + 1) * D]
        ).astype(BF16)


def on_device(features, in_weight, out_weight, cotangent, key_slots, block_count, wanted):
    head_count = lax.axis_size("head")
    node_count = lax.axis_size("node")
    rows = features.shape[0]
    node_rows = rows * head_count
    total_nodes = node_rows * node_count
    table_size = BLK + node_count * CAP
    limit = (14 + table_size // 4) * MIB
    place = jnp.stack([lax.axis_index("head"), lax.axis_index("node")]).astype(jnp.int32)
    block_set = (CAP, BLOCK, BLOCK)

    def swap(value, axis, mask):
        size = lax.axis_size(axis)
        return lax.ppermute(value, axis, [(i, i ^ mask) for i in range(size)])

    def pair_up(value, across, after=()):
        (pair,) = call(
            pair_kernel,
            "pair",
            [((2 * value.shape[0], value.shape[1]), value.dtype)],
            [vmem()] * (2 + len(after)),
            4 * MIB,
        )(value, across, *after)
        return pair, swap(pair, "head", 1)

    def exchange(pieces, axis, unit=1):
        moved = list(pieces)
        for mask in reversed(range(1, len(pieces))):
            moved[mask] = swap(pieces[mask], axis, mask * unit)
        return moved

    def add_nodes(pieces, shift, factor):
        moved = exchange(pieces, "node", 1 << shift)
        piece = (pieces[0].shape, F32)
        (total,) = call(
            functools.partial(sum_kernel, factor),
            "sum",
            [piece],
            [vmem()] * 4,
            4 * MIB,
        )(moved[0], *moved[:0:-1])
        if shift == 1:
            total = total + swap(total, "node", 1)
        elif shift > 1:
            lower = call(
                functools.partial(split_kernel, shift - 2),
                "split",
                [((piece[0][0] // 4, D), F32)] * 4,
                [smem(), vmem()],
                limit,
            )(place, total)
            (total,) = call(
                functools.partial(join_kernel, shift - 2),
                "join",
                [piece],
                [smem()] + [vmem()] * 4,
                limit,
            )(place, *add_nodes(lower, shift - 2, 1.0))
        return exchange([total.astype(pieces[0].dtype)] * 4, "node", 1 << shift)

    order = issue_order(node_count)
    across = swap(features, "head", 2)
    c_across = swap(cotangent, "head", 2)
    wants = lax.all_to_all(
        wanted.reshape(node_count, 1, CAP), "node", split_axis=0, concat_axis=0, tiled=True
    )
    xs = pair_up(features, across, [wants])
    qz, kv, *outgoing = call(
        functools.partial(project_kernel, node_count),
        "project",
        [((node_rows, BLOCK), BF16)] * 2 + [(block_set, BF16)] * node_count,
        [smem()] * 2 + [vmem()] * 2 + [hbm()],
        limit,
        flops=2 * node_rows * D * D,
        scratch=[
            pltpu.VMEM((D, D), BF16),
            pltpu.VMEM((D, 3 * D), BF16),
            pltpu.SemaphoreType.DMA,
        ],
    )(place, wants, *xs, in_weight)
    incoming = exchange(outgoing, "node")
    xt, kvt = call(
        prepare_kernel,
        "prepare",
        [((D, node_rows), BF16), ((BLK, BLOCK, BLOCK), BF16)],
        [smem()] * 3 + [vmem()] * 4,
        limit,
        flops=2 * node_rows * D * D,
    )(place, key_slots, block_count, *xs, kv, c_across)
    att, attt, table, tablet, top, inv = call(
        functools.partial(forward_kernel, node_count),
        "forward",
        [
            ((PAIRS * BLOCK, BLOCK), BF16),
            ((HD, node_rows), BF16),
            ((table_size, BLOCK, BLOCK), BF16),
            ((table_size, BLOCK, BLOCK), BF16),
            ((BLK, 8, BLOCK), F32),
            ((BLK, 8, BLOCK), F32),
        ],
        [smem()] * 3 + [vmem()] * (3 + node_count),
        limit,
        flops=4 * node_rows * PER * BLOCK * BLOCK,
        scratch=[pltpu.VMEM((PER * BLOCK, BLOCK), F32)] * 2,
    )(place, key_slots, block_count, qz, kv, kvt, *[incoming[m] for m in order])
    parts = pair_up(att, swap(att, "head", 2))
    cs = pair_up(cotangent, c_across, [top])
    output, norm_grad, gz, dots, owg = call(
        middle_kernel,
        "middle",
        [
            ((rows, D), BF16),
            ((rows, D), F32),
            ((node_rows, BLOCK), BF16),
            ((BLK, 8, BLOCK), F32),
            ((HD, D), F32),
        ],
        [smem()] + [vmem()] * 8,
        limit,
        flops=8 * node_rows * D * D,
        scratch=[
            pltpu.VMEM((2 * D, 2 * D), BF16),
            pltpu.VMEM((BLOCK, D), BF16),
            pltpu.VMEM((rows, D), F32),
            pltpu.SemaphoreType.DMA,
        ],
        out_specs=[vmem(), hbm()] + [vmem()] * 3,
    )(place, *xs, *cs, *parts, attt, out_weight)
    own, dqt, *rest = call(
        functools.partial(backward_kernel, node_count),
        "backward",
        [((BLK, BLOCK, BLOCK), F32), ((HD, node_rows), BF16)]
        + [((rows // 2, BLOCK), BF16)] * 4
        + [(block_set, BF16)] * node_count,
        [smem()] * 3 + [vmem()] * 7,
        limit,
        flops=10 * node_rows * PER * BLOCK * BLOCK,
        scratch=[
            pltpu.VMEM((table_size, BLOCK, BLOCK), F32),
            pltpu.VMEM((PAIRS * BLOCK, BLOCK), BF16),
            pltpu.VMEM((PER * BLOCK, 2 * BLOCK), F32),
            pltpu.VMEM((PER * BLOCK, 2 * BLOCK), F32),
        ],
    )(place, key_slots, block_count, qz, gz, table, tablet, top, inv, dots)
    returned = exchange(rest[4:], "node")
    query_wg, wkv, wq = call(
        query_weight_kernel,
        "query_weight",
        [((HD, D), F32), ((D, 2 * D), BF16), ((2 * D, 2 * D), BF16)],
        [smem()] + [vmem()] * 4,
        limit,
        flops=2 * node_rows * D * HD,
        scratch=[pltpu.VMEM((HEADS, D, BLOCK), BF16), pltpu.VMEM((HEADS, 2 * D, BLOCK), BF16)],
    )(place, dqt, *xs, in_weight)
    collected = call(
        functools.partial(collect_kernel, node_count),
        "collect",
        [((rows * 3 // 2, BLOCK), BF16)] * 4 + [((HD, D), BF16)] * 4,
        [smem()] * 2 + [vmem()] * (8 + node_count),
        limit,
        flops=2 * node_rows * D * BLOCK,
        scratch=[pltpu.VMEM((BLK, BLOCK, BLOCK), F32)],
    )(place, wants, own, *[returned[m] for m in order], *rest[:4], xt, owg, query_wg)
    arrived = exchange(collected[:4], "head")
    feature_grad, finished = call(
        finish_kernel,
        "finish",
        [((rows, D), BF16), ((8, BLOCK), F32)],
        [hbm()] + [vmem()] * 6,
        limit,
        flops=4 * rows * 3 * D * D,
        scratch=[pltpu.VMEM((rows, D), F32), pltpu.SemaphoreType.DMA],
    )(norm_grad, arrived[0], *arrived[:0:-1], wq, wkv)
    shift = top_shift(node_count)
    factor = total_nodes ** (-0.5)
    late = add_nodes(collected[4:], shift, factor)
    in_grad, out_grad = call(
        functools.partial(result_kernel, shift),
        "result",
        [((3 * HD, D), F32), ((HD, D), F32)],
        [smem()] + [vmem()] * 5,
        limit,
    )(place, *late, finished)
    return (output, feature_grad, in_grad.T, out_grad)


def solution(mesh):
    placed = (
        P(("node", "head"), None),
        P(),
        P(),
        P(("node", "head"), None),
        P("node", None),
        P("node"),
        P("node", None, None),
    )
    return jax.shard_map(
        on_device,
        mesh=mesh,
        in_specs=placed,
        out_specs=(
            P(("node", "head"), None),
            P(("node", "head"), None),
            P(None, "head"),
            P("head", None),
        ),
        check_vma=False,
    )
```

profile of v0, /device:TPU:0, one launch (start us, length us, event | category | flops | bytes accessed | tf_op | source)
XLA Modules:
  0.0 107.4 jit_solution(14243016638475876598)
XLA Ops:
  0.6 3.0 %collective-permute-start = (bf16[512,256]{1,0:T(8,128)(2,1)}, bf16[512,256]{1,0:T(8,128)(2,1)S(1)}, u32[]{:S(2)}, u32[]{:S(2)}) collective-permute-start(bf16[512,256]{1,0:T(8,128)(2,1)} %own_ref.2), channel_id=1, source_target_pairs={{0,2},{1,3},{2,0},{3,1},{4,6},{5,7},{6,4},{7,5},{8,10},{9,11},{10,... | collective-permute-start | bytes 786440 | tf_op jit(solution)/shard_map/ppermute | solution.py:432
  3.7 12.1 %all_to_all.5.refs_0_.wanted_ref = s32[8,1,2]{2,1,0:T(1,128)S(1)} all-to-all(s32[8,1,2]{2,1,0:T(1,128)S(1)} %copy.11), channel_id=1, replica_groups=mesh['node'=8,'head'=4] {'node'}, dimensions={0} | all-to-all | bytes 128 | tf_op jit(solution)/shard_map/all_to_all | solution.py:482
  18.9 1.4 %project.1 = (bf16[2048,128]{1,0:T(8,128)(2,1)S(1)}, bf16[2048,128]{1,0:T(8,128)(2,1)S(1)}, bf16[2,128,128]{2,1,0:T(8,128)(2,1)S(1)}, bf16[2,128,128]{2,1,0:T(8,...) custom-call(s32[2]{0:T(128)S(1)} %pad_add_fusion.place_ref, ...), custom_call_target="tpu_custom_call" | custom-call | flops 268435456 | bytes 4194304 | tf_op jit(solution)/shard_map/project/pallas_call | solution.py:486
  20.9 2.4 %collective-permute-start.4 = (bf16[2,128,128]{2,1,0:T(8,128)(2,1)S(1)}, bf16[2,128,128]{2,1,0:T(8,128)(2,1)S(1)}, u32[]{:S(2)}, u32[]{:S(2)}) collective-permute-start(bf16[2,128,128]{2,1,0:T(8,128)(2,1)S(1)} %get-tuple-element.61), channel_id=1, source_target_pairs={{0,20},{4,16},{8,28},{12,24},{16,4},{20,0},{24,12},{28,8},{1,21},{... | collective-permute-start | bytes 196616 | tf_op jit(solution)/shard_map/ppermute | solution.py:432
  23.3 1.5 %collective-permute-start.5 = (bf16[2,128,128]{2,1,0:T(8,128)(2,1)S(1)}, bf16[2,128,128]{2,1,0:T(8,128)(2,1)S(1)}, u32[]{:S(2)}, u32[]{:S(2)}) collective-permute-start(bf16[2,128,128]{2,1,0:T(8,128)(2,1)S(1)} %get-tuple-element.62), channel_id=1, source_target_pairs={{0,4},{4,0},{8,12},{12,8},{16,20},{20,16},{24,28},{28,24},{1,5},{5... | collective-permute-start | bytes 196616 | tf_op jit(solution)/shard_map/ppermute | solution.py:432
  26.8 1.6 %collective-permute-done.3.refs_1_ = bf16[2,128,128]{2,1,0:T(8,128)(2,1)S(1)} collective-permute-done((bf16[2,128,128]{2,1,0:T(8,128)(2,1)S(1)}, bf16[2,128,128]{2,1,0:T(8,128)(2,1)S(1)}, u32[]{:S(2)}, u32[]{:S(2)}) %collective-permute-start.3) | collective-permute-done | bytes 65568 | tf_op jit(solution)/shard_map/ppermute | solution.py:432
  29.7 2.5 %collective-permute-start.9 = (bf16[2,128,128]{2,1,0:T(8,128)(2,1)S(1)}, bf16[2,128,128]{2,1,0:T(8,128)(2,1)S(1)}, u32[]{:S(2)}, u32[]{:S(2)}) collective-permute-start(bf16[2,128,128]{2,1,0:T(8,128)(2,1)S(1)} %get-tuple-element.66), channel_id=1, source_target_pairs={{0,28},{4,24},{8,20},{12,16},{16,12},{20,8},{24,4},{28,0},{1,29},{... | collective-permute-start | bytes 196616 | tf_op jit(solution)/shard_map/ppermute | solution.py:432
  34.4 2.2 %collective-permute-done.9.refs_7_ = bf16[2,128,128]{2,1,0:T(8,128)(2,1)S(1)} collective-permute-done((bf16[2,128,128]{2,1,0:T(8,128)(2,1)S(1)}, bf16[2,128,128]{2,1,0:T(8,128)(2,1)S(1)}, u32[]{:S(2)}, u32[]{:S(2)}) %collective-permute-start.9) | collective-permute-done | bytes 65568 | tf_op jit(solution)/shard_map/ppermute | solution.py:432
  36.7 8.5 %forward.1 = (bf16[1024,128]{1,0:T(8,128)(2,1)S(1)}, bf16[64,2048]{1,0:T(8,128)(2,1)S(1)}, bf16[32,128,128]{2,1,0:T(8,128)(2,1)S(1)}, bf16[32,128,128]{2,1,0:T(8...) custom-call(s32[2]{0:T(128)S(1)} %pad_add_fusion.place_ref, s32[16,12]{1,0:T(8,128)S(1)} %copy-done.3, ...), custom_call_target="tpu_custom_call" | custom-call | flops 1610612736 | bytes 4194304 | tf_op jit(solution)/shard_map/forward/pallas_call | solution.py:508
  45.9 6.2 %collective-permute-done.11.across_ref = bf16[1024,128]{1,0:T(8,128)(2,1)S(1)} collective-permute-done((bf16[1024,128]{1,0:T(8,128)(2,1)S(1)}, bf16[1024,128]{1,0:T(8,128)(2,1)S(1)}, u32[]{:S(2)}, u32[]{:S(2)}) %collective-permute-start.11) | collective-permute-done | bytes 262176 | tf_op jit(solution)/shard_map/ppermute | solution.py:432
  52.3 1.9 %collective-permute-done.12.a_other = bf16[2048,128]{1,0:T(8,128)(2,1)S(1)} collective-permute-done((bf16[2048,128]{1,0:T(8,128)(2,1)S(1)}, bf16[2048,128]{1,0:T(8,128)(2,1)S(1)}, u32[]{:S(2)}, u32[]{:S(2)}) %collective-permute-start.12) | collective-permute-done | bytes 524320 | tf_op jit(solution)/shard_map/ppermute | solution.py:432
  54.2 4.1 %middle.1 = (bf16[512,256]{1,0:T(8,128)(2,1)}, f32[512,256]{1,0:T(8,128)S(1)}, bf16[2048,128]{1,0:T(8,128)(2,1)S(1)}, f32[16,8,128]{2,1,0:T(8,128)S(1)}, f32[64,256]{1,0:T(8,128)S(1)}) custom-call(s32[2]{0:T(128)S(1)} %pad_add_fusion.place_ref, bf16[1024,256]{1,0:T(8,128)(2,1)S(1)} %pair.3.pair_ref.x_pair, ...), custom_call_target="tpu_custom_call" | custom-call | flops 1073741824 | bytes 4194304 | tf_op jit(solution)/shard_map/middle/pallas_call | solution.py:526
  58.3 11.2 %backward.1 = (f32[16,128,128]{2,1,0:T(8,128)S(1)}, bf16[64,2048]{1,0:T(8,128)(2,1)S(1)}, bf16[256,128]{1,0:T(8,128)(2,1)S(1)}, bf16[256,128]{1,0:T(8,128)(2,1)S...) custom-call(s32[2]{0:T(128)S(1)} %pad_add_fusion.place_ref, ...), custom_call_target="tpu_custom_call" | custom-call | flops 4026531840 | bytes 4194304 | tf_op jit(solution)/shard_map/backward/pallas_call | solution.py:547
  69.5 3.9 %collective-permute-start.14 = (bf16[2,128,128]{2,1,0:T(8,128)(2,1)S(1)}, bf16[2,128,128]{2,1,0:T(8,128)(2,1)S(1)}, u32[]{:S(2)}, u32[]{:S(2)}) collective-permute-start(bf16[2,128,128]{2,1,0:T(8,128)(2,1)S(1)} %get-tuple-element.80), channel_id=1, source_target_pairs={{0,20},{4,16},{8,28},{12,24},{16,4},{20,0},{24,12},{28,8},{1,21},{... | collective-permute-start | bytes 196616 | tf_op jit(solution)/shard_map/ppermute | solution.py:432
  73.9 3.0 %collective-permute-start.17 = (bf16[2,128,128]{2,1,0:T(8,128)(2,1)S(1)}, bf16[2,128,128]{2,1,0:T(8,128)(2,1)S(1)}, u32[]{:S(2)}, u32[]{:S(2)}) collective-permute-start(bf16[2,128,128]{2,1,0:T(8,128)(2,1)S(1)} %get-tuple-element.83), channel_id=1, source_target_pairs={{0,12},{4,8},{8,4},{12,0},{16,28},{20,24},{24,20},{28,16},{1,13},{... | collective-permute-start | bytes 196616 | tf_op jit(solution)/shard_map/ppermute | solution.py:432
  78.5 2.5 %collective-permute-start.19 = (bf16[2,128,128]{2,1,0:T(8,128)(2,1)S(1)}, bf16[2,128,128]{2,1,0:T(8,128)(2,1)S(1)}, u32[]{:S(2)}, u32[]{:S(2)}) collective-permute-start(bf16[2,128,128]{2,1,0:T(8,128)(2,1)S(1)} %get-tuple-element.85), channel_id=1, source_target_pairs={{0,28},{4,24},{8,20},{12,16},{16,12},{20,8},{24,4},{28,0},{1,29},{... | collective-permute-start | bytes 196616 | tf_op jit(solution)/shard_map/ppermute | solution.py:432
  83.0 2.5 %collective-permute-done.19.refs_7_ = bf16[2,128,128]{2,1,0:T(8,128)(2,1)S(1)} collective-permute-done((bf16[2,128,128]{2,1,0:T(8,128)(2,1)S(1)}, bf16[2,128,128]{2,1,0:T(8,128)(2,1)S(1)}, u32[]{:S(2)}, u32[]{:S(2)}) %collective-permute-start.19) | collective-permute-done | bytes 65568 | tf_op jit(solution)/shard_map/ppermute | solution.py:432
  86.9 2.5 %collective-permute-start.23 = (bf16[64,256]{1,0:T(8,128)(2,1)S(1)}, bf16[64,256]{1,0:T(8,128)(2,1)S(1)}, u32[]{:S(2)}, u32[]{:S(2)}) collective-permute-start(bf16[64,256]{1,0:T(8,128)(2,1)S(1)} %get-tuple-element.102), channel_id=1, source_target_pairs={{0,24},{4,28},{8,16},{12,20},{16,8},{20,12},{24,0},{28,4},{1,25},{... | collective-permute-start | bytes 98312 | tf_op jit(solution)/shard_map/ppermute | solution.py:432
  89.4 1.9 %collective-permute-start.25 = (bf16[64,256]{1,0:T(8,128)(2,1)S(1)}, bf16[64,256]{1,0:T(8,128)(2,1)S(1)}, u32[]{:S(2)}, u32[]{:S(2)}) collective-permute-start(bf16[64,256]{1,0:T(8,128)(2,1)S(1)} %get-tuple-element.104), channel_id=1, source_target_pairs={{0,8},{4,12},{8,0},{12,4},{16,24},{20,28},{24,16},{28,20},{1,9},{5... | collective-permute-start | bytes 98312 | tf_op jit(solution)/shard_map/ppermute | solution.py:432
  91.4 1.5 %collective-permute-done.23.refs_1_ = bf16[64,256]{1,0:T(8,128)(2,1)S(1)} collective-permute-done((bf16[64,256]{1,0:T(8,128)(2,1)S(1)}, bf16[64,256]{1,0:T(8,128)(2,1)S(1)}, u32[]{:S(2)}, u32[]{:S(2)}) %collective-permute-start.23) | collective-permute-done | bytes 32800 | tf_op jit(solution)/shard_map/ppermute | solution.py:432
  92.8 1.4 %collective-permute-done.24.refs_2_ = bf16[64,256]{1,0:T(8,128)(2,1)S(1)} collective-permute-done((bf16[64,256]{1,0:T(8,128)(2,1)S(1)}, bf16[64,256]{1,0:T(8,128)(2,1)S(1)}, u32[]{:S(2)}, u32[]{:S(2)}) %collective-permute-start.24) | collective-permute-done | bytes 32800 | tf_op jit(solution)/shard_map/ppermute | solution.py:432
  96.9 1.7 %collective-permute-done.26 = f32[64,256]{1,0:T(8,128)S(1)} collective-permute-done((f32[64,256]{1,0:T(8,128)S(1)}, f32[64,256]{1,0:T(8,128)S(1)}, u32[]{:S(2)}, u32[]{:S(2)}) %collective-permute-start.26) | collective-permute-done | bytes 65568 | tf_op jit(solution)/shard_map/ppermute | solution.py:432
  98.6 1.9 %collective-permute-start.29 = (bf16[64,256]{1,0:T(8,128)(2,1)S(1)}, bf16[64,256]{1,0:T(8,128)(2,1)S(1)}, u32[]{:S(2)}, u32[]{:S(2)}) collective-permute-start(bf16[64,256]{1,0:T(8,128)(2,1)S(1)} %add_convert_fusion.l0), channel_id=1, source_target_pairs={{0,24},{4,28},{8,16},{12,20},{16,8},{20,12},{24,0},{28,4},{1,25},{... | collective-permute-start | bytes 98312 | tf_op jit(solution)/shard_map/ppermute | solution.py:432
  102.2 1.7 %collective-permute-start.27 = (bf16[64,256]{1,0:T(8,128)(2,1)S(1)}, bf16[64,256]{1,0:T(8,128)(2,1)S(1)}, u32[]{:S(2)}, u32[]{:S(2)}) collective-permute-start(bf16[64,256]{1,0:T(8,128)(2,1)S(1)} %add_convert_fusion.l0), channel_id=1, source_target_pairs={{0,8},{4,12},{8,0},{12,4},{16,24},{20,28},{24,16},{28,20},{1,9},{5... | collective-permute-start | bytes 98312 | tf_op jit(solution)/shard_map/ppermute | solution.py:432
  (67 shorter events, 23.6 us)
Async XLA Ops:
  0.6 15.2 %collective-permute-start = (bf16[512,256]{1,0:T(8,128)(2,1)}, bf16[512,256]{1,0:T(8,128)(2,1)S(1)}, u32[]{:S(2)}, u32[]{:S(2)}) collective-permute-start(bf16[512,256]{1,0:T(8,128)(2,1)} %own_ref.2), channel_id=1, source_target_pairs={{0,2},{1,3},{2,0},{3,1},{4,6},{5,7},{6,4},{7,5},{8,10},{9,11},{10,... | collective-permute-start | bytes 786440 | tf_op jit(solution)/shard_map/ppermute | solution.py:432
  17.0 8.7 %collective-permute-start.2 = (bf16[512,256]{1,0:T(8,128)(2,1)S(1)}, bf16[512,256]{1,0:T(8,128)(2,1)S(1)}, u32[]{:S(2)}, u32[]{:S(2)}) collective-permute-start(bf16[512,256]{1,0:T(8,128)(2,1)S(1)} %copy-done.1), channel_id=1, source_target_pairs={{0,2},{1,3},{2,0},{3,1},{4,6},{5,7},{6,4},{7,5},{8,10},{9,11},{10,... | collective-permute-start | bytes 786440 | tf_op jit(solution)/shard_map/ppermute | solution.py:432
  20.3 8.1 %collective-permute-start.3 = (bf16[2,128,128]{2,1,0:T(8,128)(2,1)S(1)}, bf16[2,128,128]{2,1,0:T(8,128)(2,1)S(1)}, u32[]{:S(2)}, u32[]{:S(2)}) collective-permute-start(bf16[2,128,128]{2,1,0:T(8,128)(2,1)S(1)} %get-tuple-element.60), channel_id=1, source_target_pairs={{0,16},{4,20},{8,24},{12,28},{16,0},{20,4},{24,8},{28,12},{1,17},{... | collective-permute-start | bytes 196616 | tf_op jit(solution)/shard_map/ppermute | solution.py:432
  20.9 8.8 %collective-permute-start.4 = (bf16[2,128,128]{2,1,0:T(8,128)(2,1)S(1)}, bf16[2,128,128]{2,1,0:T(8,128)(2,1)S(1)}, u32[]{:S(2)}, u32[]{:S(2)}) collective-permute-start(bf16[2,128,128]{2,1,0:T(8,128)(2,1)S(1)} %get-tuple-element.61), channel_id=1, source_target_pairs={{0,20},{4,16},{8,28},{12,24},{16,4},{20,0},{24,12},{28,8},{1,21},{... | collective-permute-start | bytes 196616 | tf_op jit(solution)/shard_map/ppermute | solution.py:432
  23.3 10.1 %collective-permute-start.5 = (bf16[2,128,128]{2,1,0:T(8,128)(2,1)S(1)}, bf16[2,128,128]{2,1,0:T(8,128)(2,1)S(1)}, u32[]{:S(2)}, u32[]{:S(2)}) collective-permute-start(bf16[2,128,128]{2,1,0:T(8,128)(2,1)S(1)} %get-tuple-element.62), channel_id=1, source_target_pairs={{0,4},{4,0},{8,12},{12,8},{16,20},{20,16},{24,28},{28,24},{1,5},{5... | collective-permute-start | bytes 196616 | tf_op jit(solution)/shard_map/ppermute | solution.py:432
  24.7 8.7 %collective-permute-start.6 = (bf16[2,128,128]{2,1,0:T(8,128)(2,1)S(1)}, bf16[2,128,128]{2,1,0:T(8,128)(2,1)S(1)}, u32[]{:S(2)}, u32[]{:S(2)}) collective-permute-start(bf16[2,128,128]{2,1,0:T(8,128)(2,1)S(1)} %get-tuple-element.63), channel_id=1, source_target_pairs={{0,8},{4,12},{8,0},{12,4},{16,24},{20,28},{24,16},{28,20},{1,9},{5... | collective-permute-start | bytes 196616 | tf_op jit(solution)/shard_map/ppermute | solution.py:432
  25.7 7.8 %collective-permute-start.7 = (bf16[2,128,128]{2,1,0:T(8,128)(2,1)S(1)}, bf16[2,128,128]{2,1,0:T(8,128)(2,1)S(1)}, u32[]{:S(2)}, u32[]{:S(2)}) collective-permute-start(bf16[2,128,128]{2,1,0:T(8,128)(2,1)S(1)} %get-tuple-element.64), channel_id=1, source_target_pairs={{0,12},{4,8},{8,4},{12,0},{16,28},{20,24},{24,20},{28,16},{1,13},{... | collective-permute-start | bytes 196616 | tf_op jit(solution)/shard_map/ppermute | solution.py:432
  28.3 6.1 %collective-permute-start.8 = (bf16[2,128,128]{2,1,0:T(8,128)(2,1)S(1)}, bf16[2,128,128]{2,1,0:T(8,128)(2,1)S(1)}, u32[]{:S(2)}, u32[]{:S(2)}) collective-permute-start(bf16[2,128,128]{2,1,0:T(8,128)(2,1)S(1)} %get-tuple-element.65), channel_id=1, source_target_pairs={{0,24},{4,28},{8,16},{12,20},{16,8},{20,12},{24,0},{28,4},{1,25},{... | collective-permute-start | bytes 196616 | tf_op jit(solution)/shard_map/ppermute | solution.py:432
  29.7 7.0 %collective-permute-start.9 = (bf16[2,128,128]{2,1,0:T(8,128)(2,1)S(1)}, bf16[2,128,128]{2,1,0:T(8,128)(2,1)S(1)}, u32[]{:S(2)}, u32[]{:S(2)}) collective-permute-start(bf16[2,128,128]{2,1,0:T(8,128)(2,1)S(1)} %get-tuple-element.66), channel_id=1, source_target_pairs={{0,28},{4,24},{8,20},{12,16},{16,12},{20,8},{24,4},{28,0},{1,29},{... | collective-permute-start | bytes 196616 | tf_op jit(solution)/shard_map/ppermute | solution.py:432
  45.1 7.0 %collective-permute-start.11 = (bf16[1024,128]{1,0:T(8,128)(2,1)S(1)}, bf16[1024,128]{1,0:T(8,128)(2,1)S(1)}, u32[]{:S(2)}, u32[]{:S(2)}) collective-permute-start(bf16[1024,128]{1,0:T(8,128)(2,1)S(1)} %get-tuple-element.68.own_ref), channel_id=1, source_target_pairs={{0,2},{1,3},{2,0},{3,1},{4,6},{5,7},{6,4},{7,5},{8,10},{9,11},{10,... | collective-permute-start | bytes 786440 | tf_op jit(solution)/shard_map/ppermute | solution.py:432
  45.9 6.4 %collective-permute-start.10 = (bf16[1024,256]{1,0:T(8,128)(2,1)S(1)}, bf16[1024,256]{1,0:T(8,128)(2,1)S(1)}, u32[]{:S(2)}, u32[]{:S(2)}) collective-permute-start(bf16[1024,256]{1,0:T(8,128)(2,1)S(1)} %pair.4.c_pair), channel_id=1, source_target_pairs={{0,1},{1,0},{2,3},{3,2},{4,5},{5,4},{6,7},{7,6},{8,9},{9,8},{10,11... | collective-permute-start | bytes 1572872 | tf_op jit(solution)/shard_map/ppermute | solution.py:432
  69.4 7.4 %collective-permute-start.13 = (bf16[2,128,128]{2,1,0:T(8,128)(2,1)S(1)}, bf16[2,128,128]{2,1,0:T(8,128)(2,1)S(1)}, u32[]{:S(2)}, u32[]{:S(2)}) collective-permute-start(bf16[2,128,128]{2,1,0:T(8,128)(2,1)S(1)} %get-tuple-element.79), channel_id=1, source_target_pairs={{0,16},{4,20},{8,24},{12,28},{16,0},{20,4},{24,8},{28,12},{1,17},{... | collective-permute-start | bytes 196616 | tf_op jit(solution)/shard_map/ppermute | solution.py:432
  69.5 9.0 %collective-permute-start.14 = (bf16[2,128,128]{2,1,0:T(8,128)(2,1)S(1)}, bf16[2,128,128]{2,1,0:T(8,128)(2,1)S(1)}, u32[]{:S(2)}, u32[]{:S(2)}) collective-permute-start(bf16[2,128,128]{2,1,0:T(8,128)(2,1)S(1)} %get-tuple-element.80), channel_id=1, source_target_pairs={{0,20},{4,16},{8,28},{12,24},{16,4},{20,0},{24,12},{28,8},{1,21},{... | collective-permute-start | bytes 196616 | tf_op jit(solution)/shard_map/ppermute | solution.py:432
  73.4 8.5 %collective-permute-start.15 = (bf16[2,128,128]{2,1,0:T(8,128)(2,1)S(1)}, bf16[2,128,128]{2,1,0:T(8,128)(2,1)S(1)}, u32[]{:S(2)}, u32[]{:S(2)}) collective-permute-start(bf16[2,128,128]{2,1,0:T(8,128)(2,1)S(1)} %get-tuple-element.81), channel_id=1, source_target_pairs={{0,4},{4,0},{8,12},{12,8},{16,20},{20,16},{24,28},{28,24},{1,5},{5... | collective-permute-start | bytes 196616 | tf_op jit(solution)/shard_map/ppermute | solution.py:432
  73.9 8.0 %collective-permute-start.16 = (bf16[2,128,128]{2,1,0:T(8,128)(2,1)S(1)}, bf16[2,128,128]{2,1,0:T(8,128)(2,1)S(1)}, u32[]{:S(2)}, u32[]{:S(2)}) collective-permute-start(bf16[2,128,128]{2,1,0:T(8,128)(2,1)S(1)} %get-tuple-element.82), channel_id=1, source_target_pairs={{0,8},{4,12},{8,0},{12,4},{16,24},{20,28},{24,16},{28,20},{1,9},{5... | collective-permute-start | bytes 196616 | tf_op jit(solution)/shard_map/ppermute | solution.py:432
  73.9 8.0 %collective-permute-start.17 = (bf16[2,128,128]{2,1,0:T(8,128)(2,1)S(1)}, bf16[2,128,128]{2,1,0:T(8,128)(2,1)S(1)}, u32[]{:S(2)}, u32[]{:S(2)}) collective-permute-start(bf16[2,128,128]{2,1,0:T(8,128)(2,1)S(1)} %get-tuple-element.83), channel_id=1, source_target_pairs={{0,12},{4,8},{8,4},{12,0},{16,28},{20,24},{24,20},{28,16},{1,13},{... | collective-permute-start | bytes 196616 | tf_op jit(solution)/shard_map/ppermute | solution.py:432
  76.9 6.2 %collective-permute-start.18 = (bf16[2,128,128]{2,1,0:T(8,128)(2,1)S(1)}, bf16[2,128,128]{2,1,0:T(8,128)(2,1)S(1)}, u32[]{:S(2)}, u32[]{:S(2)}) collective-permute-start(bf16[2,128,128]{2,1,0:T(8,128)(2,1)S(1)} %get-tuple-element.84), channel_id=1, source_target_pairs={{0,24},{4,28},{8,16},{12,20},{16,8},{20,12},{24,0},{28,4},{1,25},{... | collective-permute-start | bytes 196616 | tf_op jit(solution)/shard_map/ppermute | solution.py:432
  78.5 7.0 %collective-permute-start.19 = (bf16[2,128,128]{2,1,0:T(8,128)(2,1)S(1)}, bf16[2,128,128]{2,1,0:T(8,128)(2,1)S(1)}, u32[]{:S(2)}, u32[]{:S(2)}) collective-permute-start(bf16[2,128,128]{2,1,0:T(8,128)(2,1)S(1)} %get-tuple-element.85), channel_id=1, source_target_pairs={{0,28},{4,24},{8,20},{12,16},{16,12},{20,8},{24,4},{28,0},{1,29},{... | collective-permute-start | bytes 196616 | tf_op jit(solution)/shard_map/ppermute | solution.py:432
  86.9 5.9 %collective-permute-start.23 = (bf16[64,256]{1,0:T(8,128)(2,1)S(1)}, bf16[64,256]{1,0:T(8,128)(2,1)S(1)}, u32[]{:S(2)}, u32[]{:S(2)}) collective-permute-start(bf16[64,256]{1,0:T(8,128)(2,1)S(1)} %get-tuple-element.102), channel_id=1, source_target_pairs={{0,24},{4,28},{8,16},{12,20},{16,8},{20,12},{24,0},{28,4},{1,25},{... | collective-permute-start | bytes 98312 | tf_op jit(solution)/shard_map/ppermute | solution.py:432
  95.0 7.2 %collective-permute-start.20 = (bf16[768,128]{1,0:T(8,128)(2,1)S(1)}, bf16[768,128]{1,0:T(8,128)(2,1)S(1)}, u32[]{:S(2)}, u32[]{:S(2)}) collective-permute-start(bf16[768,128]{1,0:T(8,128)(2,1)S(1)} %get-tuple-element.95), channel_id=1, source_target_pairs={{0,3},{1,2},{2,1},{3,0},{4,7},{5,6},{6,5},{7,4},{8,11},{9,10},{10,... | collective-permute-start | bytes 589832 | tf_op jit(solution)/shard_map/ppermute | solution.py:432
  95.0 9.8 %collective-permute-start.21 = (bf16[768,128]{1,0:T(8,128)(2,1)S(1)}, bf16[768,128]{1,0:T(8,128)(2,1)S(1)}, u32[]{:S(2)}, u32[]{:S(2)}) collective-permute-start(bf16[768,128]{1,0:T(8,128)(2,1)S(1)} %get-tuple-element.96), channel_id=1, source_target_pairs={{0,2},{1,3},{2,0},{3,1},{4,6},{5,7},{6,4},{7,5},{8,10},{9,11},{10,... | collective-permute-start | bytes 589832 | tf_op jit(solution)/shard_map/ppermute | solution.py:432
  95.7 9.1 %collective-permute-start.22 = (bf16[768,128]{1,0:T(8,128)(2,1)S(1)}, bf16[768,128]{1,0:T(8,128)(2,1)S(1)}, u32[]{:S(2)}, u32[]{:S(2)}) collective-permute-start(bf16[768,128]{1,0:T(8,128)(2,1)S(1)} %get-tuple-element.97), channel_id=1, source_target_pairs={{0,1},{1,0},{2,3},{3,2},{4,5},{5,4},{6,7},{7,6},{8,9},{9,8},{10,11... | collective-permute-start | bytes 589832 | tf_op jit(solution)/shard_map/ppermute | solution.py:432
  98.6 7.5 %collective-permute-start.29 = (bf16[64,256]{1,0:T(8,128)(2,1)S(1)}, bf16[64,256]{1,0:T(8,128)(2,1)S(1)}, u32[]{:S(2)}, u32[]{:S(2)}) collective-permute-start(bf16[64,256]{1,0:T(8,128)(2,1)S(1)} %add_convert_fusion.l0), channel_id=1, source_target_pairs={{0,24},{4,28},{8,16},{12,20},{16,8},{20,12},{24,0},{28,4},{1,25},{... | collective-permute-start | bytes 98312 | tf_op jit(solution)/shard_map/ppermute | solution.py:432
  100.5 5.6 %collective-permute-start.28 = (bf16[64,256]{1,0:T(8,128)(2,1)S(1)}, bf16[64,256]{1,0:T(8,128)(2,1)S(1)}, u32[]{:S(2)}, u32[]{:S(2)}) collective-permute-start(bf16[64,256]{1,0:T(8,128)(2,1)S(1)} %add_convert_fusion.l0), channel_id=1, source_target_pairs={{0,16},{4,20},{8,24},{12,28},{16,0},{20,4},{24,8},{28,12},{1,17},{... | collective-permute-start | bytes 98312 | tf_op jit(solution)/shard_map/ppermute | solution.py:432
  (13 other events, 52.9 us)
where the time goes:
time: 108 us; the launch traced here: 107 us
  starting transfers between devices  36.3 us (34%)
  Pallas kernels  31.3 us (29%)
  waiting for transfers between devices  25.7 us (24%)
  blocking collectives  12.1 us (11%)
  local copies, waits for them, and re-layouts  1.12 us (1%)
    ppermute x30, starting transfers between devices, swap(): return lax.ppermute(value, axis, [(i, i ^ mask) for i in range(size)])  36.3 us
    ppermute x30, waiting for transfers between devices, swap(): return lax.ppermute(value, axis, [(i, i ^ mask) for i in range(size)])  25.7 us
    all_to_all x1, blocking collectives, on_device(): lax.all_to_all(wanted.reshape(node_count, 1, CAP), 'node', split_axis=0,...  12.1 us
    pallas_call x1, Pallas kernels, on_device(): call(functools.partial(backward_kernel, node_count), 'backward', [((BLK,...  11.2 us
    pallas_call x1, Pallas kernels, on_device(): call(functools.partial(forward_kernel, node_count), 'forward', [((PAIRS *...  8.47 us
    pallas_call x1, Pallas kernels, on_device(): call(middle_kernel, 'middle', [((rows, D), BF16), ((rows, D), F32), ((nod...  4.07 us
  transfers between devices with their start and end apart: 30, of which 16 were waited for; matrix products, arithmetic and copies ran while one was open for 0% of the time, Pallas kernels for 4%

commit v1 on v0

--- a/solution.py
+++ b/solution.py
@@ -96,8 +96,8 @@
 
 
 def sum_kernel(factor, *refs):
-    refs, out_ref = refs[:4], refs[-1]
-    values = [ref[...].astype(F32) for ref in refs]
+    out_ref = refs[-1]
+    values = [ref[...].astype(F32) for ref in refs[:4]]
     out_ref[...] = ((values[0] + values[1]) + (values[2] + values[3])) * factor
 
 
@@ -115,11 +115,11 @@
             in_ref[span((at - 1) * HD, HD), :] = piece_ref[...].astype(F32)
 
 
-def pair_kernel(own_ref, across_ref, *refs):
+def pair_kernel(count, *refs):
     out_ref = refs[-1]
-    rows = own_ref.shape[0]
-    out_ref[:rows, :] = own_ref[...]
-    out_ref[rows:, :] = across_ref[...]
+    rows = refs[0].shape[0]
+    for i in range(count):
+        out_ref[i * rows : (i + 1) * rows, :] = refs[i][...]
 
 
 def parts_of(pair_ref, other_ref):
@@ -128,8 +128,7 @@
 
 
 def issue_order(count):
-    near, far = list(range(1, count // 2)), list(range(count // 2, count))
-    return [0] + far[:2] + near + far[2:]
+    return [0] + list(range(count - 1, 0, -1))
 
 
 def by_mask(refs):
@@ -175,21 +174,46 @@
         kvt_ref[i] = kv_ref[i * BLOCK : (i + 1) * BLOCK, :].T
 
 
-def forward_kernel(count, place_ref, slot_ref, count_ref, qz_ref, kv_ref, kvt_ref, *refs):
-    in_refs, refs = by_mask(refs[:count]), refs[count:]
-    att_ref, attt_ref, table_ref, tablet_ref, top_ref, inv_ref, refs = *refs[:6], refs[6:]
-    even_ref, odd_ref = refs
-    node = place_ref[1]
+def table_kernel_part(node, kv_ref, kvt_ref, in_refs, table_ref, tablet_ref):
     for i in range(BLK):
         table_ref[i] = kv_ref[i * BLOCK : (i + 1) * BLOCK, :]
         tablet_ref[i] = kvt_ref[i]
-    for m in range(count):
+    for m, in_ref in enumerate(in_refs):
         for c in range(CAP):
-            block = in_refs[m][c]
+            block = in_ref[c]
             at = BLK + (node ^ m) * CAP + c
             table_ref[at] = block
             tablet_ref[at] = block.T
 
+
+def early_forward_kernel(count, place_ref, slot_ref, count_ref, qz_ref, kv_ref, kvt_ref, *refs):
+    in_refs, refs = by_mask(refs[:count]), refs[count:]
+    att_ref, attt_ref, table_ref, tablet_ref, top_ref, inv_ref, even_ref, odd_ref = refs
+    table_kernel_part(place_ref[1], kv_ref, kvt_ref, in_refs, table_ref, tablet_ref)
+    attend_blocks(
+        0, slot_ref, count_ref, qz_ref, table_ref, tablet_ref,
+        att_ref, attt_ref, top_ref, inv_ref, even_ref, odd_ref,
+    )
+
+
+def late_forward_kernel(
+    slot_ref, count_ref, qz_ref, table_ref, tablet_ref, early_attt_ref, early_top_ref, early_inv_ref,
+    att_ref, attt_ref, top_ref, inv_ref, even_ref, odd_ref,
+):
+    half = BLK // 2
+    attt_ref[:, : half * BLOCK] = early_attt_ref[...]
+    top_ref[:half] = early_top_ref[...]
+    inv_ref[:half] = early_inv_ref[...]
+    attend_blocks(
+        half, slot_ref, count_ref, qz_ref, table_ref, tablet_ref,
+        att_ref, attt_ref, top_ref, inv_ref, even_ref, odd_ref,
+    )
+
+
+def attend_blocks(
+    start, slot_ref, count_ref, qz_ref, table_ref, tablet_ref,
+    att_ref, attt_ref, top_ref, inv_ref, even_ref, odd_ref,
+):
     def slots_of(i):
         return [slot_ref[i, j] for j in range(PER)]
 
@@ -223,15 +247,16 @@
         return result
 
     def pair(t, even_top):
-        odd_top = score(2 * t + 1, odd_ref)
-        first = attend(2 * t, even_ref, even_top)
-        even_top = score(jnp.minimum(2 * t + 2, BLK - 1), even_ref)
-        second = attend(2 * t + 1, odd_ref, odd_top)
+        first_at = start + 2 * t
+        odd_top = score(first_at + 1, odd_ref)
+        first = attend(first_at, even_ref, even_top)
+        even_top = score(jnp.minimum(first_at + 2, BLK - 1), even_ref)
+        second = attend(first_at + 1, odd_ref, odd_top)
         both = jnp.concatenate([first, second], axis=0)
         att_ref[span(t * BLOCK, BLOCK), :] = both.T.astype(BF16)
         return even_top
 
-    lax.fori_loop(0, PAIRS, pair, score(0, even_ref))
+    lax.fori_loop(0, PAIRS // 2, pair, score(start, even_ref))
 
 
 def middle_kernel(
@@ -277,10 +302,10 @@
             grad_copy.start()
         low = jnp.concatenate(lows, axis=0)
         at = span(group * rows, rows)
-        gz_ref[at, :] = dot_last(low, pad_ref[...]).astype(BF16)
+        gz_ref[at, :] = dot_last(low, pad_ref[...]).astype(BF16) * jnp.asarray(SCALE, BF16)
         turned = dot_last(own_w, low).astype(BF16).astype(F32)
         attended = attt_ref[:, at]
-        sums = jnp.sum(turned * attended.astype(F32), axis=0, keepdims=True)
+        sums = jnp.sum(turned * attended.astype(F32), axis=0, keepdims=True) * SCALE
         for i in range(2 * pairs):
             dots_ref[group * (2 * pairs) + i] = jnp.broadcast_to(
                 sums[:, i * BLOCK : (i + 1) * BLOCK], (8, BLOCK)
@@ -322,7 +347,7 @@
             weight = jnp.exp2((both_ref[here, :BLOCK] - top) * SCALE_LOG2E) * inverse
             weight = jnp.where(j < live, weight, 0.0)
             weights.append(weight.astype(BF16))
-            grads.append((weight * (both_ref[here, BLOCK:] - dots) * SCALE).astype(BF16))
+            grads.append((weight * (both_ref[here, BLOCK:] - dots)).astype(BF16))
         score_grad = jnp.concatenate(grads, axis=0)
         low = jnp.concatenate(weights, axis=0)
         pair_grads = dot(jnp.concatenate([score_grad, low], axis=1), rows_of(i))
@@ -344,10 +369,12 @@
         both = jnp.concatenate([first, second], axis=0)
         dq_ref[span(t * BLOCK, BLOCK), :] = both.T.astype(BF16)
 
-    own_ref[...] = acc_ref[:BLK]
+    lane = lax.broadcasted_iota(jnp.int32, (1, BLOCK), 1)
+    unscale = jnp.where(lane < HD, 1.0, 1.0 / SCALE)
+    own_ref[...] = acc_ref[:BLK] * unscale
     for m in range(count):
         for c in range(CAP):
-            leave_refs[m][c] = acc_ref[BLK + (node ^ m) * CAP + c].astype(BF16)
+            leave_refs[m][c] = (acc_ref[BLK + (node ^ m) * CAP + c] * unscale).astype(BF16)
     for part in range(4):
         size = dq_refs[part].shape[0]
         dq_refs[part][...] = dq_ref[span((head ^ part) * size, size), :]
@@ -376,7 +403,9 @@
 def collect_kernel(count, place_ref, wanted_ref, own_ref, *refs):
     back_refs, dq_refs, refs = by_mask(refs[:count]), refs[count : count + 4], refs[count + 4 :]
     xt_ref, owg_ref, qwg_ref, refs = *refs[:3], refs[3:]
-    send_refs, piece_refs, sum_ref = refs[:4], refs[4:8], refs[8]
+    own_send, beside_send, across_send, piece_refs, sum_ref = *refs[:3], refs[3:7], refs[7]
+    size = own_send.shape[0]
+    send_refs = (own_send, beside_send, across_send.at[:size], across_send.at[size:])
     head, node = place_ref[0], place_ref[1]
     sum_ref[...] = own_ref[...]
     for m in range(count):
@@ -396,12 +425,19 @@
     split(every, group_of(node, top_shift(count)), piece_refs)
 
 
-def finish_kernel(grad_from, s0, s3, s2, s1, wq_ref, wkv_ref, out_ref, done_ref, grad_ref, sem):
+def relay_kernel(beside_ref, across_ref, after_ref, out_ref):
+    size = beside_ref.shape[0]
+    out_ref[:size, :] = beside_ref[...]
+    out_ref[size:, :] = across_ref[size:, :]
+
+
+def finish_kernel(grad_from, own_ref, beside_ref, across_ref, wq_ref, wkv_ref, out_ref, done_ref, grad_ref, sem):
     done_ref[...] = jnp.zeros_like(done_ref)
     grad_copy = pltpu.make_async_copy(grad_from, grad_ref, sem)
     grad_copy.start()
     rows = out_ref.shape[0]
-    s_refs = (s0, s1, s2, s3)
+    size = own_ref.shape[0]
+    s_refs = (own_ref, beside_ref.at[:size], across_ref.at[:size], beside_ref.at[size:])
     kv = jnp.concatenate([s[:rows, :] for s in s_refs], axis=1)
     base = dot_last(kv, wkv_ref[...])
     lhs = jnp.concatenate([s[rows:, :] for s in s_refs], axis=1)
@@ -431,14 +467,15 @@
         size = lax.axis_size(axis)
         return lax.ppermute(value, axis, [(i, i ^ mask) for i in range(size)])
 
-    def pair_up(value, across, after=()):
+    def pair_up(values, after=()):
+        rows, width = values[0].shape
         (pair,) = call(
-            pair_kernel,
+            functools.partial(pair_kernel, len(values)),
             "pair",
-            [((2 * value.shape[0], value.shape[1]), value.dtype)],
-            [vmem()] * (2 + len(after)),
+            [((len(values) * rows, width), values[0].dtype)],
+            [vmem()] * (len(values) + len(after)),
             4 * MIB,
-        )(value, across, *after)
+        )(*values, *after)
         return pair, swap(pair, "head", 1)
 
     def exchange(pieces, axis, unit=1):
@@ -447,16 +484,16 @@
             moved[mask] = swap(pieces[mask], axis, mask * unit)
         return moved
 
-    def add_nodes(pieces, shift, factor):
+    def add_nodes(pieces, shift, factor, after=()):
         moved = exchange(pieces, "node", 1 << shift)
         piece = (pieces[0].shape, F32)
         (total,) = call(
             functools.partial(sum_kernel, factor),
             "sum",
             [piece],
-            [vmem()] * 4,
+            [vmem()] * (4 + len(after)),
             4 * MIB,
-        )(moved[0], *moved[:0:-1])
+        )(moved[0], *moved[:0:-1], *after)
         if shift == 1:
             total = total + swap(total, "node", 1)
         elif shift > 1:
@@ -473,8 +510,9 @@
                 [piece],
                 [smem()] + [vmem()] * 4,
                 limit,
-            )(place, *add_nodes(lower, shift - 2, 1.0))
-        return exchange([total.astype(pieces[0].dtype)] * 4, "node", 1 << shift)
+            )(place, *add_nodes(lower, shift - 2, 1.0)[0])
+        total = total.astype(pieces[0].dtype)
+        return exchange([total] * 4, "node", 1 << shift), total
 
     order = issue_order(node_count)
     across = swap(features, "head", 2)
@@ -482,7 +520,7 @@
     wants = lax.all_to_all(
         wanted.reshape(node_count, 1, CAP), "node", split_axis=0, concat_axis=0, tiled=True
     )
-    xs = pair_up(features, across, [wants])
+    xs = pair_up([features, across], [wants])
     qz, kv, *outgoing = call(
         functools.partial(project_kernel, node_count),
         "project",
@@ -505,24 +543,42 @@
         limit,
         flops=2 * node_rows * D * D,
     )(place, key_slots, block_count, *xs, kv, c_across)
-    att, attt, table, tablet, top, inv = call(
-        functools.partial(forward_kernel, node_count),
-        "forward",
+    half = BLK // 2
+    half_att = ((half * BLOCK // 2, BLOCK), BF16)
+    early_att, early_attt, table, tablet, early_top, early_inv = call(
+        functools.partial(early_forward_kernel, node_count),
+        "early_forward",
         [
-            ((PAIRS * BLOCK, BLOCK), BF16),
-            ((HD, node_rows), BF16),
+            half_att,
+            ((HD, half * BLOCK), BF16),
             ((table_size, BLOCK, BLOCK), BF16),
             ((table_size, BLOCK, BLOCK), BF16),
+            ((half, 8, BLOCK), F32),
+            ((half, 8, BLOCK), F32),
+        ],
+        [smem()] * 3 + [vmem()] * (3 + node_count),
+        limit,
+        flops=2 * node_rows * PER * BLOCK * BLOCK,
+        scratch=[pltpu.VMEM((PER * BLOCK, BLOCK), F32)] * 2,
+    )(place, key_slots, block_count, qz, kv, kvt, *[incoming[m] for m in order])
+    early_across = swap(early_att, "head", 2)
+    late_att, attt, top, inv = call(
+        late_forward_kernel,
+        "late_forward",
+        [
+            half_att,
+            ((HD, node_rows), BF16),
             ((BLK, 8, BLOCK), F32),
             ((BLK, 8, BLOCK), F32),
         ],
-        [smem()] * 3 + [vmem()] * (3 + node_count),
-        limit,
-        flops=4 * node_rows * PER * BLOCK * BLOCK,
+        [smem()] * 2 + [vmem()] * 6,
+        limit,
+        flops=2 * node_rows * PER * BLOCK * BLOCK,
         scratch=[pltpu.VMEM((PER * BLOCK, BLOCK), F32)] * 2,
-    )(place, key_slots, block_count, qz, kv, kvt, *[incoming[m] for m in order])
-    parts = pair_up(att, swap(att, "head", 2))
-    cs = pair_up(cotangent, c_across, [top])
+    )(key_slots, block_count, qz, table, tablet, early_attt, early_top, early_inv)
+    late_across = swap(late_att, "head", 2)
+    parts = pair_up([early_att, late_att, early_across, late_across])
+    cs = pair_up([cotangent, c_across], [top])
     output, norm_grad, gz, dots, owg = call(
         middle_kernel,
         "middle",
@@ -570,28 +626,34 @@
         flops=2 * node_rows * D * HD,
         scratch=[pltpu.VMEM((HEADS, D, BLOCK), BF16), pltpu.VMEM((HEADS, 2 * D, BLOCK), BF16)],
     )(place, dqt, *xs, in_weight)
+    sent = ((rows * 3 // 2, BLOCK), BF16)
     collected = call(
         functools.partial(collect_kernel, node_count),
         "collect",
-        [((rows * 3 // 2, BLOCK), BF16)] * 4 + [((HD, D), BF16)] * 4,
+        [sent, sent, ((rows * 3, BLOCK), BF16)] + [((HD, D), BF16)] * 4,
         [smem()] * 2 + [vmem()] * (8 + node_count),
         limit,
         flops=2 * node_rows * D * BLOCK,
         scratch=[pltpu.VMEM((BLK, BLOCK, BLOCK), F32)],
     )(place, wants, own, *[returned[m] for m in order], *rest[:4], xt, owg, query_wg)
-    arrived = exchange(collected[:4], "head")
+    own_send, beside_send, across_send = collected[:3]
+    across = swap(across_send, "head", 2)
+    shift = top_shift(node_count)
+    factor = total_nodes ** (-0.5)
+    late, summed = add_nodes(collected[3:], shift, factor)
+    (relay,) = call(
+        relay_kernel, "relay", [((rows * 3, BLOCK), BF16)], [vmem()] * 3, 4 * MIB
+    )(beside_send, across, summed)
+    beside = swap(relay, "head", 1)
     feature_grad, finished = call(
         finish_kernel,
         "finish",
         [((rows, D), BF16), ((8, BLOCK), F32)],
-        [hbm()] + [vmem()] * 6,
+        [hbm()] + [vmem()] * 5,
         limit,
         flops=4 * rows * 3 * D * D,
         scratch=[pltpu.VMEM((rows, D), F32), pltpu.SemaphoreType.DMA],
-    )(norm_grad, arrived[0], *arrived[:0:-1], wq, wkv)
-    shift = top_shift(node_count)
-    factor = total_nodes ** (-0.5)
-    late = add_nodes(collected[4:], shift, factor)
+    )(norm_grad, own_send, beside, across, wq, wkv)
     in_grad, out_grad = call(
         functools.partial(result_kernel, shift),
         "result",

time: 108 us -> 108 us (level)
  waiting for transfers between devices: 25.7 us -> 18.4 us
  starting transfers between devices: 36.3 us -> 43 us
    ppermute x30, waiting for transfers between devices: 25.7 us -> 18.4 us  [swap(): return lax.ppermute(value, axis, [(i, i ^ mask) for i in range(size)])]
    ppermute x30, starting transfers between devices: 36.3 us -> 43 us  [swap(): return lax.ppermute(value, axis, [(i, i ^ mask) for i in range(size)])]
    pallas_call x6 -> x8, Pallas kernels: 10 us -> 10.7 us  [the longest x1 4.66 us: on_device(): call(functools.partial(early_forward_kernel, node_count), 'early_forward'...]
  transfers between devices with their start and end apart: 30 -> 30, of which waited for: 16 -> 17; matrix products, arithmetic and copies ran while one was open for 0% -> 0% of each run, Pallas kernels for 4% -> 9%
where the time goes in v1:
time: 108 us
  starting transfers between devices  43 us (40%)
  Pallas kernels  31.8 us (29%)
  waiting for transfers between devices  18.4 us (17%)
  blocking collectives  12.1 us (11%)
  local copies, waits for them, and re-layouts  1.49 us (1%)
    ppermute x30, starting transfers between devices, swap(): return lax.ppermute(value, axis, [(i, i ^ mask) for i in range(size)])  43 us
    ppermute x30, waiting for transfers between devices, swap(): return lax.ppermute(value, axis, [(i, i ^ mask) for i in range(size)])  18.4 us
    all_to_all x1, blocking collectives, on_device(): lax.all_to_all(wanted.reshape(node_count, 1, CAP), 'node', split_axis=0,...  12.1 us
    pallas_call x1, Pallas kernels, on_device(): call(functools.partial(backward_kernel, node_count), 'backward', [((BLK,...  11 us
    pallas_call x1, Pallas kernels, on_device(): call(functools.partial(early_forward_kernel, node_count), 'early_forward'...  4.66 us
    pallas_call x1, Pallas kernels, on_device(): call(late_forward_kernel, 'late_forward', [half_att, ((HD, node_rows), BF...  4.48 us
    pallas_call x1, Pallas kernels, on_device(): call(middle_kernel, 'middle', [((rows, D), BF16), ((rows, D), F32), ((nod...  4.08 us
  transfers between devices with their start and end apart: 30, of which 17 were waited for; matrix products, arithmetic and copies ran while one was open for 0% of the time, Pallas kernels for 9%

profile of v1, /device:TPU:0, one launch (start us, length us, event | category | flops | bytes accessed | tf_op | source)
XLA Modules:
  0.0 107.7 jit_solution(2101550305743163194)
XLA Ops:
  0.6 3.0 %collective-permute-start = (bf16[512,256]{1,0:T(8,128)(2,1)}, bf16[512,256]{1,0:T(8,128)(2,1)S(1)}, u32[]{:S(2)}, u32[]{:S(2)}) collective-permute-start(bf16[512,256]{1,0:T(8,128)(2,1)} %refs_0_.2), channel_id=1, source_target_pairs={{0,2},{1,3},{2,0},{3,1},{4,6},{5,7},{6,4},{7,5},{8,10},{9,11},{10,... | collective-permute-start | bytes 786440 | tf_op jit(solution)/shard_map/ppermute | solution.py:468
  3.7 12.1 %all_to_all.5.refs_2_.wanted_ref = s32[8,1,2]{2,1,0:T(1,128)S(1)} all-to-all(s32[8,1,2]{2,1,0:T(1,128)S(1)} %copy.11), channel_id=1, replica_groups=mesh['node'=8,'head'=4] {'node'}, dimensions={0} | all-to-all | bytes 128 | tf_op jit(solution)/shard_map/all_to_all | solution.py:520
  18.9 1.4 %project.1 = (bf16[2048,128]{1,0:T(8,128)(2,1)S(1)}, bf16[2048,128]{1,0:T(8,128)(2,1)S(1)}, bf16[2,128,128]{2,1,0:T(8,128)(2,1)S(1)}, bf16[2,128,128]{2,1,0:T(8,...) custom-call(s32[2]{0:T(128)S(1)} %pad_add_fusion.place_ref, ...), custom_call_target="tpu_custom_call" | custom-call | flops 268435456 | bytes 4194304 | tf_op jit(solution)/shard_map/project/pallas_call | solution.py:524
  20.9 3.2 %collective-permute-start.4 = (bf16[2,128,128]{2,1,0:T(8,128)(2,1)S(1)}, bf16[2,128,128]{2,1,0:T(8,128)(2,1)S(1)}, u32[]{:S(2)}, u32[]{:S(2)}) collective-permute-start(bf16[2,128,128]{2,1,0:T(8,128)(2,1)S(1)} %get-tuple-element.64), channel_id=1, source_target_pairs={{0,24},{4,28},{8,16},{12,20},{16,8},{20,12},{24,0},{28,4},{1,25},{... | collective-permute-start | bytes 196616 | tf_op jit(solution)/shard_map/ppermute | solution.py:468
  24.2 3.8 %collective-permute-start.6 = (bf16[2,128,128]{2,1,0:T(8,128)(2,1)S(1)}, bf16[2,128,128]{2,1,0:T(8,128)(2,1)S(1)}, u32[]{:S(2)}, u32[]{:S(2)}) collective-permute-start(bf16[2,128,128]{2,1,0:T(8,128)(2,1)S(1)} %get-tuple-element.66), channel_id=1, source_target_pairs={{0,16},{4,20},{8,24},{12,28},{16,0},{20,4},{24,8},{28,12},{1,17},{... | collective-permute-start | bytes 196616 | tf_op jit(solution)/shard_map/ppermute | solution.py:468
  28.1 4.0 %collective-permute-start.8 = (bf16[2,128,128]{2,1,0:T(8,128)(2,1)S(1)}, bf16[2,128,128]{2,1,0:T(8,128)(2,1)S(1)}, u32[]{:S(2)}, u32[]{:S(2)}) collective-permute-start(bf16[2,128,128]{2,1,0:T(8,128)(2,1)S(1)} %get-tuple-element.68), channel_id=1, source_target_pairs={{0,8},{4,12},{8,0},{12,4},{16,24},{20,28},{24,16},{28,20},{1,9},{5... | collective-permute-start | bytes 196616 | tf_op jit(solution)/shard_map/ppermute | solution.py:468
  36.4 4.7 %early_forward.1 = (bf16[512,128]{1,0:T(8,128)(2,1)S(1)}, bf16[64,1024]{1,0:T(8,128)(2,1)S(1)}, bf16[32,128,128]{2,1,0:T(8,128)(2,1)S(1)}, bf16[32,128,128]{2,1,...) custom-call(s32[2]{0:T(128)S(1)} %pad_add_fusion.place_ref, s32[16,12]{1,0:T(8,128)S(1)} %copy-done.3, ...), custom_call_target="tpu_custom_call" | custom-call | flops 805306368 | bytes 4194304 | tf_op jit(solution)/shard_map/early_forward/pallas_call | solution.py:548
  41.7 4.5 %late_forward.1 = (bf16[512,128]{1,0:T(8,128)(2,1)S(1)}, bf16[64,2048]{1,0:T(8,128)(2,1)S(1)}, f32[16,8,128]{2,1,0:T(8,128)S(1)}, f32[16,8,128]{2,1,0:T(8,128)S(1)}) custom-call(s32[16,12]{1,0:T(8,128)S(1)} %copy-done.3, s32[16]{0:T(128)S(1)} %copy-done.4, bf16[2048,128]{1,0:T(8,128)(2,1)S(1)} %get-tuple-element.59.qz_ref, ...), custom_call_target="tpu_custom_call" | custom-call | flops 805306368 | bytes 4194304 | tf_op jit(solution)/shard_map/late_forward/pallas_call | solution.py:565
  46.2 1.5 %collective-permute-start.12 = (bf16[512,128]{1,0:T(8,128)(2,1)S(1)}, bf16[512,128]{1,0:T(8,128)(2,1)S(1)}, u32[]{:S(2)}, u32[]{:S(2)}) collective-permute-start(bf16[512,128]{1,0:T(8,128)(2,1)S(1)} %get-tuple-element.77.refs_1_), channel_id=1, source_target_pairs={{0,2},{1,3},{2,0},{3,1},{4,6},{5,7},{6,4},{7,5},{8,10},{9,11},{10,... | collective-permute-start | bytes 393224 | tf_op jit(solution)/shard_map/ppermute | solution.py:468
  47.8 3.4 %collective-permute-done.12.refs_3_ = bf16[512,128]{1,0:T(8,128)(2,1)S(1)} collective-permute-done((bf16[512,128]{1,0:T(8,128)(2,1)S(1)}, bf16[512,128]{1,0:T(8,128)(2,1)S(1)}, u32[]{:S(2)}, u32[]{:S(2)}) %collective-permute-start.12) | collective-permute-done | bytes 131104 | tf_op jit(solution)/shard_map/ppermute | solution.py:468
  51.3 1.9 %collective-permute-done.13.a_other = bf16[2048,128]{1,0:T(8,128)(2,1)S(1)} collective-permute-done((bf16[2048,128]{1,0:T(8,128)(2,1)S(1)}, bf16[2048,128]{1,0:T(8,128)(2,1)S(1)}, u32[]{:S(2)}, u32[]{:S(2)}) %collective-permute-start.13) | collective-permute-done | bytes 524320 | tf_op jit(solution)/shard_map/ppermute | solution.py:468
  53.2 4.1 %middle.1 = (bf16[512,256]{1,0:T(8,128)(2,1)}, f32[512,256]{1,0:T(8,128)S(1)}, bf16[2048,128]{1,0:T(8,128)(2,1)S(1)}, f32[16,8,128]{2,1,0:T(8,128)S(1)}, f32[64,256]{1,0:T(8,128)S(1)}) custom-call(s32[2]{0:T(128)S(1)} %pad_add_fusion.place_ref, bf16[1024,256]{1,0:T(8,128)(2,1)S(1)} %pair.3.pair_ref.x_pair, ...), custom_call_target="tpu_custom_call" | custom-call | flops 1073741824 | bytes 4194304 | tf_op jit(solution)/shard_map/middle/pallas_call | solution.py:582
  57.3 11.0 %backward.1 = (f32[16,128,128]{2,1,0:T(8,128)S(1)}, bf16[64,2048]{1,0:T(8,128)(2,1)S(1)}, bf16[256,128]{1,0:T(8,128)(2,1)S(1)}, bf16[256,128]{1,0:T(8,128)(2,1)S...) custom-call(s32[2]{0:T(128)S(1)} %pad_add_fusion.place_ref, ...), custom_call_target="tpu_custom_call" | custom-call | flops 4026531840 | bytes 4194304 | tf_op jit(solution)/shard_map/backward/pallas_call | solution.py:603
  69.1 2.9 %collective-permute-start.15 = (bf16[2,128,128]{2,1,0:T(8,128)(2,1)S(1)}, bf16[2,128,128]{2,1,0:T(8,128)(2,1)S(1)}, u32[]{:S(2)}, u32[]{:S(2)}) collective-permute-start(bf16[2,128,128]{2,1,0:T(8,128)(2,1)S(1)} %get-tuple-element.87), channel_id=1, source_target_pairs={{0,24},{4,28},{8,16},{12,20},{16,8},{20,12},{24,0},{28,4},{1,25},{... | collective-permute-start | bytes 196616 | tf_op jit(solution)/shard_map/ppermute | solution.py:468
  72.1 3.9 %collective-permute-start.17 = (bf16[2,128,128]{2,1,0:T(8,128)(2,1)S(1)}, bf16[2,128,128]{2,1,0:T(8,128)(2,1)S(1)}, u32[]{:S(2)}, u32[]{:S(2)}) collective-permute-start(bf16[2,128,128]{2,1,0:T(8,128)(2,1)S(1)} %get-tuple-element.89), channel_id=1, source_target_pairs={{0,16},{4,20},{8,24},{12,28},{16,0},{20,4},{24,8},{28,12},{1,17},{... | collective-permute-start | bytes 196616 | tf_op jit(solution)/shard_map/ppermute | solution.py:468
  76.1 4.3 %collective-permute-start.19 = (bf16[2,128,128]{2,1,0:T(8,128)(2,1)S(1)}, bf16[2,128,128]{2,1,0:T(8,128)(2,1)S(1)}, u32[]{:S(2)}, u32[]{:S(2)}) collective-permute-start(bf16[2,128,128]{2,1,0:T(8,128)(2,1)S(1)} %get-tuple-element.91), channel_id=1, source_target_pairs={{0,8},{4,12},{8,0},{12,4},{16,24},{20,28},{24,16},{28,20},{1,9},{5... | collective-permute-start | bytes 196616 | tf_op jit(solution)/shard_map/ppermute | solution.py:468
  80.4 1.5 %collective-permute-start.20 = (bf16[2,128,128]{2,1,0:T(8,128)(2,1)S(1)}, bf16[2,128,128]{2,1,0:T(8,128)(2,1)S(1)}, u32[]{:S(2)}, u32[]{:S(2)}) collective-permute-start(bf16[2,128,128]{2,1,0:T(8,128)(2,1)S(1)} %get-tuple-element.92), channel_id=1, source_target_pairs={{0,4},{4,0},{8,12},{12,8},{16,20},{20,16},{24,28},{28,24},{1,5},{5... | collective-permute-start | bytes 196616 | tf_op jit(solution)/shard_map/ppermute | solution.py:468
  84.9 1.4 %collect.1 = (bf16[768,128]{1,0:T(8,128)(2,1)S(1)}, bf16[768,128]{1,0:T(8,128)(2,1)S(1)}, bf16[1536,128]{1,0:T(8,128)(2,1)S(1)}, bf16[64,256]{1,0:T(8,128)(2,1)S...) custom-call(s32[2]{0:T(128)S(1)} %pad_add_fusion.place_ref, ...), custom_call_target="tpu_custom_call" | custom-call | flops 134217728 | bytes 4194304 | tf_op jit(solution)/shard_map/collect/pallas_call | solution.py:630
  86.3 1.5 %collective-permute-start.21 = (bf16[1536,128]{1,0:T(8,128)(2,1)S(1)}, bf16[1536,128]{1,0:T(8,128)(2,1)S(1)}, u32[]{:S(2)}, u32[]{:S(2)}) collective-permute-start(bf16[1536,128]{1,0:T(8,128)(2,1)S(1)} %get-tuple-element.103), channel_id=1, source_target_pairs={{0,2},{1,3},{2,0},{3,1},{4,6},{5,7},{6,4},{7,5},{8,10},{9,11},{10,... | collective-permute-start | bytes 1179656 | tf_op jit(solution)/shard_map/ppermute | solution.py:468
  88.0 2.4 %collective-permute-start.23 = (bf16[64,256]{1,0:T(8,128)(2,1)S(1)}, bf16[64,256]{1,0:T(8,128)(2,1)S(1)}, u32[]{:S(2)}, u32[]{:S(2)}) collective-permute-start(bf16[64,256]{1,0:T(8,128)(2,1)S(1)} %get-tuple-element.106), channel_id=1, source_target_pairs={{0,16},{4,20},{8,24},{12,28},{16,0},{20,4},{24,8},{28,12},{1,17},{... | collective-permute-start | bytes 98312 | tf_op jit(solution)/shard_map/ppermute | solution.py:468
  90.5 1.7 %collective-permute-start.24 = (bf16[64,256]{1,0:T(8,128)(2,1)S(1)}, bf16[64,256]{1,0:T(8,128)(2,1)S(1)}, u32[]{:S(2)}, u32[]{:S(2)}) collective-permute-start(bf16[64,256]{1,0:T(8,128)(2,1)S(1)} %get-tuple-element.107), channel_id=1, source_target_pairs={{0,8},{4,12},{8,0},{12,4},{16,24},{20,28},{24,16},{28,20},{1,9},{5... | collective-permute-start | bytes 98312 | tf_op jit(solution)/shard_map/ppermute | solution.py:468
  92.2 1.3 %collective-permute-done.22.refs_1_ = bf16[64,256]{1,0:T(8,128)(2,1)S(1)} collective-permute-done((bf16[64,256]{1,0:T(8,128)(2,1)S(1)}, bf16[64,256]{1,0:T(8,128)(2,1)S(1)}, u32[]{:S(2)}, u32[]{:S(2)}) %collective-permute-start.22) | collective-permute-done | bytes 32800 | tf_op jit(solution)/shard_map/ppermute | solution.py:468
  95.4 3.3 %collective-permute-done.25 = f32[64,256]{1,0:T(8,128)S(1)} collective-permute-done((f32[64,256]{1,0:T(8,128)S(1)}, f32[64,256]{1,0:T(8,128)S(1)}, u32[]{:S(2)}, u32[]{:S(2)}) %collective-permute-start.25) | collective-permute-done | bytes 65568 | tf_op jit(solution)/shard_map/ppermute | solution.py:468
  98.9 2.2 %collective-permute-start.29 = (bf16[64,256]{1,0:T(8,128)(2,1)S(1)}, bf16[64,256]{1,0:T(8,128)(2,1)S(1)}, u32[]{:S(2)}, u32[]{:S(2)}) collective-permute-start(bf16[64,256]{1,0:T(8,128)(2,1)S(1)} %add_convert_fusion.after_ref.l0), channel_id=1, source_target_pairs={{0,24},{4,28},{8,16},{12,20},{16,8},{20,12},{24,0},{28,4},{1,25},{... | collective-permute-start | bytes 98312 | tf_op jit(solution)/shard_map/ppermute | solution.py:468
  (69 shorter events, 21.8 us)
Async XLA Ops:
  0.6 15.2 %collective-permute-start = (bf16[512,256]{1,0:T(8,128)(2,1)}, bf16[512,256]{1,0:T(8,128)(2,1)S(1)}, u32[]{:S(2)}, u32[]{:S(2)}) collective-permute-start(bf16[512,256]{1,0:T(8,128)(2,1)} %refs_0_.2), channel_id=1, source_target_pairs={{0,2},{1,3},{2,0},{3,1},{4,6},{5,7},{6,4},{7,5},{8,10},{9,11},{10,... | collective-permute-start | bytes 786440 | tf_op jit(solution)/shard_map/ppermute | solution.py:468
  17.0 11.0 %collective-permute-start.2 = (bf16[512,256]{1,0:T(8,128)(2,1)S(1)}, bf16[512,256]{1,0:T(8,128)(2,1)S(1)}, u32[]{:S(2)}, u32[]{:S(2)}) collective-permute-start(bf16[512,256]{1,0:T(8,128)(2,1)S(1)} %copy-done.1), channel_id=1, source_target_pairs={{0,2},{1,3},{2,0},{3,1},{4,6},{5,7},{6,4},{7,5},{8,10},{9,11},{10,... | collective-permute-start | bytes 786440 | tf_op jit(solution)/shard_map/ppermute | solution.py:468
  20.3 7.8 %collective-permute-start.3 = (bf16[2,128,128]{2,1,0:T(8,128)(2,1)S(1)}, bf16[2,128,128]{2,1,0:T(8,128)(2,1)S(1)}, u32[]{:S(2)}, u32[]{:S(2)}) collective-permute-start(bf16[2,128,128]{2,1,0:T(8,128)(2,1)S(1)} %get-tuple-element.63), channel_id=1, source_target_pairs={{0,28},{4,24},{8,20},{12,16},{16,12},{20,8},{24,4},{28,0},{1,29},{... | collective-permute-start | bytes 196616 | tf_op jit(solution)/shard_map/ppermute | solution.py:468
  20.9 11.2 %collective-permute-start.4 = (bf16[2,128,128]{2,1,0:T(8,128)(2,1)S(1)}, bf16[2,128,128]{2,1,0:T(8,128)(2,1)S(1)}, u32[]{:S(2)}, u32[]{:S(2)}) collective-permute-start(bf16[2,128,128]{2,1,0:T(8,128)(2,1)S(1)} %get-tuple-element.64), channel_id=1, source_target_pairs={{0,24},{4,28},{8,16},{12,20},{16,8},{20,12},{24,0},{28,4},{1,25},{... | collective-permute-start | bytes 196616 | tf_op jit(solution)/shard_map/ppermute | solution.py:468
  24.2 10.4 %collective-permute-start.5 = (bf16[2,128,128]{2,1,0:T(8,128)(2,1)S(1)}, bf16[2,128,128]{2,1,0:T(8,128)(2,1)S(1)}, u32[]{:S(2)}, u32[]{:S(2)}) collective-permute-start(bf16[2,128,128]{2,1,0:T(8,128)(2,1)S(1)} %get-tuple-element.65), channel_id=1, source_target_pairs={{0,20},{4,16},{8,28},{12,24},{16,4},{20,0},{24,12},{28,8},{1,21},{... | collective-permute-start | bytes 196616 | tf_op jit(solution)/shard_map/ppermute | solution.py:468
  24.2 10.4 %collective-permute-start.6 = (bf16[2,128,128]{2,1,0:T(8,128)(2,1)S(1)}, bf16[2,128,128]{2,1,0:T(8,128)(2,1)S(1)}, u32[]{:S(2)}, u32[]{:S(2)}) collective-permute-start(bf16[2,128,128]{2,1,0:T(8,128)(2,1)S(1)} %get-tuple-element.66), channel_id=1, source_target_pairs={{0,16},{4,20},{8,24},{12,28},{16,0},{20,4},{24,8},{28,12},{1,17},{... | collective-permute-start | bytes 196616 | tf_op jit(solution)/shard_map/ppermute | solution.py:468
  28.0 7.5 %collective-permute-start.7 = (bf16[2,128,128]{2,1,0:T(8,128)(2,1)S(1)}, bf16[2,128,128]{2,1,0:T(8,128)(2,1)S(1)}, u32[]{:S(2)}, u32[]{:S(2)}) collective-permute-start(bf16[2,128,128]{2,1,0:T(8,128)(2,1)S(1)} %get-tuple-element.67), channel_id=1, source_target_pairs={{0,12},{4,8},{8,4},{12,0},{16,28},{20,24},{24,20},{28,16},{1,13},{... | collective-permute-start | bytes 196616 | tf_op jit(solution)/shard_map/ppermute | solution.py:468
  28.1 7.4 %collective-permute-start.8 = (bf16[2,128,128]{2,1,0:T(8,128)(2,1)S(1)}, bf16[2,128,128]{2,1,0:T(8,128)(2,1)S(1)}, u32[]{:S(2)}, u32[]{:S(2)}) collective-permute-start(bf16[2,128,128]{2,1,0:T(8,128)(2,1)S(1)} %get-tuple-element.68), channel_id=1, source_target_pairs={{0,8},{4,12},{8,0},{12,4},{16,24},{20,28},{24,16},{28,20},{1,9},{5... | collective-permute-start | bytes 196616 | tf_op jit(solution)/shard_map/ppermute | solution.py:468
  41.0 6.8 %collective-permute-start.11 = (bf16[512,128]{1,0:T(8,128)(2,1)S(1)}, bf16[512,128]{1,0:T(8,128)(2,1)S(1)}, u32[]{:S(2)}, u32[]{:S(2)}) collective-permute-start(bf16[512,128]{1,0:T(8,128)(2,1)S(1)} %get-tuple-element.76.refs_0_), channel_id=1, source_target_pairs={{0,2},{1,3},{2,0},{3,1},{4,6},{5,7},{6,4},{7,5},{8,10},{9,11},{10,... | collective-permute-start | bytes 393224 | tf_op jit(solution)/shard_map/ppermute | solution.py:468
  46.2 5.0 %collective-permute-start.12 = (bf16[512,128]{1,0:T(8,128)(2,1)S(1)}, bf16[512,128]{1,0:T(8,128)(2,1)S(1)}, u32[]{:S(2)}, u32[]{:S(2)}) collective-permute-start(bf16[512,128]{1,0:T(8,128)(2,1)S(1)} %get-tuple-element.77.refs_1_), channel_id=1, source_target_pairs={{0,2},{1,3},{2,0},{3,1},{4,6},{5,7},{6,4},{7,5},{8,10},{9,11},{10,... | collective-permute-start | bytes 393224 | tf_op jit(solution)/shard_map/ppermute | solution.py:468
  68.3 7.8 %collective-permute-start.14 = (bf16[2,128,128]{2,1,0:T(8,128)(2,1)S(1)}, bf16[2,128,128]{2,1,0:T(8,128)(2,1)S(1)}, u32[]{:S(2)}, u32[]{:S(2)}) collective-permute-start(bf16[2,128,128]{2,1,0:T(8,128)(2,1)S(1)} %get-tuple-element.86), channel_id=1, source_target_pairs={{0,28},{4,24},{8,20},{12,16},{16,12},{20,8},{24,4},{28,0},{1,29},{... | collective-permute-start | bytes 196616 | tf_op jit(solution)/shard_map/ppermute | solution.py:468
  69.1 11.3 %collective-permute-start.15 = (bf16[2,128,128]{2,1,0:T(8,128)(2,1)S(1)}, bf16[2,128,128]{2,1,0:T(8,128)(2,1)S(1)}, u32[]{:S(2)}, u32[]{:S(2)}) collective-permute-start(bf16[2,128,128]{2,1,0:T(8,128)(2,1)S(1)} %get-tuple-element.87), channel_id=1, source_target_pairs={{0,24},{4,28},{8,16},{12,20},{16,8},{20,12},{24,0},{28,4},{1,25},{... | collective-permute-start | bytes 196616 | tf_op jit(solution)/shard_map/ppermute | solution.py:468
  72.1 10.8 %collective-permute-start.16 = (bf16[2,128,128]{2,1,0:T(8,128)(2,1)S(1)}, bf16[2,128,128]{2,1,0:T(8,128)(2,1)S(1)}, u32[]{:S(2)}, u32[]{:S(2)}) collective-permute-start(bf16[2,128,128]{2,1,0:T(8,128)(2,1)S(1)} %get-tuple-element.88), channel_id=1, source_target_pairs={{0,20},{4,16},{8,28},{12,24},{16,4},{20,0},{24,12},{28,8},{1,21},{... | collective-permute-start | bytes 196616 | tf_op jit(solution)/shard_map/ppermute | solution.py:468
  72.1 11.5 %collective-permute-start.17 = (bf16[2,128,128]{2,1,0:T(8,128)(2,1)S(1)}, bf16[2,128,128]{2,1,0:T(8,128)(2,1)S(1)}, u32[]{:S(2)}, u32[]{:S(2)}) collective-permute-start(bf16[2,128,128]{2,1,0:T(8,128)(2,1)S(1)} %get-tuple-element.89), channel_id=1, source_target_pairs={{0,16},{4,20},{8,24},{12,28},{16,0},{20,4},{24,8},{28,12},{1,17},{... | collective-permute-start | bytes 196616 | tf_op jit(solution)/shard_map/ppermute | solution.py:468
  76.0 8.4 %collective-permute-start.18 = (bf16[2,128,128]{2,1,0:T(8,128)(2,1)S(1)}, bf16[2,128,128]{2,1,0:T(8,128)(2,1)S(1)}, u32[]{:S(2)}, u32[]{:S(2)}) collective-permute-start(bf16[2,128,128]{2,1,0:T(8,128)(2,1)S(1)} %get-tuple-element.90), channel_id=1, source_target_pairs={{0,12},{4,8},{8,4},{12,0},{16,28},{20,24},{24,20},{28,16},{1,13},{... | collective-permute-start | bytes 196616 | tf_op jit(solution)/shard_map/ppermute | solution.py:468
  76.1 8.3 %collective-permute-start.19 = (bf16[2,128,128]{2,1,0:T(8,128)(2,1)S(1)}, bf16[2,128,128]{2,1,0:T(8,128)(2,1)S(1)}, u32[]{:S(2)}, u32[]{:S(2)}) collective-permute-start(bf16[2,128,128]{2,1,0:T(8,128)(2,1)S(1)} %get-tuple-element.91), channel_id=1, source_target_pairs={{0,8},{4,12},{8,0},{12,4},{16,24},{20,28},{24,16},{28,20},{1,9},{5... | collective-permute-start | bytes 196616 | tf_op jit(solution)/shard_map/ppermute | solution.py:468
  80.4 4.5 %collective-permute-start.20 = (bf16[2,128,128]{2,1,0:T(8,128)(2,1)S(1)}, bf16[2,128,128]{2,1,0:T(8,128)(2,1)S(1)}, u32[]{:S(2)}, u32[]{:S(2)}) collective-permute-start(bf16[2,128,128]{2,1,0:T(8,128)(2,1)S(1)} %get-tuple-element.92), channel_id=1, source_target_pairs={{0,4},{4,0},{8,12},{12,8},{16,20},{20,16},{24,28},{28,24},{1,5},{5... | collective-permute-start | bytes 196616 | tf_op jit(solution)/shard_map/ppermute | solution.py:468
  86.3 12.5 %collective-permute-start.21 = (bf16[1536,128]{1,0:T(8,128)(2,1)S(1)}, bf16[1536,128]{1,0:T(8,128)(2,1)S(1)}, u32[]{:S(2)}, u32[]{:S(2)}) collective-permute-start(bf16[1536,128]{1,0:T(8,128)(2,1)S(1)} %get-tuple-element.103), channel_id=1, source_target_pairs={{0,2},{1,3},{2,0},{3,1},{4,6},{5,7},{6,4},{7,5},{8,10},{9,11},{10,... | collective-permute-start | bytes 1179656 | tf_op jit(solution)/shard_map/ppermute | solution.py:468
  87.8 5.7 %collective-permute-start.22 = (bf16[64,256]{1,0:T(8,128)(2,1)S(1)}, bf16[64,256]{1,0:T(8,128)(2,1)S(1)}, u32[]{:S(2)}, u32[]{:S(2)}) collective-permute-start(bf16[64,256]{1,0:T(8,128)(2,1)S(1)} %get-tuple-element.105), channel_id=1, source_target_pairs={{0,24},{4,28},{8,16},{12,20},{16,8},{20,12},{24,0},{28,4},{1,25},{... | collective-permute-start | bytes 98312 | tf_op jit(solution)/shard_map/ppermute | solution.py:468
  88.0 5.5 %collective-permute-start.23 = (bf16[64,256]{1,0:T(8,128)(2,1)S(1)}, bf16[64,256]{1,0:T(8,128)(2,1)S(1)}, u32[]{:S(2)}, u32[]{:S(2)}) collective-permute-start(bf16[64,256]{1,0:T(8,128)(2,1)S(1)} %get-tuple-element.106), channel_id=1, source_target_pairs={{0,16},{4,20},{8,24},{12,28},{16,0},{20,4},{24,8},{28,12},{1,17},{... | collective-permute-start | bytes 98312 | tf_op jit(solution)/shard_map/ppermute | solution.py:468
  98.8 4.5 %collective-permute-start.26 = (bf16[1536,128]{1,0:T(8,128)(2,1)S(1)}, bf16[1536,128]{1,0:T(8,128)(2,1)S(1)}, u32[]{:S(2)}, u32[]{:S(2)}) collective-permute-start(bf16[1536,128]{1,0:T(8,128)(2,1)S(1)} %relay.1), channel_id=1, source_target_pairs={{0,1},{1,0},{2,3},{3,2},{4,5},{5,4},{6,7},{7,6},{8,9},{9,8},{10,11... | collective-permute-start | bytes 1179656 | tf_op jit(solution)/shard_map/ppermute | solution.py:468
  98.9 6.2 %collective-permute-start.29 = (bf16[64,256]{1,0:T(8,128)(2,1)S(1)}, bf16[64,256]{1,0:T(8,128)(2,1)S(1)}, u32[]{:S(2)}, u32[]{:S(2)}) collective-permute-start(bf16[64,256]{1,0:T(8,128)(2,1)S(1)} %add_convert_fusion.after_ref.l0), channel_id=1, source_target_pairs={{0,24},{4,28},{8,16},{12,20},{16,8},{20,12},{24,0},{28,4},{1,25},{... | collective-permute-start | bytes 98312 | tf_op jit(solution)/shard_map/ppermute | solution.py:468
  101.1 5.0 %collective-permute-start.28 = (bf16[64,256]{1,0:T(8,128)(2,1)S(1)}, bf16[64,256]{1,0:T(8,128)(2,1)S(1)}, u32[]{:S(2)}, u32[]{:S(2)}) collective-permute-start(bf16[64,256]{1,0:T(8,128)(2,1)S(1)} %add_convert_fusion.after_ref.l0), channel_id=1, source_target_pairs={{0,16},{4,20},{8,24},{12,28},{16,0},{20,4},{24,8},{28,12},{1,17},{... | collective-permute-start | bytes 98312 | tf_op jit(solution)/shard_map/ppermute | solution.py:468
  102.1 4.3 %collective-permute-start.27 = (bf16[64,256]{1,0:T(8,128)(2,1)S(1)}, bf16[64,256]{1,0:T(8,128)(2,1)S(1)}, u32[]{:S(2)}, u32[]{:S(2)}) collective-permute-start(bf16[64,256]{1,0:T(8,128)(2,1)S(1)} %add_convert_fusion.after_ref.l0), channel_id=1, source_target_pairs={{0,8},{4,12},{8,0},{12,4},{16,24},{20,28},{24,16},{28,20},{1,9},{5... | collective-permute-start | bytes 98312 | tf_op jit(solution)/shard_map/ppermute | solution.py:468
  (13 other events, 46.5 us)

commit v2 on v1

--- a/solution.py
+++ b/solution.py
@@ -16,6 +16,7 @@
 CAP = 2
 D = 256
 PAIRS = BLK // 2
+DIRECT = 8
 SCALE = HD ** (-0.5)
 SCALE_LOG2E = SCALE * math.log2(math.e)
 BF16 = jnp.bfloat16
@@ -62,17 +63,22 @@
 
 
 def top_shift(count):
-    return count.bit_length() - 3
-
-
-def group_of(node, shift):
-    return (node >> shift) & 3
+    return max(count.bit_length() - 3, 0) if count > DIRECT else 0
+
+
+def top_pieces(count):
+    return 4 if count > DIRECT else count
+
+
+def group_of(node, shift, pieces=4):
+    return (node >> shift) & (pieces - 1)
 
 
 def split(value, group, piece_refs):
-    size = value.shape[0] // 4
-    for g in range(4):
-        for m in range(4):
+    pieces = len(piece_refs)
+    size = value.shape[0] // pieces
+    for g in range(pieces):
+        for m in range(pieces):
 
             @pl.when((group ^ m) == g)
             def _():
@@ -96,23 +102,28 @@
 
 
 def sum_kernel(factor, *refs):
-    out_ref = refs[-1]
-    values = [ref[...].astype(F32) for ref in refs[:4]]
-    out_ref[...] = ((values[0] + values[1]) + (values[2] + values[3])) * factor
-
-
-def result_kernel(shift, place_ref, l0, l1, l2, l3, after_ref, in_ref, out_ref):
-    group = group_of(place_ref[1], shift)
-    for m, piece_ref in enumerate((l0, l1, l2, l3)):
+    values = [ref[...].astype(F32) for ref in refs[:-1]]
+    while len(values) > 1:
+        values = [a + b for a, b in zip(values[::2], values[1::2])]
+    refs[-1][...] = (values[0] * factor).astype(refs[-1].dtype)
+
+
+def result_kernel(shift, place_ref, *refs):
+    piece_refs, in_ref, out_ref = refs[:1] + refs[1:-3][::-1], refs[-2], refs[-1]
+    pieces = len(piece_refs)
+    size = 4 * HD // pieces
+    first = HD // size
+    group = group_of(place_ref[1], shift, pieces)
+    for m, piece_ref in enumerate(piece_refs):
         at = group ^ m
 
-        @pl.when(at == 0)
+        @pl.when(at < first)
         def _():
-            out_ref[...] = piece_ref[...].astype(F32)
-
-        @pl.when(at > 0)
+            out_ref[span(at * size, size), :] = piece_ref[...].astype(F32)
+
+        @pl.when(at >= first)
         def _():
-            in_ref[span((at - 1) * HD, HD), :] = piece_ref[...].astype(F32)
+            in_ref[span((at - first) * size, size), :] = piece_ref[...].astype(F32)
 
 
 def pair_kernel(count, *refs):
@@ -165,13 +176,16 @@
             out_refs[m][c] = kv_ref[span(block * BLOCK, BLOCK), :]
 
 
-def prepare_kernel(place_ref, slot_ref, count_ref, pair_ref, other_ref, kv_ref, after_ref, xt_ref, kvt_ref):
+def prepare_kernel(slot_ref, count_ref, kv_ref, after_ref, kvt_ref):
+    for i in range(BLK):
+        kvt_ref[i] = kv_ref[i * BLOCK : (i + 1) * BLOCK, :].T
+
+
+def turn_kernel(place_ref, pair_ref, other_ref, after_ref, xt_ref):
     head = place_ref[0]
     rows = pair_ref.shape[0] // 2
     for part, x_ref in enumerate(parts_of(pair_ref, other_ref)):
         xt_ref[:, span((head ^ part) * rows, rows)] = x_ref[...].T
-    for i in range(BLK):
-        kvt_ref[i] = kv_ref[i * BLOCK : (i + 1) * BLOCK, :].T
 
 
 def table_kernel_part(node, kv_ref, kvt_ref, in_refs, table_ref, tablet_ref):
@@ -260,7 +274,7 @@
 
 
 def middle_kernel(
-    place_ref, x_pair, x_other, c_pair, c_other, a_pair, a_other, attt_ref, w_ref,
+    place_ref, x_pair, x_other, c_pair, c_other, a_pair, a_other, attt_ref, w_ref, after_ref,
     out_ref, grad_out, gz_ref, dots_ref, owg_ref, wide_ref, pad_ref, grad_ref, sem,
 ):
     head = place_ref[0]
@@ -403,7 +417,7 @@
 def collect_kernel(count, place_ref, wanted_ref, own_ref, *refs):
     back_refs, dq_refs, refs = by_mask(refs[:count]), refs[count : count + 4], refs[count + 4 :]
     xt_ref, owg_ref, qwg_ref, refs = *refs[:3], refs[3:]
-    own_send, beside_send, across_send, piece_refs, sum_ref = *refs[:3], refs[3:7], refs[7]
+    own_send, beside_send, across_send, piece_refs, sum_ref = *refs[:3], refs[3:-1], refs[-1]
     size = own_send.shape[0]
     send_refs = (own_send, beside_send, across_send.at[:size], across_send.at[size:])
     head, node = place_ref[0], place_ref[1]
@@ -422,10 +436,11 @@
         rows = 2 * dq_refs[part].shape[0]
         total += dot(xt_ref[:, span((head ^ part) * rows, rows)], send_refs[part][:rows, :])
     every = jnp.concatenate([owg_ref[...], qwg_ref[...], total.T], axis=0)
-    split(every, group_of(node, top_shift(count)), piece_refs)
-
-
-def relay_kernel(beside_ref, across_ref, after_ref, out_ref):
+    split(every, group_of(node, top_shift(count), len(piece_refs)), piece_refs)
+
+
+def relay_kernel(beside_ref, across_ref, *refs):
+    out_ref = refs[-1]
     size = beside_ref.shape[0]
     out_ref[:size, :] = beside_ref[...]
     out_ref[size:, :] = across_ref[size:, :]
@@ -484,35 +499,35 @@
             moved[mask] = swap(pieces[mask], axis, mask * unit)
         return moved
 
-    def add_nodes(pieces, shift, factor, after=()):
+    def add_nodes(pieces, shift, factor):
+        wire = pieces[0].dtype
         moved = exchange(pieces, "node", 1 << shift)
-        piece = (pieces[0].shape, F32)
+        shape = pieces[0].shape
         (total,) = call(
             functools.partial(sum_kernel, factor),
             "sum",
-            [piece],
-            [vmem()] * (4 + len(after)),
+            [(shape, F32 if shift else wire)],
+            [vmem()] * len(pieces),
             4 * MIB,
-        )(moved[0], *moved[:0:-1], *after)
+        )(moved[0], *moved[:0:-1])
         if shift == 1:
             total = total + swap(total, "node", 1)
         elif shift > 1:
             lower = call(
                 functools.partial(split_kernel, shift - 2),
                 "split",
-                [((piece[0][0] // 4, D), F32)] * 4,
+                [((shape[0] // 4, D), F32)] * 4,
                 [smem(), vmem()],
                 limit,
             )(place, total)
             (total,) = call(
                 functools.partial(join_kernel, shift - 2),
                 "join",
-                [piece],
+                [(shape, F32)],
                 [smem()] + [vmem()] * 4,
                 limit,
-            )(place, *add_nodes(lower, shift - 2, 1.0)[0])
-        total = total.astype(pieces[0].dtype)
-        return exchange([total] * 4, "node", 1 << shift), total
+            )(place, *add_nodes(lower, shift - 2, 1.0))
+        return exchange([total.astype(wire)] * len(pieces), "node", 1 << shift)
 
     order = issue_order(node_count)
     across = swap(features, "head", 2)
@@ -535,14 +550,14 @@
         ],
     )(place, wants, *xs, in_weight)
     incoming = exchange(outgoing, "node")
-    xt, kvt = call(
+    (kvt,) = call(
         prepare_kernel,
         "prepare",
-        [((D, node_rows), BF16), ((BLK, BLOCK, BLOCK), BF16)],
-        [smem()] * 3 + [vmem()] * 4,
-        limit,
-        flops=2 * node_rows * D * D,
-    )(place, key_slots, block_count, *xs, kv, c_across)
+        [((BLK, BLOCK, BLOCK), BF16)],
+        [smem()] * 2 + [vmem()] * 2,
+        limit,
+        flops=node_rows * D * D,
+    )(key_slots, block_count, kv, c_across)
     half = BLK // 2
     half_att = ((half * BLOCK // 2, BLOCK), BF16)
     early_att, early_attt, table, tablet, early_top, early_inv = call(
@@ -577,6 +592,14 @@
         scratch=[pltpu.VMEM((PER * BLOCK, BLOCK), F32)] * 2,
     )(key_slots, block_count, qz, table, tablet, early_attt, early_top, early_inv)
     late_across = swap(late_att, "head", 2)
+    (xt,) = call(
+        turn_kernel,
+        "turn",
+        [((D, node_rows), BF16)],
+        [smem()] + [vmem()] * 3,
+        limit,
+        flops=node_rows * D * D,
+    )(place, *xs, late_att)
     parts = pair_up([early_att, late_att, early_across, late_across])
     cs = pair_up([cotangent, c_across], [top])
     output, norm_grad, gz, dots, owg = call(
@@ -589,7 +612,7 @@
             ((BLK, 8, BLOCK), F32),
             ((HD, D), F32),
         ],
-        [smem()] + [vmem()] * 8,
+        [smem()] + [vmem()] * 9,
         limit,
         flops=8 * node_rows * D * D,
         scratch=[
@@ -599,7 +622,7 @@
             pltpu.SemaphoreType.DMA,
         ],
         out_specs=[vmem(), hbm()] + [vmem()] * 3,
-    )(place, *xs, *cs, *parts, attt, out_weight)
+    )(place, *xs, *cs, *parts, attt, out_weight, xt)
     own, dqt, *rest = call(
         functools.partial(backward_kernel, node_count),
         "backward",
@@ -627,10 +650,11 @@
         scratch=[pltpu.VMEM((HEADS, D, BLOCK), BF16), pltpu.VMEM((HEADS, 2 * D, BLOCK), BF16)],
     )(place, dqt, *xs, in_weight)
     sent = ((rows * 3 // 2, BLOCK), BF16)
+    pieces = top_pieces(node_count)
     collected = call(
         functools.partial(collect_kernel, node_count),
         "collect",
-        [sent, sent, ((rows * 3, BLOCK), BF16)] + [((HD, D), BF16)] * 4,
+        [sent, sent, ((rows * 3, BLOCK), BF16)] + [((4 * HD // pieces, D), BF16)] * pieces,
         [smem()] * 2 + [vmem()] * (8 + node_count),
         limit,
         flops=2 * node_rows * D * BLOCK,
@@ -640,10 +664,10 @@
     across = swap(across_send, "head", 2)
     shift = top_shift(node_count)
     factor = total_nodes ** (-0.5)
-    late, summed = add_nodes(collected[3:], shift, factor)
+    late = add_nodes(collected[3:], shift, factor)
     (relay,) = call(
-        relay_kernel, "relay", [((rows * 3, BLOCK), BF16)], [vmem()] * 3, 4 * MIB
-    )(beside_send, across, summed)
+        relay_kernel, "relay", [((rows * 3, BLOCK), BF16)], [vmem()] * 5, 4 * MIB
+    )(beside_send, across, *late[1:4])
     beside = swap(relay, "head", 1)
     feature_grad, finished = call(
         finish_kernel,
@@ -658,9 +682,9 @@
         functools.partial(result_kernel, shift),
         "result",
         [((3 * HD, D), F32), ((HD, D), F32)],
-        [smem()] + [vmem()] * 5,
-        limit,
-    )(place, *late, finished)
+        [smem()] + [vmem()] * (1 + pieces),
+        limit,
+    )(place, late[0], *late[:0:-1], finished)
     return (output, feature_grad, in_grad.T, out_grad)
 
 

time: 108 us -> 120 us (1.11)
  starting transfers between devices: 43 us -> 55.5 us
  waiting for transfers between devices: 18.4 us -> 17.1 us
    ppermute x30 -> x37, starting transfers between devices: 43 us -> 55.5 us  [swap(): return lax.ppermute(value, axis, [(i, i ^ mask) for i in range(size)])]
    ppermute x30 -> x37, waiting for transfers between devices: 18.4 us -> 17.1 us  [swap(): return lax.ppermute(value, axis, [(i, i ^ mask) for i in range(size)])]
  transfers between devices with their start and end apart: 30 -> 37, of which waited for: 17 -> 17; matrix products, arithmetic and copies ran while one was open for 0% -> 0% of each run, Pallas kernels for 9% -> 8%
where the time goes in v2:
time: 120 us
  starting transfers between devices  55.5 us (46%)
  Pallas kernels  33 us (28%)
  waiting for transfers between devices  17.1 us (14%)
  blocking collectives  12.1 us (10%)
  local copies, waits for them, and re-layouts  1.49 us (1%)
    ppermute x37, starting transfers between devices, swap(): return lax.ppermute(value, axis, [(i, i ^ mask) for i in range(size)])  55.5 us
    ppermute x37, waiting for transfers between devices, swap(): return lax.ppermute(value, axis, [(i, i ^ mask) for i in range(size)])  17.1 us
    all_to_all x1, blocking collectives, on_device(): lax.all_to_all(wanted.reshape(node_count, 1, CAP), 'node', split_axis=0,...  12.1 us
    pallas_call x1, Pallas kernels, on_device(): call(functools.partial(backward_kernel, node_count), 'backward', [((BLK,...  11.1 us
    pallas_call x1, Pallas kernels, on_device(): call(functools.partial(early_forward_kernel, node_count), 'early_forward'...  4.75 us
    pallas_call x1, Pallas kernels, on_device(): call(late_forward_kernel, 'late_forward', [half_att, ((HD, node_rows), BF...  4.59 us
    pallas_call x1, Pallas kernels, on_device(): call(middle_kernel, 'middle', [((rows, D), BF16), ((rows, D), F32), ((nod...  4.08 us
  transfers between devices with their start and end apart: 37, of which 17 were waited for; matrix products, arithmetic and copies ran while one was open for 0% of the time, Pallas kernels for 8%

profile of v2, /device:TPU:0, one launch (start us, length us, event | category | flops | bytes accessed | tf_op | source)
XLA Modules:
  0.0 120.2 jit_solution(1608905185186337692)
XLA Ops:
  0.6 3.0 %collective-permute-start = (bf16[512,256]{1,0:T(8,128)(2,1)}, bf16[512,256]{1,0:T(8,128)(2,1)S(1)}, u32[]{:S(2)}, u32[]{:S(2)}) collective-permute-start(bf16[512,256]{1,0:T(8,128)(2,1)} %refs_0_.2), channel_id=1, source_target_pairs={{0,2},{1,3},{2,0},{3,1},{4,6},{5,7},{6,4},{7,5},{8,10},{9,11},{10,... | collective-permute-start | bytes 786440 | tf_op jit(solution)/shard_map/ppermute | solution.py:483
  3.7 12.1 %all_to_all.5.refs_2_.wanted_ref = s32[8,1,2]{2,1,0:T(1,128)S(1)} all-to-all(s32[8,1,2]{2,1,0:T(1,128)S(1)} %copy.11), channel_id=1, replica_groups=mesh['node'=8,'head'=4] {'node'}, dimensions={0} | all-to-all | bytes 128 | tf_op jit(solution)/shard_map/all_to_all | solution.py:535
  20.9 3.2 %collective-permute-start.4 = (bf16[2,128,128]{2,1,0:T(8,128)(2,1)S(1)}, bf16[2,128,128]{2,1,0:T(8,128)(2,1)S(1)}, u32[]{:S(2)}, u32[]{:S(2)}) collective-permute-start(bf16[2,128,128]{2,1,0:T(8,128)(2,1)S(1)} %get-tuple-element.65), channel_id=1, source_target_pairs={{0,24},{4,28},{8,16},{12,20},{16,8},{20,12},{24,0},{28,4},{1,25},{... | collective-permute-start | bytes 196616 | tf_op jit(solution)/shard_map/ppermute | solution.py:483
  24.2 3.8 %collective-permute-start.6 = (bf16[2,128,128]{2,1,0:T(8,128)(2,1)S(1)}, bf16[2,128,128]{2,1,0:T(8,128)(2,1)S(1)}, u32[]{:S(2)}, u32[]{:S(2)}) collective-permute-start(bf16[2,128,128]{2,1,0:T(8,128)(2,1)S(1)} %get-tuple-element.67), channel_id=1, source_target_pairs={{0,16},{4,20},{8,24},{12,28},{16,0},{20,4},{24,8},{28,12},{1,17},{... | collective-permute-start | bytes 196616 | tf_op jit(solution)/shard_map/ppermute | solution.py:483
  28.1 4.0 %collective-permute-start.8 = (bf16[2,128,128]{2,1,0:T(8,128)(2,1)S(1)}, bf16[2,128,128]{2,1,0:T(8,128)(2,1)S(1)}, u32[]{:S(2)}, u32[]{:S(2)}) collective-permute-start(bf16[2,128,128]{2,1,0:T(8,128)(2,1)S(1)} %get-tuple-element.69), channel_id=1, source_target_pairs={{0,8},{4,12},{8,0},{12,4},{16,24},{20,28},{24,16},{28,20},{1,9},{5... | collective-permute-start | bytes 196616 | tf_op jit(solution)/shard_map/ppermute | solution.py:483
  36.4 4.8 %early_forward.1 = (bf16[512,128]{1,0:T(8,128)(2,1)S(1)}, bf16[64,1024]{1,0:T(8,128)(2,1)S(1)}, bf16[32,128,128]{2,1,0:T(8,128)(2,1)S(1)}, bf16[32,128,128]{2,1,...) custom-call(s32[2]{0:T(128)S(1)} %pad_add_fusion.place_ref, s32[16,12]{1,0:T(8,128)S(1)} %copy-done.4, ...), custom_call_target="tpu_custom_call" | custom-call | flops 805306368 | bytes 4194304 | tf_op jit(solution)/shard_map/early_forward/pallas_call | solution.py:563
  41.8 4.6 %late_forward.1 = (bf16[512,128]{1,0:T(8,128)(2,1)S(1)}, bf16[64,2048]{1,0:T(8,128)(2,1)S(1)}, f32[16,8,128]{2,1,0:T(8,128)S(1)}, f32[16,8,128]{2,1,0:T(8,128)S(1)}) custom-call(s32[16,12]{1,0:T(8,128)S(1)} %copy-done.4, s32[16]{0:T(128)S(1)} %copy-done.5, bf16[2048,128]{1,0:T(8,128)(2,1)S(1)} %get-tuple-element.61.qz_ref, ...), custom_call_target="tpu_custom_call" | custom-call | flops 805306368 | bytes 4194304 | tf_op jit(solution)/shard_map/late_forward/pallas_call | solution.py:580
  46.4 1.5 %collective-permute-start.12 = (bf16[512,128]{1,0:T(8,128)(2,1)S(1)}, bf16[512,128]{1,0:T(8,128)(2,1)S(1)}, u32[]{:S(2)}, u32[]{:S(2)}) collective-permute-start(bf16[512,128]{1,0:T(8,128)(2,1)S(1)} %get-tuple-element.78.refs_1_.after_ref), channel_id=1, source_target_pairs={{0,2},{1,3},{2,0},{3,1},{4,6},{5,7},{6,4},{7,5},{8,10},{9,11},{10,... | collective-permute-start | bytes 393224 | tf_op jit(solution)/shard_map/ppermute | solution.py:483
  48.0 3.4 %collective-permute-done.12.refs_3_ = bf16[512,128]{1,0:T(8,128)(2,1)S(1)} collective-permute-done((bf16[512,128]{1,0:T(8,128)(2,1)S(1)}, bf16[512,128]{1,0:T(8,128)(2,1)S(1)}, u32[]{:S(2)}, u32[]{:S(2)}) %collective-permute-start.12) | collective-permute-done | bytes 131104 | tf_op jit(solution)/shard_map/ppermute | solution.py:483
  53.4 4.1 %middle.1 = (bf16[512,256]{1,0:T(8,128)(2,1)}, f32[512,256]{1,0:T(8,128)S(1)}, bf16[2048,128]{1,0:T(8,128)(2,1)S(1)}, f32[16,8,128]{2,1,0:T(8,128)S(1)}, f32[64,256]{1,0:T(8,128)S(1)}) custom-call(s32[2]{0:T(128)S(1)} %pad_add_fusion.place_ref, bf16[1024,256]{1,0:T(8,128)(2,1)S(1)} %pair.3.pair_ref.x_pair, ...), custom_call_target="tpu_custom_call" | custom-call | flops 1073741824 | bytes 4194304 | tf_op jit(solution)/shard_map/middle/pallas_call | solution.py:605
  57.5 11.1 %backward.1 = (f32[16,128,128]{2,1,0:T(8,128)S(1)}, bf16[64,2048]{1,0:T(8,128)(2,1)S(1)}, bf16[256,128]{1,0:T(8,128)(2,1)S(1)}, bf16[256,128]{1,0:T(8,128)(2,1)S...) custom-call(s32[2]{0:T(128)S(1)} %pad_add_fusion.place_ref, ...), custom_call_target="tpu_custom_call" | custom-call | flops 4026531840 | bytes 4194304 | tf_op jit(solution)/shard_map/backward/pallas_call | solution.py:626
  69.5 2.9 %collective-permute-start.15 = (bf16[2,128,128]{2,1,0:T(8,128)(2,1)S(1)}, bf16[2,128,128]{2,1,0:T(8,128)(2,1)S(1)}, u32[]{:S(2)}, u32[]{:S(2)}) collective-permute-start(bf16[2,128,128]{2,1,0:T(8,128)(2,1)S(1)} %get-tuple-element.88), channel_id=1, source_target_pairs={{0,24},{4,28},{8,16},{12,20},{16,8},{20,12},{24,0},{28,4},{1,25},{... | collective-permute-start | bytes 196616 | tf_op jit(solution)/shard_map/ppermute | solution.py:483
  72.5 3.9 %collective-permute-start.17 = (bf16[2,128,128]{2,1,0:T(8,128)(2,1)S(1)}, bf16[2,128,128]{2,1,0:T(8,128)(2,1)S(1)}, u32[]{:S(2)}, u32[]{:S(2)}) collective-permute-start(bf16[2,128,128]{2,1,0:T(8,128)(2,1)S(1)} %get-tuple-element.90), channel_id=1, source_target_pairs={{0,16},{4,20},{8,24},{12,28},{16,0},{20,4},{24,8},{28,12},{1,17},{... | collective-permute-start | bytes 196616 | tf_op jit(solution)/shard_map/ppermute | solution.py:483
  76.5 4.3 %collective-permute-start.19 = (bf16[2,128,128]{2,1,0:T(8,128)(2,1)S(1)}, bf16[2,128,128]{2,1,0:T(8,128)(2,1)S(1)}, u32[]{:S(2)}, u32[]{:S(2)}) collective-permute-start(bf16[2,128,128]{2,1,0:T(8,128)(2,1)S(1)} %get-tuple-element.92), channel_id=1, source_target_pairs={{0,8},{4,12},{8,0},{12,4},{16,24},{20,28},{24,16},{28,20},{1,9},{5... | collective-permute-start | bytes 196616 | tf_op jit(solution)/shard_map/ppermute | solution.py:483
  80.8 1.5 %collective-permute-start.20 = (bf16[2,128,128]{2,1,0:T(8,128)(2,1)S(1)}, bf16[2,128,128]{2,1,0:T(8,128)(2,1)S(1)}, u32[]{:S(2)}, u32[]{:S(2)}) collective-permute-start(bf16[2,128,128]{2,1,0:T(8,128)(2,1)S(1)} %get-tuple-element.93), channel_id=1, source_target_pairs={{0,4},{4,0},{8,12},{12,8},{16,20},{20,16},{24,28},{28,24},{1,5},{5... | collective-permute-start | bytes 196616 | tf_op jit(solution)/shard_map/ppermute | solution.py:483
  85.3 1.6 %collect.1 = (bf16[768,128]{1,0:T(8,128)(2,1)S(1)}, bf16[768,128]{1,0:T(8,128)(2,1)S(1)}, bf16[1536,128]{1,0:T(8,128)(2,1)S(1)}, bf16[32,256]{1,0:T(8,128)(2,1)S...) custom-call(s32[2]{0:T(128)S(1)} %pad_add_fusion.place_ref, ...), custom_call_target="tpu_custom_call" | custom-call | flops 134217728 | bytes 4194304 | tf_op jit(solution)/shard_map/collect/pallas_call | solution.py:654
  86.9 1.5 %collective-permute-start.21 = (bf16[1536,128]{1,0:T(8,128)(2,1)S(1)}, bf16[1536,128]{1,0:T(8,128)(2,1)S(1)}, u32[]{:S(2)}, u32[]{:S(2)}) collective-permute-start(bf16[1536,128]{1,0:T(8,128)(2,1)S(1)} %get-tuple-element.103), channel_id=1, source_target_pairs={{0,2},{1,3},{2,0},{3,1},{4,6},{5,7},{6,4},{7,5},{8,10},{9,11},{10,... | collective-permute-start | bytes 1179656 | tf_op jit(solution)/shard_map/ppermute | solution.py:483
  88.9 4.1 %collective-permute-start.23 = (bf16[32,256]{1,0:T(8,128)(2,1)S(1)}, bf16[32,256]{1,0:T(8,128)(2,1)S(1)}, u32[]{:S(2)}, u32[]{:S(2)}) collective-permute-start(bf16[32,256]{1,0:T(8,128)(2,1)S(1)} %get-tuple-element.106), channel_id=1, source_target_pairs={{0,24},{4,28},{8,16},{12,20},{16,8},{20,12},{24,0},{28,4},{1,25},{... | collective-permute-start | bytes 49160 | tf_op jit(solution)/shard_map/ppermute | solution.py:483
  92.9 3.1 %collective-permute-start.25 = (bf16[32,256]{1,0:T(8,128)(2,1)S(1)}, bf16[32,256]{1,0:T(8,128)(2,1)S(1)}, u32[]{:S(2)}, u32[]{:S(2)}) collective-permute-start(bf16[32,256]{1,0:T(8,128)(2,1)S(1)} %get-tuple-element.108), channel_id=1, source_target_pairs={{0,16},{4,20},{8,24},{12,28},{16,0},{20,4},{24,8},{28,12},{1,17},{... | collective-permute-start | bytes 49160 | tf_op jit(solution)/shard_map/ppermute | solution.py:483
  96.1 2.7 %collective-permute-start.27 = (bf16[32,256]{1,0:T(8,128)(2,1)S(1)}, bf16[32,256]{1,0:T(8,128)(2,1)S(1)}, u32[]{:S(2)}, u32[]{:S(2)}) collective-permute-start(bf16[32,256]{1,0:T(8,128)(2,1)S(1)} %get-tuple-element.110), channel_id=1, source_target_pairs={{0,8},{4,12},{8,0},{12,4},{16,24},{20,28},{24,16},{28,20},{1,9},{5... | collective-permute-start | bytes 49160 | tf_op jit(solution)/shard_map/ppermute | solution.py:483
  100.7 1.8 %collective-permute-done.28.refs_7_ = bf16[32,256]{1,0:T(8,128)(2,1)S(1)} collective-permute-done((bf16[32,256]{1,0:T(8,128)(2,1)S(1)}, bf16[32,256]{1,0:T(8,128)(2,1)S(1)}, u32[]{:S(2)}, u32[]{:S(2)}) %collective-permute-start.28) | collective-permute-done | bytes 16416 | tf_op jit(solution)/shard_map/ppermute | solution.py:483
  102.9 2.0 %collective-permute-start.30 = (bf16[32,256]{1,0:T(8,128)(2,1)S(1)}, bf16[32,256]{1,0:T(8,128)(2,1)S(1)}, u32[]{:S(2)}, u32[]{:S(2)}) collective-permute-start(bf16[32,256]{1,0:T(8,128)(2,1)S(1)} %sum.1.refs_0_), channel_id=1, source_target_pairs={{0,8},{4,12},{8,0},{12,4},{16,24},{20,28},{24,16},{28,20},{1,9},{5... | collective-permute-start | bytes 49160 | tf_op jit(solution)/shard_map/ppermute | solution.py:483
  109.0 3.3 %collective-permute-start.35 = (bf16[32,256]{1,0:T(8,128)(2,1)S(1)}, bf16[32,256]{1,0:T(8,128)(2,1)S(1)}, u32[]{:S(2)}, u32[]{:S(2)}) collective-permute-start(bf16[32,256]{1,0:T(8,128)(2,1)S(1)} %sum.1.refs_0_), channel_id=1, source_target_pairs={{0,20},{4,16},{8,28},{12,24},{16,4},{20,0},{24,12},{28,8},{1,21},{... | collective-permute-start | bytes 49160 | tf_op jit(solution)/shard_map/ppermute | solution.py:483
  112.4 4.0 %collective-permute-start.33 = (bf16[32,256]{1,0:T(8,128)(2,1)S(1)}, bf16[32,256]{1,0:T(8,128)(2,1)S(1)}, u32[]{:S(2)}, u32[]{:S(2)}) collective-permute-start(bf16[32,256]{1,0:T(8,128)(2,1)S(1)} %sum.1.refs_0_), channel_id=1, source_target_pairs={{0,28},{4,24},{8,20},{12,16},{16,12},{20,8},{24,4},{28,0},{1,29},{... | collective-permute-start | bytes 49160 | tf_op jit(solution)/shard_map/ppermute | solution.py:483
  (83 shorter events, 26.9 us)
Async XLA Ops:
  0.6 15.2 %collective-permute-start = (bf16[512,256]{1,0:T(8,128)(2,1)}, bf16[512,256]{1,0:T(8,128)(2,1)S(1)}, u32[]{:S(2)}, u32[]{:S(2)}) collective-permute-start(bf16[512,256]{1,0:T(8,128)(2,1)} %refs_0_.2), channel_id=1, source_target_pairs={{0,2},{1,3},{2,0},{3,1},{4,6},{5,7},{6,4},{7,5},{8,10},{9,11},{10,... | collective-permute-start | bytes 786440 | tf_op jit(solution)/shard_map/ppermute | solution.py:483
  17.0 11.0 %collective-permute-start.2 = (bf16[512,256]{1,0:T(8,128)(2,1)S(1)}, bf16[512,256]{1,0:T(8,128)(2,1)S(1)}, u32[]{:S(2)}, u32[]{:S(2)}) collective-permute-start(bf16[512,256]{1,0:T(8,128)(2,1)S(1)} %copy-done.1), channel_id=1, source_target_pairs={{0,2},{1,3},{2,0},{3,1},{4,6},{5,7},{6,4},{7,5},{8,10},{9,11},{10,... | collective-permute-start | bytes 786440 | tf_op jit(solution)/shard_map/ppermute | solution.py:483
  20.3 7.8 %collective-permute-start.3 = (bf16[2,128,128]{2,1,0:T(8,128)(2,1)S(1)}, bf16[2,128,128]{2,1,0:T(8,128)(2,1)S(1)}, u32[]{:S(2)}, u32[]{:S(2)}) collective-permute-start(bf16[2,128,128]{2,1,0:T(8,128)(2,1)S(1)} %get-tuple-element.64), channel_id=1, source_target_pairs={{0,28},{4,24},{8,20},{12,16},{16,12},{20,8},{24,4},{28,0},{1,29},{... | collective-permute-start | bytes 196616 | tf_op jit(solution)/shard_map/ppermute | solution.py:483
  20.9 11.2 %collective-permute-start.4 = (bf16[2,128,128]{2,1,0:T(8,128)(2,1)S(1)}, bf16[2,128,128]{2,1,0:T(8,128)(2,1)S(1)}, u32[]{:S(2)}, u32[]{:S(2)}) collective-permute-start(bf16[2,128,128]{2,1,0:T(8,128)(2,1)S(1)} %get-tuple-element.65), channel_id=1, source_target_pairs={{0,24},{4,28},{8,16},{12,20},{16,8},{20,12},{24,0},{28,4},{1,25},{... | collective-permute-start | bytes 196616 | tf_op jit(solution)/shard_map/ppermute | solution.py:483
  24.2 10.4 %collective-permute-start.5 = (bf16[2,128,128]{2,1,0:T(8,128)(2,1)S(1)}, bf16[2,128,128]{2,1,0:T(8,128)(2,1)S(1)}, u32[]{:S(2)}, u32[]{:S(2)}) collective-permute-start(bf16[2,128,128]{2,1,0:T(8,128)(2,1)S(1)} %get-tuple-element.66), channel_id=1, source_target_pairs={{0,20},{4,16},{8,28},{12,24},{16,4},{20,0},{24,12},{28,8},{1,21},{... | collective-permute-start | bytes 196616 | tf_op jit(solution)/shard_map/ppermute | solution.py:483
  24.2 10.4 %collective-permute-start.6 = (bf16[2,128,128]{2,1,0:T(8,128)(2,1)S(1)}, bf16[2,128,128]{2,1,0:T(8,128)(2,1)S(1)}, u32[]{:S(2)}, u32[]{:S(2)}) collective-permute-start(bf16[2,128,128]{2,1,0:T(8,128)(2,1)S(1)} %get-tuple-element.67), channel_id=1, source_target_pairs={{0,16},{4,20},{8,24},{12,28},{16,0},{20,4},{24,8},{28,12},{1,17},{... | collective-permute-start | bytes 196616 | tf_op jit(solution)/shard_map/ppermute | solution.py:483
  28.0 7.5 %collective-permute-start.7 = (bf16[2,128,128]{2,1,0:T(8,128)(2,1)S(1)}, bf16[2,128,128]{2,1,0:T(8,128)(2,1)S(1)}, u32[]{:S(2)}, u32[]{:S(2)}) collective-permute-start(bf16[2,128,128]{2,1,0:T(8,128)(2,1)S(1)} %get-tuple-element.68), channel_id=1, source_target_pairs={{0,12},{4,8},{8,4},{12,0},{16,28},{20,24},{24,20},{28,16},{1,13},{... | collective-permute-start | bytes 196616 | tf_op jit(solution)/shard_map/ppermute | solution.py:483
  28.1 7.4 %collective-permute-start.8 = (bf16[2,128,128]{2,1,0:T(8,128)(2,1)S(1)}, bf16[2,128,128]{2,1,0:T(8,128)(2,1)S(1)}, u32[]{:S(2)}, u32[]{:S(2)}) collective-permute-start(bf16[2,128,128]{2,1,0:T(8,128)(2,1)S(1)} %get-tuple-element.69), channel_id=1, source_target_pairs={{0,8},{4,12},{8,0},{12,4},{16,24},{20,28},{24,16},{28,20},{1,9},{5... | collective-permute-start | bytes 196616 | tf_op jit(solution)/shard_map/ppermute | solution.py:483
  41.1 6.9 %collective-permute-start.11 = (bf16[512,128]{1,0:T(8,128)(2,1)S(1)}, bf16[512,128]{1,0:T(8,128)(2,1)S(1)}, u32[]{:S(2)}, u32[]{:S(2)}) collective-permute-start(bf16[512,128]{1,0:T(8,128)(2,1)S(1)} %get-tuple-element.77.refs_0_), channel_id=1, source_target_pairs={{0,2},{1,3},{2,0},{3,1},{4,6},{5,7},{6,4},{7,5},{8,10},{9,11},{10,... | collective-permute-start | bytes 393224 | tf_op jit(solution)/shard_map/ppermute | solution.py:483
  68.7 7.8 %collective-permute-start.14 = (bf16[2,128,128]{2,1,0:T(8,128)(2,1)S(1)}, bf16[2,128,128]{2,1,0:T(8,128)(2,1)S(1)}, u32[]{:S(2)}, u32[]{:S(2)}) collective-permute-start(bf16[2,128,128]{2,1,0:T(8,128)(2,1)S(1)} %get-tuple-element.87), channel_id=1, source_target_pairs={{0,28},{4,24},{8,20},{12,16},{16,12},{20,8},{24,4},{28,0},{1,29},{... | collective-permute-start | bytes 196616 | tf_op jit(solution)/shard_map/ppermute | solution.py:483
  69.5 11.3 %collective-permute-start.15 = (bf16[2,128,128]{2,1,0:T(8,128)(2,1)S(1)}, bf16[2,128,128]{2,1,0:T(8,128)(2,1)S(1)}, u32[]{:S(2)}, u32[]{:S(2)}) collective-permute-start(bf16[2,128,128]{2,1,0:T(8,128)(2,1)S(1)} %get-tuple-element.88), channel_id=1, source_target_pairs={{0,24},{4,28},{8,16},{12,20},{16,8},{20,12},{24,0},{28,4},{1,25},{... | collective-permute-start | bytes 196616 | tf_op jit(solution)/shard_map/ppermute | solution.py:483
  72.5 10.8 %collective-permute-start.16 = (bf16[2,128,128]{2,1,0:T(8,128)(2,1)S(1)}, bf16[2,128,128]{2,1,0:T(8,128)(2,1)S(1)}, u32[]{:S(2)}, u32[]{:S(2)}) collective-permute-start(bf16[2,128,128]{2,1,0:T(8,128)(2,1)S(1)} %get-tuple-element.89), channel_id=1, source_target_pairs={{0,20},{4,16},{8,28},{12,24},{16,4},{20,0},{24,12},{28,8},{1,21},{... | collective-permute-start | bytes 196616 | tf_op jit(solution)/shard_map/ppermute | solution.py:483
  72.5 11.5 %collective-permute-start.17 = (bf16[2,128,128]{2,1,0:T(8,128)(2,1)S(1)}, bf16[2,128,128]{2,1,0:T(8,128)(2,1)S(1)}, u32[]{:S(2)}, u32[]{:S(2)}) collective-permute-start(bf16[2,128,128]{2,1,0:T(8,128)(2,1)S(1)} %get-tuple-element.90), channel_id=1, source_target_pairs={{0,16},{4,20},{8,24},{12,28},{16,0},{20,4},{24,8},{28,12},{1,17},{... | collective-permute-start | bytes 196616 | tf_op jit(solution)/shard_map/ppermute | solution.py:483
  76.4 8.4 %collective-permute-start.18 = (bf16[2,128,128]{2,1,0:T(8,128)(2,1)S(1)}, bf16[2,128,128]{2,1,0:T(8,128)(2,1)S(1)}, u32[]{:S(2)}, u32[]{:S(2)}) collective-permute-start(bf16[2,128,128]{2,1,0:T(8,128)(2,1)S(1)} %get-tuple-element.91), channel_id=1, source_target_pairs={{0,12},{4,8},{8,4},{12,0},{16,28},{20,24},{24,20},{28,16},{1,13},{... | collective-permute-start | bytes 196616 | tf_op jit(solution)/shard_map/ppermute | solution.py:483
  76.5 8.3 %collective-permute-start.19 = (bf16[2,128,128]{2,1,0:T(8,128)(2,1)S(1)}, bf16[2,128,128]{2,1,0:T(8,128)(2,1)S(1)}, u32[]{:S(2)}, u32[]{:S(2)}) collective-permute-start(bf16[2,128,128]{2,1,0:T(8,128)(2,1)S(1)} %get-tuple-element.92), channel_id=1, source_target_pairs={{0,8},{4,12},{8,0},{12,4},{16,24},{20,28},{24,16},{28,20},{1,9},{5... | collective-permute-start | bytes 196616 | tf_op jit(solution)/shard_map/ppermute | solution.py:483
  86.9 21.7 %collective-permute-start.21 = (bf16[1536,128]{1,0:T(8,128)(2,1)S(1)}, bf16[1536,128]{1,0:T(8,128)(2,1)S(1)}, u32[]{:S(2)}, u32[]{:S(2)}) collective-permute-start(bf16[1536,128]{1,0:T(8,128)(2,1)S(1)} %get-tuple-element.103), channel_id=1, source_target_pairs={{0,2},{1,3},{2,0},{3,1},{4,6},{5,7},{6,4},{7,5},{8,10},{9,11},{10,... | collective-permute-start | bytes 1179656 | tf_op jit(solution)/shard_map/ppermute | solution.py:483
  88.4 7.7 %collective-permute-start.22 = (bf16[32,256]{1,0:T(8,128)(2,1)S(1)}, bf16[32,256]{1,0:T(8,128)(2,1)S(1)}, u32[]{:S(2)}, u32[]{:S(2)}) collective-permute-start(bf16[32,256]{1,0:T(8,128)(2,1)S(1)} %get-tuple-element.105), channel_id=1, source_target_pairs={{0,28},{4,24},{8,20},{12,16},{16,12},{20,8},{24,4},{28,0},{1,29},{... | collective-permute-start | bytes 49160 | tf_op jit(solution)/shard_map/ppermute | solution.py:483
  88.9 7.2 %collective-permute-start.23 = (bf16[32,256]{1,0:T(8,128)(2,1)S(1)}, bf16[32,256]{1,0:T(8,128)(2,1)S(1)}, u32[]{:S(2)}, u32[]{:S(2)}) collective-permute-start(bf16[32,256]{1,0:T(8,128)(2,1)S(1)} %get-tuple-element.106), channel_id=1, source_target_pairs={{0,24},{4,28},{8,16},{12,20},{16,8},{20,12},{24,0},{28,4},{1,25},{... | collective-permute-start | bytes 49160 | tf_op jit(solution)/shard_map/ppermute | solution.py:483
  92.9 5.9 %collective-permute-start.24 = (bf16[32,256]{1,0:T(8,128)(2,1)S(1)}, bf16[32,256]{1,0:T(8,128)(2,1)S(1)}, u32[]{:S(2)}, u32[]{:S(2)}) collective-permute-start(bf16[32,256]{1,0:T(8,128)(2,1)S(1)} %get-tuple-element.107), channel_id=1, source_target_pairs={{0,20},{4,16},{8,28},{12,24},{16,4},{20,0},{24,12},{28,8},{1,21},{... | collective-permute-start | bytes 49160 | tf_op jit(solution)/shard_map/ppermute | solution.py:483
  92.9 6.6 %collective-permute-start.25 = (bf16[32,256]{1,0:T(8,128)(2,1)S(1)}, bf16[32,256]{1,0:T(8,128)(2,1)S(1)}, u32[]{:S(2)}, u32[]{:S(2)}) collective-permute-start(bf16[32,256]{1,0:T(8,128)(2,1)S(1)} %get-tuple-element.108), channel_id=1, source_target_pairs={{0,16},{4,20},{8,24},{12,28},{16,0},{20,4},{24,8},{28,12},{1,17},{... | collective-permute-start | bytes 49160 | tf_op jit(solution)/shard_map/ppermute | solution.py:483
  108.6 7.8 %collective-permute-start.32 = (bf16[1536,128]{1,0:T(8,128)(2,1)S(1)}, bf16[1536,128]{1,0:T(8,128)(2,1)S(1)}, u32[]{:S(2)}, u32[]{:S(2)}) collective-permute-start(bf16[1536,128]{1,0:T(8,128)(2,1)S(1)} %relay.1), channel_id=1, source_target_pairs={{0,1},{1,0},{2,3},{3,2},{4,5},{5,4},{6,7},{7,6},{8,9},{9,8},{10,11... | collective-permute-start | bytes 1179656 | tf_op jit(solution)/shard_map/ppermute | solution.py:483
  108.7 9.0 %collective-permute-start.36 = (bf16[32,256]{1,0:T(8,128)(2,1)S(1)}, bf16[32,256]{1,0:T(8,128)(2,1)S(1)}, u32[]{:S(2)}, u32[]{:S(2)}) collective-permute-start(bf16[32,256]{1,0:T(8,128)(2,1)S(1)} %sum.1.refs_0_), channel_id=1, source_target_pairs={{0,16},{4,20},{8,24},{12,28},{16,0},{20,4},{24,8},{28,12},{1,17},{... | collective-permute-start | bytes 49160 | tf_op jit(solution)/shard_map/ppermute | solution.py:483
  109.0 8.7 %collective-permute-start.35 = (bf16[32,256]{1,0:T(8,128)(2,1)S(1)}, bf16[32,256]{1,0:T(8,128)(2,1)S(1)}, u32[]{:S(2)}, u32[]{:S(2)}) collective-permute-start(bf16[32,256]{1,0:T(8,128)(2,1)S(1)} %sum.1.refs_0_), channel_id=1, source_target_pairs={{0,20},{4,16},{8,28},{12,24},{16,4},{20,0},{24,12},{28,8},{1,21},{... | collective-permute-start | bytes 49160 | tf_op jit(solution)/shard_map/ppermute | solution.py:483
  112.4 6.4 %collective-permute-start.33 = (bf16[32,256]{1,0:T(8,128)(2,1)S(1)}, bf16[32,256]{1,0:T(8,128)(2,1)S(1)}, u32[]{:S(2)}, u32[]{:S(2)}) collective-permute-start(bf16[32,256]{1,0:T(8,128)(2,1)S(1)} %sum.1.refs_0_), channel_id=1, source_target_pairs={{0,28},{4,24},{8,20},{12,16},{16,12},{20,8},{24,4},{28,0},{1,29},{... | collective-permute-start | bytes 49160 | tf_op jit(solution)/shard_map/ppermute | solution.py:483
  (20 other events, 76.6 us)

commit v3 on v1

--- a/solution.py
+++ b/solution.py
@@ -131,8 +131,12 @@
     return [0] + list(range(count - 1, 0, -1))
 
 
-def by_mask(refs):
-    order = issue_order(len(refs))
+def back_order(count):
+    near, far = list(range(1, count // 2)), list(range(count // 2, count))
+    return [0] + far[:2] + near + far[2:]
+
+
+def by_mask(refs, order):
     return [refs[order.index(m)] for m in range(len(refs))]
 
 
@@ -187,7 +191,7 @@
 
 
 def early_forward_kernel(count, place_ref, slot_ref, count_ref, qz_ref, kv_ref, kvt_ref, *refs):
-    in_refs, refs = by_mask(refs[:count]), refs[count:]
+    in_refs, refs = by_mask(refs[:count], issue_order(count)), refs[count:]
     att_ref, attt_ref, table_ref, tablet_ref, top_ref, inv_ref, even_ref, odd_ref = refs
     table_kernel_part(place_ref[1], kv_ref, kvt_ref, in_refs, table_ref, tablet_ref)
     attend_blocks(
@@ -401,11 +405,9 @@
 
 
 def collect_kernel(count, place_ref, wanted_ref, own_ref, *refs):
-    back_refs, dq_refs, refs = by_mask(refs[:count]), refs[count : count + 4], refs[count + 4 :]
+    back_refs, dq_refs, refs = by_mask(refs[:count], back_order(count)), refs[count : count + 4], refs[count + 4 :]
     xt_ref, owg_ref, qwg_ref, refs = *refs[:3], refs[3:]
-    own_send, beside_send, across_send, piece_refs, sum_ref = *refs[:3], refs[3:7], refs[7]
-    size = own_send.shape[0]
-    send_refs = (own_send, beside_send, across_send.at[:size], across_send.at[size:])
+    send_refs, piece_refs, sum_ref = refs[:4], refs[4:8], refs[8]
     head, node = place_ref[0], place_ref[1]
     sum_ref[...] = own_ref[...]
     for m in range(count):
@@ -425,19 +427,12 @@
     split(every, group_of(node, top_shift(count)), piece_refs)
 
 
-def relay_kernel(beside_ref, across_ref, after_ref, out_ref):
-    size = beside_ref.shape[0]
-    out_ref[:size, :] = beside_ref[...]
-    out_ref[size:, :] = across_ref[size:, :]
-
-
-def finish_kernel(grad_from, own_ref, beside_ref, across_ref, wq_ref, wkv_ref, out_ref, done_ref, grad_ref, sem):
+def finish_kernel(grad_from, s0, s3, s2, s1, wq_ref, wkv_ref, out_ref, done_ref, grad_ref, sem):
     done_ref[...] = jnp.zeros_like(done_ref)
     grad_copy = pltpu.make_async_copy(grad_from, grad_ref, sem)
     grad_copy.start()
     rows = out_ref.shape[0]
-    size = own_ref.shape[0]
-    s_refs = (own_ref, beside_ref.at[:size], across_ref.at[:size], beside_ref.at[size:])
+    s_refs = (s0, s1, s2, s3)
     kv = jnp.concatenate([s[:rows, :] for s in s_refs], axis=1)
     base = dot_last(kv, wkv_ref[...])
     lhs = jnp.concatenate([s[rows:, :] for s in s_refs], axis=1)
@@ -510,9 +505,9 @@
                 [piece],
                 [smem()] + [vmem()] * 4,
                 limit,
-            )(place, *add_nodes(lower, shift - 2, 1.0)[0])
+            )(place, *add_nodes(lower, shift - 2, 1.0))
         total = total.astype(pieces[0].dtype)
-        return exchange([total] * 4, "node", 1 << shift), total
+        return exchange([total] * 4, "node", 1 << shift)
 
     order = issue_order(node_count)
     across = swap(features, "head", 2)
@@ -626,34 +621,28 @@
         flops=2 * node_rows * D * HD,
         scratch=[pltpu.VMEM((HEADS, D, BLOCK), BF16), pltpu.VMEM((HEADS, 2 * D, BLOCK), BF16)],
     )(place, dqt, *xs, in_weight)
-    sent = ((rows * 3 // 2, BLOCK), BF16)
     collected = call(
         functools.partial(collect_kernel, node_count),
         "collect",
-        [sent, sent, ((rows * 3, BLOCK), BF16)] + [((HD, D), BF16)] * 4,
+        [((rows * 3 // 2, BLOCK), BF16)] * 4 + [((HD, D), BF16)] * 4,
         [smem()] * 2 + [vmem()] * (8 + node_count),
         limit,
         flops=2 * node_rows * D * BLOCK,
         scratch=[pltpu.VMEM((BLK, BLOCK, BLOCK), F32)],
-    )(place, wants, own, *[returned[m] for m in order], *rest[:4], xt, owg, query_wg)
-    own_send, beside_send, across_send = collected[:3]
-    across = swap(across_send, "head", 2)
+    )(place, wants, own, *[returned[m] for m in back_order(node_count)], *rest[:4], xt, owg, query_wg)
+    arrived = exchange(collected[:4], "head")
     shift = top_shift(node_count)
     factor = total_nodes ** (-0.5)
-    late, summed = add_nodes(collected[3:], shift, factor)
-    (relay,) = call(
-        relay_kernel, "relay", [((rows * 3, BLOCK), BF16)], [vmem()] * 3, 4 * MIB
-    )(beside_send, across, summed)
-    beside = swap(relay, "head", 1)
+    late = add_nodes(collected[4:], shift, factor)
     feature_grad, finished = call(
         finish_kernel,
         "finish",
         [((rows, D), BF16), ((8, BLOCK), F32)],
-        [hbm()] + [vmem()] * 5,
+        [hbm()] + [vmem()] * 6,
         limit,
         flops=4 * rows * 3 * D * D,
         scratch=[pltpu.VMEM((rows, D), F32), pltpu.SemaphoreType.DMA],
-    )(norm_grad, own_send, beside, across, wq, wkv)
+    )(norm_grad, arrived[0], *arrived[:0:-1], wq, wkv)
     in_grad, out_grad = call(
         functools.partial(result_kernel, shift),
         "result",

time: 108 us -> 109 us (level)
  waiting for transfers between devices: 18.4 us -> 23.8 us
  starting transfers between devices: 43 us -> 38.5 us
    ppermute x30 -> x31, waiting for transfers between devices: 18.4 us -> 23.8 us  [swap(): return lax.ppermute(value, axis, [(i, i ^ mask) for i in range(size)])]
    ppermute x30 -> x31, starting transfers between devices: 43 us -> 38.5 us  [swap(): return lax.ppermute(value, axis, [(i, i ^ mask) for i in range(size)])]
  transfers between devices with their start and end apart: 30 -> 31, of which waited for: 17 -> 16; matrix products, arithmetic and copies ran while one was open for 0% -> 0% of each run, Pallas kernels for 9% -> 9%
where the time goes in v3:
time: 109 us
  starting transfers between devices  38.5 us (35%)
  Pallas kernels  31.8 us (29%)
  waiting for transfers between devices  23.8 us (22%)
  blocking collectives  12.1 us (11%)
  local copies, waits for them, and re-layouts  1.49 us (1%)
    ppermute x31, starting transfers between devices, swap(): return lax.ppermute(value, axis, [(i, i ^ mask) for i in range(size)])  38.5 us
    ppermute x31, waiting for transfers between devices, swap(): return lax.ppermute(value, axis, [(i, i ^ mask) for i in range(size)])  23.8 us
    all_to_all x1, blocking collectives, on_device(): lax.all_to_all(wanted.reshape(node_count, 1, CAP), 'node', split_axis=0,...  12.1 us
    pallas_call x1, Pallas kernels, on_device(): call(functools.partial(backward_kernel, node_count), 'backward', [((BLK,...  11 us
    pallas_call x1, Pallas kernels, on_device(): call(functools.partial(early_forward_kernel, node_count), 'early_forward'...  4.66 us
    pallas_call x1, Pallas kernels, on_device(): call(late_forward_kernel, 'late_forward', [half_att, ((HD, node_rows), BF...  4.48 us
    pallas_call x1, Pallas kernels, on_device(): call(middle_kernel, 'middle', [((rows, D), BF16), ((rows, D), F32), ((nod...  4.07 us
  transfers between devices with their start and end apart: 31, of which 16 were waited for; matrix products, arithmetic and copies ran while one was open for 0% of the time, Pallas kernels for 9%

profile of v3, /device:TPU:0, one launch (start us, length us, event | category | flops | bytes accessed | tf_op | source)
XLA Modules:
  0.0 108.7 jit_solution(15913287998414121411)
XLA Ops:
  0.6 3.0 %collective-permute-start = (bf16[512,256]{1,0:T(8,128)(2,1)}, bf16[512,256]{1,0:T(8,128)(2,1)S(1)}, u32[]{:S(2)}, u32[]{:S(2)}) collective-permute-start(bf16[512,256]{1,0:T(8,128)(2,1)} %refs_0_.2), channel_id=1, source_target_pairs={{0,2},{1,3},{2,0},{3,1},{4,6},{5,7},{6,4},{7,5},{8,10},{9,11},{10,... | collective-permute-start | bytes 786440 | tf_op jit(solution)/shard_map/ppermute | solution.py:463
  3.7 12.1 %all_to_all.5.refs_2_.wanted_ref = s32[8,1,2]{2,1,0:T(1,128)S(1)} all-to-all(s32[8,1,2]{2,1,0:T(1,128)S(1)} %copy.11), channel_id=1, replica_groups=mesh['node'=8,'head'=4] {'node'}, dimensions={0} | all-to-all | bytes 128 | tf_op jit(solution)/shard_map/all_to_all | solution.py:515
  20.9 3.2 %collective-permute-start.4 = (bf16[2,128,128]{2,1,0:T(8,128)(2,1)S(1)}, bf16[2,128,128]{2,1,0:T(8,128)(2,1)S(1)}, u32[]{:S(2)}, u32[]{:S(2)}) collective-permute-start(bf16[2,128,128]{2,1,0:T(8,128)(2,1)S(1)} %get-tuple-element.65), channel_id=1, source_target_pairs={{0,24},{4,28},{8,16},{12,20},{16,8},{20,12},{24,0},{28,4},{1,25},{... | collective-permute-start | bytes 196616 | tf_op jit(solution)/shard_map/ppermute | solution.py:463
  24.2 3.8 %collective-permute-start.6 = (bf16[2,128,128]{2,1,0:T(8,128)(2,1)S(1)}, bf16[2,128,128]{2,1,0:T(8,128)(2,1)S(1)}, u32[]{:S(2)}, u32[]{:S(2)}) collective-permute-start(bf16[2,128,128]{2,1,0:T(8,128)(2,1)S(1)} %get-tuple-element.67), channel_id=1, source_target_pairs={{0,16},{4,20},{8,24},{12,28},{16,0},{20,4},{24,8},{28,12},{1,17},{... | collective-permute-start | bytes 196616 | tf_op jit(solution)/shard_map/ppermute | solution.py:463
  28.1 4.0 %collective-permute-start.8 = (bf16[2,128,128]{2,1,0:T(8,128)(2,1)S(1)}, bf16[2,128,128]{2,1,0:T(8,128)(2,1)S(1)}, u32[]{:S(2)}, u32[]{:S(2)}) collective-permute-start(bf16[2,128,128]{2,1,0:T(8,128)(2,1)S(1)} %get-tuple-element.69), channel_id=1, source_target_pairs={{0,8},{4,12},{8,0},{12,4},{16,24},{20,28},{24,16},{28,20},{1,9},{5... | collective-permute-start | bytes 196616 | tf_op jit(solution)/shard_map/ppermute | solution.py:463
  36.4 4.7 %early_forward.1 = (bf16[512,128]{1,0:T(8,128)(2,1)S(1)}, bf16[64,1024]{1,0:T(8,128)(2,1)S(1)}, bf16[32,128,128]{2,1,0:T(8,128)(2,1)S(1)}, bf16[32,128,128]{2,1,...) custom-call(s32[2]{0:T(128)S(1)} %pad_add_fusion.place_ref, s32[16,12]{1,0:T(8,128)S(1)} %copy-done.3, ...), custom_call_target="tpu_custom_call" | custom-call | flops 805306368 | bytes 4194304 | tf_op jit(solution)/shard_map/early_forward/pallas_call | solution.py:543
  41.7 4.5 %late_forward.1 = (bf16[512,128]{1,0:T(8,128)(2,1)S(1)}, bf16[64,2048]{1,0:T(8,128)(2,1)S(1)}, f32[16,8,128]{2,1,0:T(8,128)S(1)}, f32[16,8,128]{2,1,0:T(8,128)S(1)}) custom-call(s32[16,12]{1,0:T(8,128)S(1)} %copy-done.3, s32[16]{0:T(128)S(1)} %copy-done.4, bf16[2048,128]{1,0:T(8,128)(2,1)S(1)} %get-tuple-element.60.qz_ref, ...), custom_call_target="tpu_custom_call" | custom-call | flops 805306368 | bytes 4194304 | tf_op jit(solution)/shard_map/late_forward/pallas_call | solution.py:560
  46.2 1.5 %collective-permute-start.12 = (bf16[512,128]{1,0:T(8,128)(2,1)S(1)}, bf16[512,128]{1,0:T(8,128)(2,1)S(1)}, u32[]{:S(2)}, u32[]{:S(2)}) collective-permute-start(bf16[512,128]{1,0:T(8,128)(2,1)S(1)} %get-tuple-element.78.refs_1_), channel_id=1, source_target_pairs={{0,2},{1,3},{2,0},{3,1},{4,6},{5,7},{6,4},{7,5},{8,10},{9,11},{10,... | collective-permute-start | bytes 393224 | tf_op jit(solution)/shard_map/ppermute | solution.py:463
  47.8 3.4 %collective-permute-done.12.refs_3_ = bf16[512,128]{1,0:T(8,128)(2,1)S(1)} collective-permute-done((bf16[512,128]{1,0:T(8,128)(2,1)S(1)}, bf16[512,128]{1,0:T(8,128)(2,1)S(1)}, u32[]{:S(2)}, u32[]{:S(2)}) %collective-permute-start.12) | collective-permute-done | bytes 131104 | tf_op jit(solution)/shard_map/ppermute | solution.py:463
  51.3 1.9 %collective-permute-done.13.a_other = bf16[2048,128]{1,0:T(8,128)(2,1)S(1)} collective-permute-done((bf16[2048,128]{1,0:T(8,128)(2,1)S(1)}, bf16[2048,128]{1,0:T(8,128)(2,1)S(1)}, u32[]{:S(2)}, u32[]{:S(2)}) %collective-permute-start.13) | collective-permute-done | bytes 524320 | tf_op jit(solution)/shard_map/ppermute | solution.py:463
  53.2 4.1 %middle.1 = (bf16[512,256]{1,0:T(8,128)(2,1)}, f32[512,256]{1,0:T(8,128)S(1)}, bf16[2048,128]{1,0:T(8,128)(2,1)S(1)}, f32[16,8,128]{2,1,0:T(8,128)S(1)}, f32[64,256]{1,0:T(8,128)S(1)}) custom-call(s32[2]{0:T(128)S(1)} %pad_add_fusion.place_ref, bf16[1024,256]{1,0:T(8,128)(2,1)S(1)} %pair.3.pair_ref.x_pair, ...), custom_call_target="tpu_custom_call" | custom-call | flops 1073741824 | bytes 4194304 | tf_op jit(solution)/shard_map/middle/pallas_call | solution.py:577
  57.3 11.0 %backward.1 = (f32[16,128,128]{2,1,0:T(8,128)S(1)}, bf16[64,2048]{1,0:T(8,128)(2,1)S(1)}, bf16[256,128]{1,0:T(8,128)(2,1)S(1)}, bf16[256,128]{1,0:T(8,128)(2,1)S...) custom-call(s32[2]{0:T(128)S(1)} %pad_add_fusion.place_ref, ...), custom_call_target="tpu_custom_call" | custom-call | flops 4026531840 | bytes 4194304 | tf_op jit(solution)/shard_map/backward/pallas_call | solution.py:598
  68.4 2.8 %collective-permute-start.15 = (bf16[2,128,128]{2,1,0:T(8,128)(2,1)S(1)}, bf16[2,128,128]{2,1,0:T(8,128)(2,1)S(1)}, u32[]{:S(2)}, u32[]{:S(2)}) collective-permute-start(bf16[2,128,128]{2,1,0:T(8,128)(2,1)S(1)} %get-tuple-element.88), channel_id=1, source_target_pairs={{0,20},{4,16},{8,28},{12,24},{16,4},{20,0},{24,12},{28,8},{1,21},{... | collective-permute-start | bytes 196616 | tf_op jit(solution)/shard_map/ppermute | solution.py:463
  71.2 1.6 %collective-permute-start.16 = (bf16[2,128,128]{2,1,0:T(8,128)(2,1)S(1)}, bf16[2,128,128]{2,1,0:T(8,128)(2,1)S(1)}, u32[]{:S(2)}, u32[]{:S(2)}) collective-permute-start(bf16[2,128,128]{2,1,0:T(8,128)(2,1)S(1)} %get-tuple-element.89), channel_id=1, source_target_pairs={{0,4},{4,0},{8,12},{12,8},{16,20},{20,16},{24,28},{28,24},{1,5},{5... | collective-permute-start | bytes 196616 | tf_op jit(solution)/shard_map/ppermute | solution.py:463
  74.7 1.9 %collective-permute-done.14.refs_1_ = bf16[2,128,128]{2,1,0:T(8,128)(2,1)S(1)} collective-permute-done((bf16[2,128,128]{2,1,0:T(8,128)(2,1)S(1)}, bf16[2,128,128]{2,1,0:T(8,128)(2,1)S(1)}, u32[]{:S(2)}, u32[]{:S(2)}) %collective-permute-start.14) | collective-permute-done | bytes 65568 | tf_op jit(solution)/shard_map/ppermute | solution.py:463
  78.0 2.6 %collective-permute-start.20 = (bf16[2,128,128]{2,1,0:T(8,128)(2,1)S(1)}, bf16[2,128,128]{2,1,0:T(8,128)(2,1)S(1)}, u32[]{:S(2)}, u32[]{:S(2)}) collective-permute-start(bf16[2,128,128]{2,1,0:T(8,128)(2,1)S(1)} %get-tuple-element.93), channel_id=1, source_target_pairs={{0,28},{4,24},{8,20},{12,16},{16,12},{20,8},{24,4},{28,0},{1,29},{... | collective-permute-start | bytes 196616 | tf_op jit(solution)/shard_map/ppermute | solution.py:463
  82.7 2.3 %collective-permute-done.20.refs_7_ = bf16[2,128,128]{2,1,0:T(8,128)(2,1)S(1)} collective-permute-done((bf16[2,128,128]{2,1,0:T(8,128)(2,1)S(1)}, bf16[2,128,128]{2,1,0:T(8,128)(2,1)S(1)}, u32[]{:S(2)}, u32[]{:S(2)}) %collective-permute-start.20) | collective-permute-done | bytes 65568 | tf_op jit(solution)/shard_map/ppermute | solution.py:463
  86.4 2.5 %collective-permute-start.24 = (bf16[64,256]{1,0:T(8,128)(2,1)S(1)}, bf16[64,256]{1,0:T(8,128)(2,1)S(1)}, u32[]{:S(2)}, u32[]{:S(2)}) collective-permute-start(bf16[64,256]{1,0:T(8,128)(2,1)S(1)} %get-tuple-element.110), channel_id=1, source_target_pairs={{0,24},{4,28},{8,16},{12,20},{16,8},{20,12},{24,0},{28,4},{1,25},{... | collective-permute-start | bytes 98312 | tf_op jit(solution)/shard_map/ppermute | solution.py:463
  88.9 2.0 %collective-permute-start.26 = (bf16[64,256]{1,0:T(8,128)(2,1)S(1)}, bf16[64,256]{1,0:T(8,128)(2,1)S(1)}, u32[]{:S(2)}, u32[]{:S(2)}) collective-permute-start(bf16[64,256]{1,0:T(8,128)(2,1)S(1)} %get-tuple-element.112), channel_id=1, source_target_pairs={{0,8},{4,12},{8,0},{12,4},{16,24},{20,28},{24,16},{28,20},{1,9},{5... | collective-permute-start | bytes 98312 | tf_op jit(solution)/shard_map/ppermute | solution.py:463
  92.2 1.5 %collective-permute-done.25.refs_2_ = bf16[64,256]{1,0:T(8,128)(2,1)S(1)} collective-permute-done((bf16[64,256]{1,0:T(8,128)(2,1)S(1)}, bf16[64,256]{1,0:T(8,128)(2,1)S(1)}, u32[]{:S(2)}, u32[]{:S(2)}) %collective-permute-start.25) | collective-permute-done | bytes 32800 | tf_op jit(solution)/shard_map/ppermute | solution.py:463
  96.5 1.5 %collective-permute-done.27 = f32[64,256]{1,0:T(8,128)S(1)} collective-permute-done((f32[64,256]{1,0:T(8,128)S(1)}, f32[64,256]{1,0:T(8,128)S(1)}, u32[]{:S(2)}, u32[]{:S(2)}) %collective-permute-start.27) | collective-permute-done | bytes 65568 | tf_op jit(solution)/shard_map/ppermute | solution.py:463
  98.1 1.9 %collective-permute-start.30 = (bf16[64,256]{1,0:T(8,128)(2,1)S(1)}, bf16[64,256]{1,0:T(8,128)(2,1)S(1)}, u32[]{:S(2)}, u32[]{:S(2)}) collective-permute-start(bf16[64,256]{1,0:T(8,128)(2,1)S(1)} %add_convert_fusion.l0), channel_id=1, source_target_pairs={{0,24},{4,28},{8,16},{12,20},{16,8},{20,12},{24,0},{28,4},{1,25},{... | collective-permute-start | bytes 98312 | tf_op jit(solution)/shard_map/ppermute | solution.py:463
  101.9 1.7 %collective-permute-start.28 = (bf16[64,256]{1,0:T(8,128)(2,1)S(1)}, bf16[64,256]{1,0:T(8,128)(2,1)S(1)}, u32[]{:S(2)}, u32[]{:S(2)}) collective-permute-start(bf16[64,256]{1,0:T(8,128)(2,1)S(1)} %add_convert_fusion.l0), channel_id=1, source_target_pairs={{0,8},{4,12},{8,0},{12,4},{16,24},{20,28},{24,16},{28,20},{1,9},{5... | collective-permute-start | bytes 98312 | tf_op jit(solution)/shard_map/ppermute | solution.py:463
  103.5 2.5 %collective-permute-done.22.s2 = bf16[768,128]{1,0:T(8,128)(2,1)S(1)} collective-permute-done((bf16[768,128]{1,0:T(8,128)(2,1)S(1)}, bf16[768,128]{1,0:T(8,128)(2,1)S(1)}, u32[]{:S(2)}, u32[]{:S(2)}) %collective-permute-start.22) | collective-permute-done | bytes 196640 | tf_op jit(solution)/shard_map/ppermute | solution.py:463
  (70 shorter events, 25.9 us)
Async XLA Ops:
  0.6 15.2 %collective-permute-start = (bf16[512,256]{1,0:T(8,128)(2,1)}, bf16[512,256]{1,0:T(8,128)(2,1)S(1)}, u32[]{:S(2)}, u32[]{:S(2)}) collective-permute-start(bf16[512,256]{1,0:T(8,128)(2,1)} %refs_0_.2), channel_id=1, source_target_pairs={{0,2},{1,3},{2,0},{3,1},{4,6},{5,7},{6,4},{7,5},{8,10},{9,11},{10,... | collective-permute-start | bytes 786440 | tf_op jit(solution)/shard_map/ppermute | solution.py:463
  17.0 11.0 %collective-permute-start.2 = (bf16[512,256]{1,0:T(8,128)(2,1)S(1)}, bf16[512,256]{1,0:T(8,128)(2,1)S(1)}, u32[]{:S(2)}, u32[]{:S(2)}) collective-permute-start(bf16[512,256]{1,0:T(8,128)(2,1)S(1)} %copy-done.1), channel_id=1, source_target_pairs={{0,2},{1,3},{2,0},{3,1},{4,6},{5,7},{6,4},{7,5},{8,10},{9,11},{10,... | collective-permute-start | bytes 786440 | tf_op jit(solution)/shard_map/ppermute | solution.py:463
  20.3 7.8 %collective-permute-start.3 = (bf16[2,128,128]{2,1,0:T(8,128)(2,1)S(1)}, bf16[2,128,128]{2,1,0:T(8,128)(2,1)S(1)}, u32[]{:S(2)}, u32[]{:S(2)}) collective-permute-start(bf16[2,128,128]{2,1,0:T(8,128)(2,1)S(1)} %get-tuple-element.64), channel_id=1, source_target_pairs={{0,28},{4,24},{8,20},{12,16},{16,12},{20,8},{24,4},{28,0},{1,29},{... | collective-permute-start | bytes 196616 | tf_op jit(solution)/shard_map/ppermute | solution.py:463
  20.9 11.2 %collective-permute-start.4 = (bf16[2,128,128]{2,1,0:T(8,128)(2,1)S(1)}, bf16[2,128,128]{2,1,0:T(8,128)(2,1)S(1)}, u32[]{:S(2)}, u32[]{:S(2)}) collective-permute-start(bf16[2,128,128]{2,1,0:T(8,128)(2,1)S(1)} %get-tuple-element.65), channel_id=1, source_target_pairs={{0,24},{4,28},{8,16},{12,20},{16,8},{20,12},{24,0},{28,4},{1,25},{... | collective-permute-start | bytes 196616 | tf_op jit(solution)/shard_map/ppermute | solution.py:463
  24.2 10.4 %collective-permute-start.5 = (bf16[2,128,128]{2,1,0:T(8,128)(2,1)S(1)}, bf16[2,128,128]{2,1,0:T(8,128)(2,1)S(1)}, u32[]{:S(2)}, u32[]{:S(2)}) collective-permute-start(bf16[2,128,128]{2,1,0:T(8,128)(2,1)S(1)} %get-tuple-element.66), channel_id=1, source_target_pairs={{0,20},{4,16},{8,28},{12,24},{16,4},{20,0},{24,12},{28,8},{1,21},{... | collective-permute-start | bytes 196616 | tf_op jit(solution)/shard_map/ppermute | solution.py:463
  24.2 10.4 %collective-permute-start.6 = (bf16[2,128,128]{2,1,0:T(8,128)(2,1)S(1)}, bf16[2,128,128]{2,1,0:T(8,128)(2,1)S(1)}, u32[]{:S(2)}, u32[]{:S(2)}) collective-permute-start(bf16[2,128,128]{2,1,0:T(8,128)(2,1)S(1)} %get-tuple-element.67), channel_id=1, source_target_pairs={{0,16},{4,20},{8,24},{12,28},{16,0},{20,4},{24,8},{28,12},{1,17},{... | collective-permute-start | bytes 196616 | tf_op jit(solution)/shard_map/ppermute | solution.py:463
  28.0 7.5 %collective-permute-start.7 = (bf16[2,128,128]{2,1,0:T(8,128)(2,1)S(1)}, bf16[2,128,128]{2,1,0:T(8,128)(2,1)S(1)}, u32[]{:S(2)}, u32[]{:S(2)}) collective-permute-start(bf16[2,128,128]{2,1,0:T(8,128)(2,1)S(1)} %get-tuple-element.68), channel_id=1, source_target_pairs={{0,12},{4,8},{8,4},{12,0},{16,28},{20,24},{24,20},{28,16},{1,13},{... | collective-permute-start | bytes 196616 | tf_op jit(solution)/shard_map/ppermute | solution.py:463
  28.1 7.4 %collective-permute-start.8 = (bf16[2,128,128]{2,1,0:T(8,128)(2,1)S(1)}, bf16[2,128,128]{2,1,0:T(8,128)(2,1)S(1)}, u32[]{:S(2)}, u32[]{:S(2)}) collective-permute-start(bf16[2,128,128]{2,1,0:T(8,128)(2,1)S(1)} %get-tuple-element.69), channel_id=1, source_target_pairs={{0,8},{4,12},{8,0},{12,4},{16,24},{20,28},{24,16},{28,20},{1,9},{5... | collective-permute-start | bytes 196616 | tf_op jit(solution)/shard_map/ppermute | solution.py:463
  41.0 6.8 %collective-permute-start.11 = (bf16[512,128]{1,0:T(8,128)(2,1)S(1)}, bf16[512,128]{1,0:T(8,128)(2,1)S(1)}, u32[]{:S(2)}, u32[]{:S(2)}) collective-permute-start(bf16[512,128]{1,0:T(8,128)(2,1)S(1)} %get-tuple-element.77.refs_0_), channel_id=1, source_target_pairs={{0,2},{1,3},{2,0},{3,1},{4,6},{5,7},{6,4},{7,5},{8,10},{9,11},{10,... | collective-permute-start | bytes 393224 | tf_op jit(solution)/shard_map/ppermute | solution.py:463
  46.2 5.0 %collective-permute-start.12 = (bf16[512,128]{1,0:T(8,128)(2,1)S(1)}, bf16[512,128]{1,0:T(8,128)(2,1)S(1)}, u32[]{:S(2)}, u32[]{:S(2)}) collective-permute-start(bf16[512,128]{1,0:T(8,128)(2,1)S(1)} %get-tuple-element.78.refs_1_), channel_id=1, source_target_pairs={{0,2},{1,3},{2,0},{3,1},{4,6},{5,7},{6,4},{7,5},{8,10},{9,11},{10,... | collective-permute-start | bytes 393224 | tf_op jit(solution)/shard_map/ppermute | solution.py:463
  68.3 8.3 %collective-permute-start.14 = (bf16[2,128,128]{2,1,0:T(8,128)(2,1)S(1)}, bf16[2,128,128]{2,1,0:T(8,128)(2,1)S(1)}, u32[]{:S(2)}, u32[]{:S(2)}) collective-permute-start(bf16[2,128,128]{2,1,0:T(8,128)(2,1)S(1)} %get-tuple-element.87), channel_id=1, source_target_pairs={{0,16},{4,20},{8,24},{12,28},{16,0},{20,4},{24,8},{28,12},{1,17},{... | collective-permute-start | bytes 196616 | tf_op jit(solution)/shard_map/ppermute | solution.py:463
  68.4 9.6 %collective-permute-start.15 = (bf16[2,128,128]{2,1,0:T(8,128)(2,1)S(1)}, bf16[2,128,128]{2,1,0:T(8,128)(2,1)S(1)}, u32[]{:S(2)}, u32[]{:S(2)}) collective-permute-start(bf16[2,128,128]{2,1,0:T(8,128)(2,1)S(1)} %get-tuple-element.88), channel_id=1, source_target_pairs={{0,20},{4,16},{8,28},{12,24},{16,4},{20,0},{24,12},{28,8},{1,21},{... | collective-permute-start | bytes 196616 | tf_op jit(solution)/shard_map/ppermute | solution.py:463
  71.2 10.4 %collective-permute-start.16 = (bf16[2,128,128]{2,1,0:T(8,128)(2,1)S(1)}, bf16[2,128,128]{2,1,0:T(8,128)(2,1)S(1)}, u32[]{:S(2)}, u32[]{:S(2)}) collective-permute-start(bf16[2,128,128]{2,1,0:T(8,128)(2,1)S(1)} %get-tuple-element.89), channel_id=1, source_target_pairs={{0,4},{4,0},{8,12},{12,8},{16,20},{20,16},{24,28},{28,24},{1,5},{5... | collective-permute-start | bytes 196616 | tf_op jit(solution)/shard_map/ppermute | solution.py:463
  72.8 8.8 %collective-permute-start.17 = (bf16[2,128,128]{2,1,0:T(8,128)(2,1)S(1)}, bf16[2,128,128]{2,1,0:T(8,128)(2,1)S(1)}, u32[]{:S(2)}, u32[]{:S(2)}) collective-permute-start(bf16[2,128,128]{2,1,0:T(8,128)(2,1)S(1)} %get-tuple-element.90), channel_id=1, source_target_pairs={{0,8},{4,12},{8,0},{12,4},{16,24},{20,28},{24,16},{28,20},{1,9},{5... | collective-permute-start | bytes 196616 | tf_op jit(solution)/shard_map/ppermute | solution.py:463
  73.6 8.0 %collective-permute-start.18 = (bf16[2,128,128]{2,1,0:T(8,128)(2,1)S(1)}, bf16[2,128,128]{2,1,0:T(8,128)(2,1)S(1)}, u32[]{:S(2)}, u32[]{:S(2)}) collective-permute-start(bf16[2,128,128]{2,1,0:T(8,128)(2,1)S(1)} %get-tuple-element.91), channel_id=1, source_target_pairs={{0,12},{4,8},{8,4},{12,0},{16,28},{20,24},{24,20},{28,16},{1,13},{... | collective-permute-start | bytes 196616 | tf_op jit(solution)/shard_map/ppermute | solution.py:463
  76.6 6.1 %collective-permute-start.19 = (bf16[2,128,128]{2,1,0:T(8,128)(2,1)S(1)}, bf16[2,128,128]{2,1,0:T(8,128)(2,1)S(1)}, u32[]{:S(2)}, u32[]{:S(2)}) collective-permute-start(bf16[2,128,128]{2,1,0:T(8,128)(2,1)S(1)} %get-tuple-element.92), channel_id=1, source_target_pairs={{0,24},{4,28},{8,16},{12,20},{16,8},{20,12},{24,0},{28,4},{1,25},{... | collective-permute-start | bytes 196616 | tf_op jit(solution)/shard_map/ppermute | solution.py:463
  78.0 7.0 %collective-permute-start.20 = (bf16[2,128,128]{2,1,0:T(8,128)(2,1)S(1)}, bf16[2,128,128]{2,1,0:T(8,128)(2,1)S(1)}, u32[]{:S(2)}, u32[]{:S(2)}) collective-permute-start(bf16[2,128,128]{2,1,0:T(8,128)(2,1)S(1)} %get-tuple-element.93), channel_id=1, source_target_pairs={{0,28},{4,24},{8,20},{12,16},{16,12},{20,8},{24,4},{28,0},{1,29},{... | collective-permute-start | bytes 196616 | tf_op jit(solution)/shard_map/ppermute | solution.py:463
  86.4 5.8 %collective-permute-start.24 = (bf16[64,256]{1,0:T(8,128)(2,1)S(1)}, bf16[64,256]{1,0:T(8,128)(2,1)S(1)}, u32[]{:S(2)}, u32[]{:S(2)}) collective-permute-start(bf16[64,256]{1,0:T(8,128)(2,1)S(1)} %get-tuple-element.110), channel_id=1, source_target_pairs={{0,24},{4,28},{8,16},{12,20},{16,8},{20,12},{24,0},{28,4},{1,25},{... | collective-permute-start | bytes 98312 | tf_op jit(solution)/shard_map/ppermute | solution.py:463
  94.7 7.2 %collective-permute-start.21 = (bf16[768,128]{1,0:T(8,128)(2,1)S(1)}, bf16[768,128]{1,0:T(8,128)(2,1)S(1)}, u32[]{:S(2)}, u32[]{:S(2)}) collective-permute-start(bf16[768,128]{1,0:T(8,128)(2,1)S(1)} %get-tuple-element.103), channel_id=1, source_target_pairs={{0,3},{1,2},{2,1},{3,0},{4,7},{5,6},{6,5},{7,4},{8,11},{9,10},{10,... | collective-permute-start | bytes 589832 | tf_op jit(solution)/shard_map/ppermute | solution.py:463
  94.7 11.4 %collective-permute-start.22 = (bf16[768,128]{1,0:T(8,128)(2,1)S(1)}, bf16[768,128]{1,0:T(8,128)(2,1)S(1)}, u32[]{:S(2)}, u32[]{:S(2)}) collective-permute-start(bf16[768,128]{1,0:T(8,128)(2,1)S(1)} %get-tuple-element.104), channel_id=1, source_target_pairs={{0,2},{1,3},{2,0},{3,1},{4,6},{5,7},{6,4},{7,5},{8,10},{9,11},{10,... | collective-permute-start | bytes 589832 | tf_op jit(solution)/shard_map/ppermute | solution.py:463
  96.1 9.9 %collective-permute-start.23 = (bf16[768,128]{1,0:T(8,128)(2,1)S(1)}, bf16[768,128]{1,0:T(8,128)(2,1)S(1)}, u32[]{:S(2)}, u32[]{:S(2)}) collective-permute-start(bf16[768,128]{1,0:T(8,128)(2,1)S(1)} %get-tuple-element.105), channel_id=1, source_target_pairs={{0,1},{1,0},{2,3},{3,2},{4,5},{5,4},{6,7},{7,6},{8,9},{9,8},{10,11... | collective-permute-start | bytes 589832 | tf_op jit(solution)/shard_map/ppermute | solution.py:463
  98.1 9.3 %collective-permute-start.30 = (bf16[64,256]{1,0:T(8,128)(2,1)S(1)}, bf16[64,256]{1,0:T(8,128)(2,1)S(1)}, u32[]{:S(2)}, u32[]{:S(2)}) collective-permute-start(bf16[64,256]{1,0:T(8,128)(2,1)S(1)} %add_convert_fusion.l0), channel_id=1, source_target_pairs={{0,24},{4,28},{8,16},{12,20},{16,8},{20,12},{24,0},{28,4},{1,25},{... | collective-permute-start | bytes 98312 | tf_op jit(solution)/shard_map/ppermute | solution.py:463
  100.0 7.4 %collective-permute-start.29 = (bf16[64,256]{1,0:T(8,128)(2,1)S(1)}, bf16[64,256]{1,0:T(8,128)(2,1)S(1)}, u32[]{:S(2)}, u32[]{:S(2)}) collective-permute-start(bf16[64,256]{1,0:T(8,128)(2,1)S(1)} %add_convert_fusion.l0), channel_id=1, source_target_pairs={{0,16},{4,20},{8,24},{12,28},{16,0},{20,4},{24,8},{28,12},{1,17},{... | collective-permute-start | bytes 98312 | tf_op jit(solution)/shard_map/ppermute | solution.py:463
  101.9 5.5 %collective-permute-start.28 = (bf16[64,256]{1,0:T(8,128)(2,1)S(1)}, bf16[64,256]{1,0:T(8,128)(2,1)S(1)}, u32[]{:S(2)}, u32[]{:S(2)}) collective-permute-start(bf16[64,256]{1,0:T(8,128)(2,1)S(1)} %add_convert_fusion.l0), channel_id=1, source_target_pairs={{0,8},{4,12},{8,0},{12,4},{16,24},{20,28},{24,16},{28,20},{1,9},{5... | collective-permute-start | bytes 98312 | tf_op jit(solution)/shard_map/ppermute | solution.py:463
  (14 other events, 52.2 us)

commit v4 on v1

--- a/solution.py
+++ b/solution.py
@@ -127,13 +127,14 @@
     return (pair_ref.at[:rows], other_ref.at[:rows], pair_ref.at[rows:], other_ref.at[rows:])
 
 
-def issue_order(count):
-    return [0] + list(range(count - 1, 0, -1))
-
-
-def by_mask(refs):
-    order = issue_order(len(refs))
-    return [refs[order.index(m)] for m in range(len(refs))]
+def step_masks(count):
+    near, far = list(range(count // 2 - 1, 0, -1)), list(range(count - 1, count // 2 - 1, -1))
+    return [0] + far + near, [0] + near + far
+
+
+def mask_at(step, head, count):
+    even, odd = step_masks(count)
+    return jnp.where((head & 1) == 1, odd[step], even[step])
 
 
 def project_kernel(count, place_ref, wanted_ref, pair_ref, other_ref, in_from, *refs):
@@ -159,10 +160,11 @@
         y = dot(x_refs[part][...], wide_ref[...]).astype(BF16)
         qz_ref[at, :] = y[:, :BLOCK]
         kv_ref[at, :] = y[:, BLOCK:]
-    for m in range(count):
+    for step in range(count):
+        other = node ^ mask_at(step, head, count)
         for c in range(CAP):
-            block = wanted_ref[node ^ m, 0, c]
-            out_refs[m][c] = kv_ref[span(block * BLOCK, BLOCK), :]
+            block = wanted_ref[other, 0, c]
+            out_refs[step][c] = kv_ref[span(block * BLOCK, BLOCK), :]
 
 
 def prepare_kernel(place_ref, slot_ref, count_ref, pair_ref, other_ref, kv_ref, after_ref, xt_ref, kvt_ref):
@@ -174,22 +176,24 @@
         kvt_ref[i] = kv_ref[i * BLOCK : (i + 1) * BLOCK, :].T
 
 
-def table_kernel_part(node, kv_ref, kvt_ref, in_refs, table_ref, tablet_ref):
+def fill_table(place_ref, kv_ref, kvt_ref, in_refs, table_ref, tablet_ref):
+    head, node = place_ref[0], place_ref[1]
     for i in range(BLK):
         table_ref[i] = kv_ref[i * BLOCK : (i + 1) * BLOCK, :]
         tablet_ref[i] = kvt_ref[i]
-    for m, in_ref in enumerate(in_refs):
+    for step, in_ref in enumerate(in_refs):
+        other = node ^ mask_at(step, head, len(in_refs))
         for c in range(CAP):
             block = in_ref[c]
-            at = BLK + (node ^ m) * CAP + c
+            at = BLK + other * CAP + c
             table_ref[at] = block
             tablet_ref[at] = block.T
 
 
 def early_forward_kernel(count, place_ref, slot_ref, count_ref, qz_ref, kv_ref, kvt_ref, *refs):
-    in_refs, refs = by_mask(refs[:count]), refs[count:]
+    in_refs, refs = refs[:count], refs[count:]
     att_ref, attt_ref, table_ref, tablet_ref, top_ref, inv_ref, even_ref, odd_ref = refs
-    table_kernel_part(place_ref[1], kv_ref, kvt_ref, in_refs, table_ref, tablet_ref)
+    fill_table(place_ref, kv_ref, kvt_ref, in_refs, table_ref, tablet_ref)
     attend_blocks(
         0, slot_ref, count_ref, qz_ref, table_ref, tablet_ref,
         att_ref, attt_ref, top_ref, inv_ref, even_ref, odd_ref,
@@ -372,9 +376,10 @@
     lane = lax.broadcasted_iota(jnp.int32, (1, BLOCK), 1)
     unscale = jnp.where(lane < HD, 1.0, 1.0 / SCALE)
     own_ref[...] = acc_ref[:BLK] * unscale
-    for m in range(count):
+    for step in range(count):
+        other = node ^ mask_at(step, head, count)
         for c in range(CAP):
-            leave_refs[m][c] = (acc_ref[BLK + (node ^ m) * CAP + c] * unscale).astype(BF16)
+            leave_refs[step][c] = (acc_ref[BLK + other * CAP + c] * unscale).astype(BF16)
     for part in range(4):
         size = dq_refs[part].shape[0]
         dq_refs[part][...] = dq_ref[span((head ^ part) * size, size), :]
@@ -401,16 +406,17 @@
 
 
 def collect_kernel(count, place_ref, wanted_ref, own_ref, *refs):
-    back_refs, dq_refs, refs = by_mask(refs[:count]), refs[count : count + 4], refs[count + 4 :]
+    back_refs, dq_refs, refs = refs[:count], refs[count : count + 4], refs[count + 4 :]
     xt_ref, owg_ref, qwg_ref, refs = *refs[:3], refs[3:]
     own_send, beside_send, across_send, piece_refs, sum_ref = *refs[:3], refs[3:7], refs[7]
     size = own_send.shape[0]
     send_refs = (own_send, beside_send, across_send.at[:size], across_send.at[size:])
     head, node = place_ref[0], place_ref[1]
     sum_ref[...] = own_ref[...]
-    for m in range(count):
+    for step in range(count):
+        other = node ^ mask_at(step, head, count)
         for c in range(CAP):
-            sum_ref[wanted_ref[node ^ m, 0, c]] += back_refs[m][c].astype(F32)
+            sum_ref[wanted_ref[other, 0, c]] += back_refs[step][c].astype(F32)
     for part in range(4):
         rows = 2 * dq_refs[part].shape[0]
         first = (head ^ part) * (rows // BLOCK)
@@ -514,7 +520,18 @@
         total = total.astype(pieces[0].dtype)
         return exchange([total] * 4, "node", 1 << shift), total
 
-    order = issue_order(node_count)
+    def exchange_nodes(pieces):
+        moved = list(pieces)
+        even, odd = step_masks(node_count)
+        for step in range(1, node_count):
+            perm = [
+                (n * head_count + h, (n ^ (odd if h & 1 else even)[step]) * head_count + h)
+                for n in range(node_count)
+                for h in range(head_count)
+            ]
+            moved[step] = lax.ppermute(pieces[step], ("node", "head"), perm)
+        return moved
+
     across = swap(features, "head", 2)
     c_across = swap(cotangent, "head", 2)
     wants = lax.all_to_all(
@@ -534,7 +551,7 @@
             pltpu.SemaphoreType.DMA,
         ],
     )(place, wants, *xs, in_weight)
-    incoming = exchange(outgoing, "node")
+    incoming = exchange_nodes(outgoing)
     xt, kvt = call(
         prepare_kernel,
         "prepare",
@@ -560,7 +577,7 @@
         limit,
         flops=2 * node_rows * PER * BLOCK * BLOCK,
         scratch=[pltpu.VMEM((PER * BLOCK, BLOCK), F32)] * 2,
-    )(place, key_slots, block_count, qz, kv, kvt, *[incoming[m] for m in order])
+    )(place, key_slots, block_count, qz, kv, kvt, *incoming)
     early_across = swap(early_att, "head", 2)
     late_att, attt, top, inv = call(
         late_forward_kernel,
@@ -616,7 +633,7 @@
             pltpu.VMEM((PER * BLOCK, 2 * BLOCK), F32),
         ],
     )(place, key_slots, block_count, qz, gz, table, tablet, top, inv, dots)
-    returned = exchange(rest[4:], "node")
+    returned = exchange_nodes(rest[4:])
     query_wg, wkv, wq = call(
         query_weight_kernel,
         "query_weight",
@@ -635,7 +652,7 @@
         limit,
         flops=2 * node_rows * D * BLOCK,
         scratch=[pltpu.VMEM((BLK, BLOCK, BLOCK), F32)],
-    )(place, wants, own, *[returned[m] for m in order], *rest[:4], xt, owg, query_wg)
+    )(place, wants, own, *returned, *rest[:4], xt, owg, query_wg)
     own_send, beside_send, across_send = collected[:3]
     across = swap(across_send, "head", 2)
     shift = top_shift(node_count)

time: 108 us -> 107 us (level)
  starting transfers between devices: 43 us -> 39.4 us
  waiting for transfers between devices: 18.4 us -> 21.3 us
    ppermute x30 -> x16, starting transfers between devices: 43 us -> 17 us  [swap(): return lax.ppermute(value, axis, [(i, i ^ mask) for i in range(size)])]
    ppermute x0 -> x14, starting transfers between devices: none -> 22.4 us  [exchange_nodes(): moved[step] = lax.ppermute(pieces[step], ('node', 'head'), perm)]
    ppermute x0 -> x14, waiting for transfers between devices: none -> 7.07 us  [exchange_nodes(): moved[step] = lax.ppermute(pieces[step], ('node', 'head'), perm)]
    ppermute x30 -> x16, waiting for transfers between devices: 18.4 us -> 14.3 us  [swap(): return lax.ppermute(value, axis, [(i, i ^ mask) for i in range(size)])]
  transfers between devices with their start and end apart: 30 -> 30, of which waited for: 17 -> 15; matrix products, arithmetic and copies ran while one was open for 0% -> 0% of each run, Pallas kernels for 9% -> 9%
where the time goes in v4:
time: 107 us
  starting transfers between devices  39.4 us (37%)
  Pallas kernels  31.8 us (30%)
  waiting for transfers between devices  21.3 us (20%)
  blocking collectives  12.1 us (11%)
  local copies, waits for them, and re-layouts  1.12 us (1%)
    ppermute x14, starting transfers between devices, exchange_nodes(): moved[step] = lax.ppermute(pieces[step], ('node', 'head'), perm)  22.4 us
    ppermute x16, starting transfers between devices, swap(): return lax.ppermute(value, axis, [(i, i ^ mask) for i in range(size)])  17 us
    ppermute x16, waiting for transfers between devices, swap(): return lax.ppermute(value, axis, [(i, i ^ mask) for i in range(size)])  14.3 us
    all_to_all x1, blocking collectives, on_device(): lax.all_to_all(wanted.reshape(node_count, 1, CAP), 'node', split_axis=0,...  12.1 us
    pallas_call x1, Pallas kernels, on_device(): call(functools.partial(backward_kernel, node_count), 'backward', [((BLK,...  11 us
    ppermute x14, waiting for transfers between devices, exchange_nodes(): moved[step] = lax.ppermute(pieces[step], ('node', 'head'), perm)  7.07 us
    pallas_call x1, Pallas kernels, on_device(): call(functools.partial(early_forward_kernel, node_count), 'early_forward'...  4.66 us
    pallas_call x1, Pallas kernels, on_device(): call(late_forward_kernel, 'late_forward', [half_att, ((HD, node_rows), BF...  4.49 us
  transfers between devices with their start and end apart: 30, of which 15 were waited for; matrix products, arithmetic and copies ran while one was open for 0% of the time, Pallas kernels for 9%

profile of v4, /device:TPU:0, one launch (start us, length us, event | category | flops | bytes accessed | tf_op | source)
XLA Modules:
  0.0 106.7 jit_solution(5388495793498084898)
XLA Ops:
  0.6 3.0 %collective-permute-start = (bf16[512,256]{1,0:T(8,128)(2,1)}, bf16[512,256]{1,0:T(8,128)(2,1)S(1)}, u32[]{:S(2)}, u32[]{:S(2)}) collective-permute-start(bf16[512,256]{1,0:T(8,128)(2,1)} %refs_0_.2), channel_id=1, source_target_pairs={{0,2},{1,3},{2,0},{3,1},{4,6},{5,7},{6,4},{7,5},{8,10},{9,11},{10,... | collective-permute-start | bytes 786440 | tf_op jit(solution)/shard_map/ppermute | solution.py:474
  3.7 12.1 %all_to_all.5.refs_2_.wanted_ref = s32[8,1,2]{2,1,0:T(1,128)S(1)} all-to-all(s32[8,1,2]{2,1,0:T(1,128)S(1)} %copy.11), channel_id=1, replica_groups=mesh['node'=8,'head'=4] {'node'}, dimensions={0} | all-to-all | bytes 128 | tf_op jit(solution)/shard_map/all_to_all | solution.py:537
  20.9 3.2 %collective-permute-start.4 = (bf16[2,128,128]{2,1,0:T(8,128)(2,1)S(1)}, bf16[2,128,128]{2,1,0:T(8,128)(2,1)S(1)}, u32[]{:S(2)}, u32[]{:S(2)}) collective-permute-start(bf16[2,128,128]{2,1,0:T(8,128)(2,1)S(1)} %get-tuple-element.64), channel_id=1, source_target_pairs={{0,24},{1,9},{2,26},{3,11},{4,28},{5,13},{6,30},{7,15},{8,16},{9,1... | collective-permute-start | bytes 196616 | tf_op jit(solution)/shard_map/ppermute | solution.py:532
  24.2 3.8 %collective-permute-start.6 = (bf16[2,128,128]{2,1,0:T(8,128)(2,1)S(1)}, bf16[2,128,128]{2,1,0:T(8,128)(2,1)S(1)}, u32[]{:S(2)}, u32[]{:S(2)}) collective-permute-start(bf16[2,128,128]{2,1,0:T(8,128)(2,1)S(1)} %get-tuple-element.66), channel_id=1, source_target_pairs={{0,16},{1,29},{2,18},{3,31},{4,20},{5,25},{6,22},{7,27},{8,24},{9,... | collective-permute-start | bytes 196616 | tf_op jit(solution)/shard_map/ppermute | solution.py:532
  28.0 2.0 %collective-permute-start.8 = (bf16[2,128,128]{2,1,0:T(8,128)(2,1)S(1)}, bf16[2,128,128]{2,1,0:T(8,128)(2,1)S(1)}, u32[]{:S(2)}, u32[]{:S(2)}) collective-permute-start(bf16[2,128,128]{2,1,0:T(8,128)(2,1)S(1)} %get-tuple-element.68), channel_id=1, source_target_pairs={{0,8},{1,21},{2,10},{3,23},{4,12},{5,17},{6,14},{7,19},{8,0},{9,29... | collective-permute-start | bytes 196616 | tf_op jit(solution)/shard_map/ppermute | solution.py:532
  30.0 1.5 %collective-permute-start.9 = (bf16[2,128,128]{2,1,0:T(8,128)(2,1)S(1)}, bf16[2,128,128]{2,1,0:T(8,128)(2,1)S(1)}, u32[]{:S(2)}, u32[]{:S(2)}) collective-permute-start(bf16[2,128,128]{2,1,0:T(8,128)(2,1)S(1)} %get-tuple-element.69), channel_id=1, source_target_pairs={{0,4},{1,17},{2,6},{3,19},{4,0},{5,21},{6,2},{7,23},{8,12},{9,25},... | collective-permute-start | bytes 196616 | tf_op jit(solution)/shard_map/ppermute | solution.py:532
  33.1 2.3 %collective-permute-done.6.refs_4_ = bf16[2,128,128]{2,1,0:T(8,128)(2,1)S(1)} collective-permute-done((bf16[2,128,128]{2,1,0:T(8,128)(2,1)S(1)}, bf16[2,128,128]{2,1,0:T(8,128)(2,1)S(1)}, u32[]{:S(2)}, u32[]{:S(2)}) %collective-permute-start.6) | collective-permute-done | bytes 65568 | tf_op jit(solution)/shard_map/ppermute | solution.py:532
  35.7 4.7 %early_forward.1 = (bf16[512,128]{1,0:T(8,128)(2,1)S(1)}, bf16[64,1024]{1,0:T(8,128)(2,1)S(1)}, bf16[32,128,128]{2,1,0:T(8,128)(2,1)S(1)}, bf16[32,128,128]{2,1,...) custom-call(s32[2]{0:T(128)S(1)} %pad_add_fusion.place_ref, s32[16,12]{1,0:T(8,128)S(1)} %copy-done.3, ...), custom_call_target="tpu_custom_call" | custom-call | flops 805306368 | bytes 4194304 | tf_op jit(solution)/shard_map/early_forward/pallas_call | solution.py:565
  41.0 4.5 %late_forward.1 = (bf16[512,128]{1,0:T(8,128)(2,1)S(1)}, bf16[64,2048]{1,0:T(8,128)(2,1)S(1)}, f32[16,8,128]{2,1,0:T(8,128)S(1)}, f32[16,8,128]{2,1,0:T(8,128)S(1)}) custom-call(s32[16,12]{1,0:T(8,128)S(1)} %copy-done.3, s32[16]{0:T(128)S(1)} %copy-done.4, bf16[2048,128]{1,0:T(8,128)(2,1)S(1)} %get-tuple-element.59.qz_ref, ...), custom_call_target="tpu_custom_call" | custom-call | flops 805306368 | bytes 4194304 | tf_op jit(solution)/shard_map/late_forward/pallas_call | solution.py:582
  45.5 1.5 %collective-permute-start.12 = (bf16[512,128]{1,0:T(8,128)(2,1)S(1)}, bf16[512,128]{1,0:T(8,128)(2,1)S(1)}, u32[]{:S(2)}, u32[]{:S(2)}) collective-permute-start(bf16[512,128]{1,0:T(8,128)(2,1)S(1)} %get-tuple-element.77.refs_1_), channel_id=1, source_target_pairs={{0,2},{1,3},{2,0},{3,1},{4,6},{5,7},{6,4},{7,5},{8,10},{9,11},{10,... | collective-permute-start | bytes 393224 | tf_op jit(solution)/shard_map/ppermute | solution.py:474
  47.1 3.5 %collective-permute-done.12.refs_3_ = bf16[512,128]{1,0:T(8,128)(2,1)S(1)} collective-permute-done((bf16[512,128]{1,0:T(8,128)(2,1)S(1)}, bf16[512,128]{1,0:T(8,128)(2,1)S(1)}, u32[]{:S(2)}, u32[]{:S(2)}) %collective-permute-start.12) | collective-permute-done | bytes 131104 | tf_op jit(solution)/shard_map/ppermute | solution.py:474
  50.7 1.9 %collective-permute-done.13.a_other = bf16[2048,128]{1,0:T(8,128)(2,1)S(1)} collective-permute-done((bf16[2048,128]{1,0:T(8,128)(2,1)S(1)}, bf16[2048,128]{1,0:T(8,128)(2,1)S(1)}, u32[]{:S(2)}, u32[]{:S(2)}) %collective-permute-start.13) | collective-permute-done | bytes 524320 | tf_op jit(solution)/shard_map/ppermute | solution.py:474
  52.6 4.1 %middle.1 = (bf16[512,256]{1,0:T(8,128)(2,1)}, f32[512,256]{1,0:T(8,128)S(1)}, bf16[2048,128]{1,0:T(8,128)(2,1)S(1)}, f32[16,8,128]{2,1,0:T(8,128)S(1)}, f32[64,256]{1,0:T(8,128)S(1)}) custom-call(s32[2]{0:T(128)S(1)} %pad_add_fusion.place_ref, bf16[1024,256]{1,0:T(8,128)(2,1)S(1)} %pair.3.pair_ref.x_pair, ...), custom_call_target="tpu_custom_call" | custom-call | flops 1073741824 | bytes 4194304 | tf_op jit(solution)/shard_map/middle/pallas_call | solution.py:599
  56.7 11.0 %backward.1 = (f32[16,128,128]{2,1,0:T(8,128)S(1)}, bf16[64,2048]{1,0:T(8,128)(2,1)S(1)}, bf16[256,128]{1,0:T(8,128)(2,1)S(1)}, bf16[256,128]{1,0:T(8,128)(2,1)S...) custom-call(s32[2]{0:T(128)S(1)} %pad_add_fusion.place_ref, ...), custom_call_target="tpu_custom_call" | custom-call | flops 4026531840 | bytes 4194304 | tf_op jit(solution)/shard_map/backward/pallas_call | solution.py:620
  67.7 2.2 %collective-permute-start.14 = (bf16[2,128,128]{2,1,0:T(8,128)(2,1)S(1)}, bf16[2,128,128]{2,1,0:T(8,128)(2,1)S(1)}, u32[]{:S(2)}, u32[]{:S(2)}) collective-permute-start(bf16[2,128,128]{2,1,0:T(8,128)(2,1)S(1)} %get-tuple-element.86), channel_id=1, source_target_pairs={{0,28},{1,13},{2,30},{3,15},{4,24},{5,9},{6,26},{7,11},{8,20},{9,5... | collective-permute-start | bytes 196616 | tf_op jit(solution)/shard_map/ppermute | solution.py:532
  69.8 2.4 %collective-permute-start.15 = (bf16[2,128,128]{2,1,0:T(8,128)(2,1)S(1)}, bf16[2,128,128]{2,1,0:T(8,128)(2,1)S(1)}, u32[]{:S(2)}, u32[]{:S(2)}) collective-permute-start(bf16[2,128,128]{2,1,0:T(8,128)(2,1)S(1)} %get-tuple-element.87), channel_id=1, source_target_pairs={{0,24},{1,9},{2,26},{3,11},{4,28},{5,13},{6,30},{7,15},{8,16},{9,1... | collective-permute-start | bytes 196616 | tf_op jit(solution)/shard_map/ppermute | solution.py:532
  72.3 3.1 %collective-permute-start.17 = (bf16[2,128,128]{2,1,0:T(8,128)(2,1)S(1)}, bf16[2,128,128]{2,1,0:T(8,128)(2,1)S(1)}, u32[]{:S(2)}, u32[]{:S(2)}) collective-permute-start(bf16[2,128,128]{2,1,0:T(8,128)(2,1)S(1)} %get-tuple-element.89), channel_id=1, source_target_pairs={{0,16},{1,29},{2,18},{3,31},{4,20},{5,25},{6,22},{7,27},{8,24},{9,... | collective-permute-start | bytes 196616 | tf_op jit(solution)/shard_map/ppermute | solution.py:532
  75.4 2.7 %collective-permute-start.19 = (bf16[2,128,128]{2,1,0:T(8,128)(2,1)S(1)}, bf16[2,128,128]{2,1,0:T(8,128)(2,1)S(1)}, u32[]{:S(2)}, u32[]{:S(2)}) collective-permute-start(bf16[2,128,128]{2,1,0:T(8,128)(2,1)S(1)} %get-tuple-element.91), channel_id=1, source_target_pairs={{0,8},{1,21},{2,10},{3,23},{4,12},{5,17},{6,14},{7,19},{8,0},{9,29... | collective-permute-start | bytes 196616 | tf_op jit(solution)/shard_map/ppermute | solution.py:532
  79.8 2.1 %collective-permute-done.16.refs_3_ = bf16[2,128,128]{2,1,0:T(8,128)(2,1)S(1)} collective-permute-done((bf16[2,128,128]{2,1,0:T(8,128)(2,1)S(1)}, bf16[2,128,128]{2,1,0:T(8,128)(2,1)S(1)}, u32[]{:S(2)}, u32[]{:S(2)}) %collective-permute-start.16) | collective-permute-done | bytes 65568 | tf_op jit(solution)/shard_map/ppermute | solution.py:532
  83.9 1.4 %collect.1 = (bf16[768,128]{1,0:T(8,128)(2,1)S(1)}, bf16[768,128]{1,0:T(8,128)(2,1)S(1)}, bf16[1536,128]{1,0:T(8,128)(2,1)S(1)}, bf16[64,256]{1,0:T(8,128)(2,1)S...) custom-call(s32[2]{0:T(128)S(1)} %pad_add_fusion.place_ref, ...), custom_call_target="tpu_custom_call" | custom-call | flops 134217728 | bytes 4194304 | tf_op jit(solution)/shard_map/collect/pallas_call | solution.py:647
  85.3 1.5 %collective-permute-start.21 = (bf16[1536,128]{1,0:T(8,128)(2,1)S(1)}, bf16[1536,128]{1,0:T(8,128)(2,1)S(1)}, u32[]{:S(2)}, u32[]{:S(2)}) collective-permute-start(bf16[1536,128]{1,0:T(8,128)(2,1)S(1)} %get-tuple-element.103), channel_id=1, source_target_pairs={{0,2},{1,3},{2,0},{3,1},{4,6},{5,7},{6,4},{7,5},{8,10},{9,11},{10,... | collective-permute-start | bytes 1179656 | tf_op jit(solution)/shard_map/ppermute | solution.py:474
  88.0 3.2 %collective-permute-start.24 = (bf16[64,256]{1,0:T(8,128)(2,1)S(1)}, bf16[64,256]{1,0:T(8,128)(2,1)S(1)}, u32[]{:S(2)}, u32[]{:S(2)}) collective-permute-start(bf16[64,256]{1,0:T(8,128)(2,1)S(1)} %get-tuple-element.107), channel_id=1, source_target_pairs={{0,8},{4,12},{8,0},{12,4},{16,24},{20,28},{24,16},{28,20},{1,9},{5... | collective-permute-start | bytes 98312 | tf_op jit(solution)/shard_map/ppermute | solution.py:474
  94.0 3.7 %collective-permute-done.25 = f32[64,256]{1,0:T(8,128)S(1)} collective-permute-done((f32[64,256]{1,0:T(8,128)S(1)}, f32[64,256]{1,0:T(8,128)S(1)}, u32[]{:S(2)}, u32[]{:S(2)}) %collective-permute-start.25) | collective-permute-done | bytes 65568 | tf_op jit(solution)/shard_map/ppermute | solution.py:474
  97.9 2.1 %collective-permute-start.29 = (bf16[64,256]{1,0:T(8,128)(2,1)S(1)}, bf16[64,256]{1,0:T(8,128)(2,1)S(1)}, u32[]{:S(2)}, u32[]{:S(2)}) collective-permute-start(bf16[64,256]{1,0:T(8,128)(2,1)S(1)} %add_convert_fusion.after_ref.l0), channel_id=1, source_target_pairs={{0,24},{4,28},{8,16},{12,20},{16,8},{20,12},{24,0},{28,4},{1,25},{... | collective-permute-start | bytes 98312 | tf_op jit(solution)/shard_map/ppermute | solution.py:474
  (69 shorter events, 22.5 us)
Async XLA Ops:
  0.6 15.2 %collective-permute-start = (bf16[512,256]{1,0:T(8,128)(2,1)}, bf16[512,256]{1,0:T(8,128)(2,1)S(1)}, u32[]{:S(2)}, u32[]{:S(2)}) collective-permute-start(bf16[512,256]{1,0:T(8,128)(2,1)} %refs_0_.2), channel_id=1, source_target_pairs={{0,2},{1,3},{2,0},{3,1},{4,6},{5,7},{6,4},{7,5},{8,10},{9,11},{10,... | collective-permute-start | bytes 786440 | tf_op jit(solution)/shard_map/ppermute | solution.py:474
  17.0 11.0 %collective-permute-start.2 = (bf16[512,256]{1,0:T(8,128)(2,1)S(1)}, bf16[512,256]{1,0:T(8,128)(2,1)S(1)}, u32[]{:S(2)}, u32[]{:S(2)}) collective-permute-start(bf16[512,256]{1,0:T(8,128)(2,1)S(1)} %copy-done.1), channel_id=1, source_target_pairs={{0,2},{1,3},{2,0},{3,1},{4,6},{5,7},{6,4},{7,5},{8,10},{9,11},{10,... | collective-permute-start | bytes 786440 | tf_op jit(solution)/shard_map/ppermute | solution.py:474
  20.3 7.7 %collective-permute-start.3 = (bf16[2,128,128]{2,1,0:T(8,128)(2,1)S(1)}, bf16[2,128,128]{2,1,0:T(8,128)(2,1)S(1)}, u32[]{:S(2)}, u32[]{:S(2)}) collective-permute-start(bf16[2,128,128]{2,1,0:T(8,128)(2,1)S(1)} %get-tuple-element.63), channel_id=1, source_target_pairs={{0,28},{1,13},{2,30},{3,15},{4,24},{5,9},{6,26},{7,11},{8,20},{9,5... | collective-permute-start | bytes 196616 | tf_op jit(solution)/shard_map/ppermute | solution.py:532
  20.9 9.1 %collective-permute-start.4 = (bf16[2,128,128]{2,1,0:T(8,128)(2,1)S(1)}, bf16[2,128,128]{2,1,0:T(8,128)(2,1)S(1)}, u32[]{:S(2)}, u32[]{:S(2)}) collective-permute-start(bf16[2,128,128]{2,1,0:T(8,128)(2,1)S(1)} %get-tuple-element.64), channel_id=1, source_target_pairs={{0,24},{1,9},{2,26},{3,11},{4,28},{5,13},{6,30},{7,15},{8,16},{9,1... | collective-permute-start | bytes 196616 | tf_op jit(solution)/shard_map/ppermute | solution.py:532
  24.2 8.9 %collective-permute-start.5 = (bf16[2,128,128]{2,1,0:T(8,128)(2,1)S(1)}, bf16[2,128,128]{2,1,0:T(8,128)(2,1)S(1)}, u32[]{:S(2)}, u32[]{:S(2)}) collective-permute-start(bf16[2,128,128]{2,1,0:T(8,128)(2,1)S(1)} %get-tuple-element.65), channel_id=1, source_target_pairs={{0,20},{1,5},{2,22},{3,7},{4,16},{5,1},{6,18},{7,3},{8,28},{9,13},... | collective-permute-start | bytes 196616 | tf_op jit(solution)/shard_map/ppermute | solution.py:532
  24.2 11.1 %collective-permute-start.6 = (bf16[2,128,128]{2,1,0:T(8,128)(2,1)S(1)}, bf16[2,128,128]{2,1,0:T(8,128)(2,1)S(1)}, u32[]{:S(2)}, u32[]{:S(2)}) collective-permute-start(bf16[2,128,128]{2,1,0:T(8,128)(2,1)S(1)} %get-tuple-element.66), channel_id=1, source_target_pairs={{0,16},{1,29},{2,18},{3,31},{4,20},{5,25},{6,22},{7,27},{8,24},{9,... | collective-permute-start | bytes 196616 | tf_op jit(solution)/shard_map/ppermute | solution.py:532
  28.0 7.3 %collective-permute-start.7 = (bf16[2,128,128]{2,1,0:T(8,128)(2,1)S(1)}, bf16[2,128,128]{2,1,0:T(8,128)(2,1)S(1)}, u32[]{:S(2)}, u32[]{:S(2)}) collective-permute-start(bf16[2,128,128]{2,1,0:T(8,128)(2,1)S(1)} %get-tuple-element.67), channel_id=1, source_target_pairs={{0,12},{1,25},{2,14},{3,27},{4,8},{5,29},{6,10},{7,31},{8,4},{9,17... | collective-permute-start | bytes 196616 | tf_op jit(solution)/shard_map/ppermute | solution.py:532
  28.0 7.7 %collective-permute-start.8 = (bf16[2,128,128]{2,1,0:T(8,128)(2,1)S(1)}, bf16[2,128,128]{2,1,0:T(8,128)(2,1)S(1)}, u32[]{:S(2)}, u32[]{:S(2)}) collective-permute-start(bf16[2,128,128]{2,1,0:T(8,128)(2,1)S(1)} %get-tuple-element.68), channel_id=1, source_target_pairs={{0,8},{1,21},{2,10},{3,23},{4,12},{5,17},{6,14},{7,19},{8,0},{9,29... | collective-permute-start | bytes 196616 | tf_op jit(solution)/shard_map/ppermute | solution.py:532
  30.0 5.6 %collective-permute-start.9 = (bf16[2,128,128]{2,1,0:T(8,128)(2,1)S(1)}, bf16[2,128,128]{2,1,0:T(8,128)(2,1)S(1)}, u32[]{:S(2)}, u32[]{:S(2)}) collective-permute-start(bf16[2,128,128]{2,1,0:T(8,128)(2,1)S(1)} %get-tuple-element.69), channel_id=1, source_target_pairs={{0,4},{1,17},{2,6},{3,19},{4,0},{5,21},{6,2},{7,23},{8,12},{9,25},... | collective-permute-start | bytes 196616 | tf_op jit(solution)/shard_map/ppermute | solution.py:532
  40.3 6.8 %collective-permute-start.11 = (bf16[512,128]{1,0:T(8,128)(2,1)S(1)}, bf16[512,128]{1,0:T(8,128)(2,1)S(1)}, u32[]{:S(2)}, u32[]{:S(2)}) collective-permute-start(bf16[512,128]{1,0:T(8,128)(2,1)S(1)} %get-tuple-element.76.refs_0_), channel_id=1, source_target_pairs={{0,2},{1,3},{2,0},{3,1},{4,6},{5,7},{6,4},{7,5},{8,10},{9,11},{10,... | collective-permute-start | bytes 393224 | tf_op jit(solution)/shard_map/ppermute | solution.py:474
  45.5 5.1 %collective-permute-start.12 = (bf16[512,128]{1,0:T(8,128)(2,1)S(1)}, bf16[512,128]{1,0:T(8,128)(2,1)S(1)}, u32[]{:S(2)}, u32[]{:S(2)}) collective-permute-start(bf16[512,128]{1,0:T(8,128)(2,1)S(1)} %get-tuple-element.77.refs_1_), channel_id=1, source_target_pairs={{0,2},{1,3},{2,0},{3,1},{4,6},{5,7},{6,4},{7,5},{8,10},{9,11},{10,... | collective-permute-start | bytes 393224 | tf_op jit(solution)/shard_map/ppermute | solution.py:474
  67.7 7.7 %collective-permute-start.14 = (bf16[2,128,128]{2,1,0:T(8,128)(2,1)S(1)}, bf16[2,128,128]{2,1,0:T(8,128)(2,1)S(1)}, u32[]{:S(2)}, u32[]{:S(2)}) collective-permute-start(bf16[2,128,128]{2,1,0:T(8,128)(2,1)S(1)} %get-tuple-element.86), channel_id=1, source_target_pairs={{0,28},{1,13},{2,30},{3,15},{4,24},{5,9},{6,26},{7,11},{8,20},{9,5... | collective-permute-start | bytes 196616 | tf_op jit(solution)/shard_map/ppermute | solution.py:532
  69.8 8.3 %collective-permute-start.15 = (bf16[2,128,128]{2,1,0:T(8,128)(2,1)S(1)}, bf16[2,128,128]{2,1,0:T(8,128)(2,1)S(1)}, u32[]{:S(2)}, u32[]{:S(2)}) collective-permute-start(bf16[2,128,128]{2,1,0:T(8,128)(2,1)S(1)} %get-tuple-element.87), channel_id=1, source_target_pairs={{0,24},{1,9},{2,26},{3,11},{4,28},{5,13},{6,30},{7,15},{8,16},{9,1... | collective-permute-start | bytes 196616 | tf_op jit(solution)/shard_map/ppermute | solution.py:532
  72.3 9.7 %collective-permute-start.16 = (bf16[2,128,128]{2,1,0:T(8,128)(2,1)S(1)}, bf16[2,128,128]{2,1,0:T(8,128)(2,1)S(1)}, u32[]{:S(2)}, u32[]{:S(2)}) collective-permute-start(bf16[2,128,128]{2,1,0:T(8,128)(2,1)S(1)} %get-tuple-element.88), channel_id=1, source_target_pairs={{0,20},{1,5},{2,22},{3,7},{4,16},{5,1},{6,18},{7,3},{8,28},{9,13},... | collective-permute-start | bytes 196616 | tf_op jit(solution)/shard_map/ppermute | solution.py:532
  72.3 10.9 %collective-permute-start.17 = (bf16[2,128,128]{2,1,0:T(8,128)(2,1)S(1)}, bf16[2,128,128]{2,1,0:T(8,128)(2,1)S(1)}, u32[]{:S(2)}, u32[]{:S(2)}) collective-permute-start(bf16[2,128,128]{2,1,0:T(8,128)(2,1)S(1)} %get-tuple-element.89), channel_id=1, source_target_pairs={{0,16},{1,29},{2,18},{3,31},{4,20},{5,25},{6,22},{7,27},{8,24},{9,... | collective-permute-start | bytes 196616 | tf_op jit(solution)/shard_map/ppermute | solution.py:532
  75.4 7.8 %collective-permute-start.18 = (bf16[2,128,128]{2,1,0:T(8,128)(2,1)S(1)}, bf16[2,128,128]{2,1,0:T(8,128)(2,1)S(1)}, u32[]{:S(2)}, u32[]{:S(2)}) collective-permute-start(bf16[2,128,128]{2,1,0:T(8,128)(2,1)S(1)} %get-tuple-element.90), channel_id=1, source_target_pairs={{0,12},{1,25},{2,14},{3,27},{4,8},{5,29},{6,10},{7,31},{8,4},{9,17... | collective-permute-start | bytes 196616 | tf_op jit(solution)/shard_map/ppermute | solution.py:532
  75.4 8.5 %collective-permute-start.19 = (bf16[2,128,128]{2,1,0:T(8,128)(2,1)S(1)}, bf16[2,128,128]{2,1,0:T(8,128)(2,1)S(1)}, u32[]{:S(2)}, u32[]{:S(2)}) collective-permute-start(bf16[2,128,128]{2,1,0:T(8,128)(2,1)S(1)} %get-tuple-element.91), channel_id=1, source_target_pairs={{0,8},{1,21},{2,10},{3,23},{4,12},{5,17},{6,14},{7,19},{8,0},{9,29... | collective-permute-start | bytes 196616 | tf_op jit(solution)/shard_map/ppermute | solution.py:532
  78.1 5.7 %collective-permute-start.20 = (bf16[2,128,128]{2,1,0:T(8,128)(2,1)S(1)}, bf16[2,128,128]{2,1,0:T(8,128)(2,1)S(1)}, u32[]{:S(2)}, u32[]{:S(2)}) collective-permute-start(bf16[2,128,128]{2,1,0:T(8,128)(2,1)S(1)} %get-tuple-element.92), channel_id=1, source_target_pairs={{0,4},{1,17},{2,6},{3,19},{4,0},{5,21},{6,2},{7,23},{8,12},{9,25},... | collective-permute-start | bytes 196616 | tf_op jit(solution)/shard_map/ppermute | solution.py:532
  85.3 12.5 %collective-permute-start.21 = (bf16[1536,128]{1,0:T(8,128)(2,1)S(1)}, bf16[1536,128]{1,0:T(8,128)(2,1)S(1)}, u32[]{:S(2)}, u32[]{:S(2)}) collective-permute-start(bf16[1536,128]{1,0:T(8,128)(2,1)S(1)} %get-tuple-element.103), channel_id=1, source_target_pairs={{0,2},{1,3},{2,0},{3,1},{4,6},{5,7},{6,4},{7,5},{8,10},{9,11},{10,... | collective-permute-start | bytes 1179656 | tf_op jit(solution)/shard_map/ppermute | solution.py:474
  86.8 5.8 %collective-permute-start.22 = (bf16[64,256]{1,0:T(8,128)(2,1)S(1)}, bf16[64,256]{1,0:T(8,128)(2,1)S(1)}, u32[]{:S(2)}, u32[]{:S(2)}) collective-permute-start(bf16[64,256]{1,0:T(8,128)(2,1)S(1)} %get-tuple-element.105), channel_id=1, source_target_pairs={{0,24},{4,28},{8,16},{12,20},{16,8},{20,12},{24,0},{28,4},{1,25},{... | collective-permute-start | bytes 98312 | tf_op jit(solution)/shard_map/ppermute | solution.py:474
  88.0 5.3 %collective-permute-start.23 = (bf16[64,256]{1,0:T(8,128)(2,1)S(1)}, bf16[64,256]{1,0:T(8,128)(2,1)S(1)}, u32[]{:S(2)}, u32[]{:S(2)}) collective-permute-start(bf16[64,256]{1,0:T(8,128)(2,1)S(1)} %get-tuple-element.106), channel_id=1, source_target_pairs={{0,16},{4,20},{8,24},{12,28},{16,0},{20,4},{24,8},{28,12},{1,17},{... | collective-permute-start | bytes 98312 | tf_op jit(solution)/shard_map/ppermute | solution.py:474
  88.0 5.4 %collective-permute-start.24 = (bf16[64,256]{1,0:T(8,128)(2,1)S(1)}, bf16[64,256]{1,0:T(8,128)(2,1)S(1)}, u32[]{:S(2)}, u32[]{:S(2)}) collective-permute-start(bf16[64,256]{1,0:T(8,128)(2,1)S(1)} %get-tuple-element.107), channel_id=1, source_target_pairs={{0,8},{4,12},{8,0},{12,4},{16,24},{20,28},{24,16},{28,20},{1,9},{5... | collective-permute-start | bytes 98312 | tf_op jit(solution)/shard_map/ppermute | solution.py:474
  97.9 6.2 %collective-permute-start.29 = (bf16[64,256]{1,0:T(8,128)(2,1)S(1)}, bf16[64,256]{1,0:T(8,128)(2,1)S(1)}, u32[]{:S(2)}, u32[]{:S(2)}) collective-permute-start(bf16[64,256]{1,0:T(8,128)(2,1)S(1)} %add_convert_fusion.after_ref.l0), channel_id=1, source_target_pairs={{0,24},{4,28},{8,16},{12,20},{16,8},{20,12},{24,0},{28,4},{1,25},{... | collective-permute-start | bytes 98312 | tf_op jit(solution)/shard_map/ppermute | solution.py:474
  100.0 5.2 %collective-permute-start.28 = (bf16[64,256]{1,0:T(8,128)(2,1)S(1)}, bf16[64,256]{1,0:T(8,128)(2,1)S(1)}, u32[]{:S(2)}, u32[]{:S(2)}) collective-permute-start(bf16[64,256]{1,0:T(8,128)(2,1)S(1)} %add_convert_fusion.after_ref.l0), channel_id=1, source_target_pairs={{0,16},{4,20},{8,24},{12,28},{16,0},{20,4},{24,8},{28,12},{1,17},{... | collective-permute-start | bytes 98312 | tf_op jit(solution)/shard_map/ppermute | solution.py:474
  (13 other events, 47.3 us)

commit v5 on v4

--- a/solution.py
+++ b/solution.py
@@ -69,30 +69,37 @@
     return (node >> shift) & 3
 
 
-def split(value, group, piece_refs):
+PIECE_STEPS = ((0, 3, 2, 1), (0, 1, 2, 3))
+
+
+def piece_at(group, step, head):
+    return group ^ jnp.where((head & 1) == 1, PIECE_STEPS[1][step], PIECE_STEPS[0][step])
+
+
+def split(value, group, head, piece_refs):
     size = value.shape[0] // 4
     for g in range(4):
-        for m in range(4):
-
-            @pl.when((group ^ m) == g)
+        for step in range(4):
+
+            @pl.when(piece_at(group, step, head) == g)
             def _():
-                piece_refs[m][...] = value[g * size : (g + 1) * size, :].astype(piece_refs[m].dtype)
+                piece_refs[step][...] = value[g * size : (g + 1) * size, :].astype(piece_refs[step].dtype)
 
 
 def split_kernel(shift, place_ref, value_ref, *piece_refs):
-    split(value_ref[...], group_of(place_ref[1], shift), piece_refs)
-
-
-def join(piece_refs, group, g):
+    split(value_ref[...], group_of(place_ref[1], shift), place_ref[0], piece_refs)
+
+
+def join(piece_refs, group, head, g):
     value = piece_refs[0][...]
-    for m in range(1, 4):
-        value = jnp.where((group ^ m) == g, piece_refs[m][...], value)
+    for step in range(1, 4):
+        value = jnp.where(piece_at(group, step, head) == g, piece_refs[step][...], value)
     return value
 
 
 def join_kernel(shift, place_ref, p0, p1, p2, p3, out_ref):
-    group = group_of(place_ref[1], shift)
-    out_ref[...] = jnp.concatenate([join((p0, p1, p2, p3), group, g) for g in range(4)], axis=0)
+    head, group = place_ref[0], group_of(place_ref[1], shift)
+    out_ref[...] = jnp.concatenate([join((p0, p1, p2, p3), group, head, g) for g in range(4)], axis=0)
 
 
 def sum_kernel(factor, *refs):
@@ -102,9 +109,9 @@
 
 
 def result_kernel(shift, place_ref, l0, l1, l2, l3, after_ref, in_ref, out_ref):
-    group = group_of(place_ref[1], shift)
-    for m, piece_ref in enumerate((l0, l1, l2, l3)):
-        at = group ^ m
+    head, group = place_ref[0], group_of(place_ref[1], shift)
+    for step, piece_ref in enumerate((l0, l1, l2, l3)):
+        at = piece_at(group, step, head)
 
         @pl.when(at == 0)
         def _():
@@ -137,15 +144,12 @@
     return jnp.where((head & 1) == 1, odd[step], even[step])
 
 
-def project_kernel(count, place_ref, wanted_ref, pair_ref, other_ref, in_from, *refs):
+def project_kernel(count, place_ref, wanted_ref, pair_ref, other_ref, in_ref, *refs):
     qz_ref, kv_ref, refs = refs[0], refs[1], refs[2:]
-    out_refs, (wide_ref, in_ref, sem) = refs[:count], refs[count:]
-    in_copy = pltpu.make_async_copy(in_from, in_ref, sem)
-    in_copy.start()
+    out_refs, wide_ref = refs[:count], refs[count]
     x_refs = parts_of(pair_ref, other_ref)
     head, node = place_ref[0], place_ref[1]
     rows = x_refs[0].shape[0]
-    in_copy.wait()
     wide_ref[:, HD:BLOCK] = jnp.zeros((D, HD), BF16)
     for g in range(HEADS):
 
@@ -265,7 +269,7 @@
 
 def middle_kernel(
     place_ref, x_pair, x_other, c_pair, c_other, a_pair, a_other, attt_ref, w_ref,
-    out_ref, grad_out, gz_ref, dots_ref, owg_ref, wide_ref, pad_ref, grad_ref, sem,
+    out_ref, grad_out, gz_ref, dots_ref, low_ref, wide_ref, pad_ref, grad_ref, sem,
 ):
     head = place_ref[0]
     rows = grad_ref.shape[0]
@@ -280,7 +284,6 @@
     pad_ref[:HD, :] = jnp.zeros((HD, D), BF16)
     pad_ref[HD:, :] = own_w
     a_refs = parts_of(a_pair, a_other)
-    owg = jnp.zeros((HD, D), F32)
     pairs = rows // (2 * BLOCK)
     for part, (x_ref, c_ref) in enumerate(zip(parts_of(x_pair, x_other), parts_of(c_pair, c_other))):
         group = head ^ part
@@ -314,8 +317,7 @@
             dots_ref[group * (2 * pairs) + i] = jnp.broadcast_to(
                 sums[:, i * BLOCK : (i + 1) * BLOCK], (8, BLOCK)
             )
-        owg += dot(attended, low)
-    owg_ref[...] = owg
+        low_ref[at, :] = low
     grad_copy.wait()
 
 
@@ -385,7 +387,11 @@
         dq_refs[part][...] = dq_ref[span((head ^ part) * size, size), :]
 
 
-def query_weight_kernel(place_ref, dqt_ref, pair_ref, other_ref, in_ref, out_ref, wkv_ref, wq_ref, k_ref, q_ref):
+def query_weight_kernel(
+    place_ref, dqt_ref, pair_ref, other_ref, in_ref, attt_ref, low_ref,
+    out_ref, owg_ref, wkv_ref, wq_ref, k_ref, q_ref,
+):
+    owg_ref[...] = dot(attt_ref[...], low_ref[...])
     head = place_ref[0]
     rows = pair_ref.shape[0] // 2
     total = jnp.zeros((HD, D), F32)
@@ -428,7 +434,7 @@
         rows = 2 * dq_refs[part].shape[0]
         total += dot(xt_ref[:, span((head ^ part) * rows, rows)], send_refs[part][:rows, :])
     every = jnp.concatenate([owg_ref[...], qwg_ref[...], total.T], axis=0)
-    split(every, group_of(node, top_shift(count)), piece_refs)
+    split(every, group_of(node, top_shift(count)), head, piece_refs)
 
 
 def relay_kernel(beside_ref, across_ref, after_ref, out_ref):
@@ -484,14 +490,19 @@
         )(*values, *after)
         return pair, swap(pair, "head", 1)
 
-    def exchange(pieces, axis, unit=1):
+    def exchange_nodes(pieces, masks, unit=1):
         moved = list(pieces)
-        for mask in reversed(range(1, len(pieces))):
-            moved[mask] = swap(pieces[mask], axis, mask * unit)
+        for step in range(1, len(pieces)):
+            perm = [
+                (n * head_count + h, (n ^ (masks[h & 1][step] * unit)) * head_count + h)
+                for n in range(node_count)
+                for h in range(head_count)
+            ]
+            moved[step] = lax.ppermute(pieces[step], ("node", "head"), perm)
         return moved
 
     def add_nodes(pieces, shift, factor, after=()):
-        moved = exchange(pieces, "node", 1 << shift)
+        moved = exchange_nodes(pieces, PIECE_STEPS, 1 << shift)
         piece = (pieces[0].shape, F32)
         (total,) = call(
             functools.partial(sum_kernel, factor),
@@ -499,7 +510,7 @@
             [piece],
             [vmem()] * (4 + len(after)),
             4 * MIB,
-        )(moved[0], *moved[:0:-1], *after)
+        )(*moved, *after)
         if shift == 1:
             total = total + swap(total, "node", 1)
         elif shift > 1:
@@ -518,19 +529,7 @@
                 limit,
             )(place, *add_nodes(lower, shift - 2, 1.0)[0])
         total = total.astype(pieces[0].dtype)
-        return exchange([total] * 4, "node", 1 << shift), total
-
-    def exchange_nodes(pieces):
-        moved = list(pieces)
-        even, odd = step_masks(node_count)
-        for step in range(1, node_count):
-            perm = [
-                (n * head_count + h, (n ^ (odd if h & 1 else even)[step]) * head_count + h)
-                for n in range(node_count)
-                for h in range(head_count)
-            ]
-            moved[step] = lax.ppermute(pieces[step], ("node", "head"), perm)
-        return moved
+        return exchange_nodes([total] * 4, PIECE_STEPS, 1 << shift), total
 
     across = swap(features, "head", 2)
     c_across = swap(cotangent, "head", 2)
@@ -542,16 +541,12 @@
         functools.partial(project_kernel, node_count),
         "project",
         [((node_rows, BLOCK), BF16)] * 2 + [(block_set, BF16)] * node_count,
-        [smem()] * 2 + [vmem()] * 2 + [hbm()],
+        [smem()] * 2 + [vmem()] * 3,
         limit,
         flops=2 * node_rows * D * D,
-        scratch=[
-            pltpu.VMEM((D, D), BF16),
-            pltpu.VMEM((D, 3 * D), BF16),
-            pltpu.SemaphoreType.DMA,
-        ],
+        scratch=[pltpu.VMEM((D, D), BF16)],
     )(place, wants, *xs, in_weight)
-    incoming = exchange_nodes(outgoing)
+    incoming = exchange_nodes(outgoing, step_masks(node_count))
     xt, kvt = call(
         prepare_kernel,
         "prepare",
@@ -596,7 +591,7 @@
     late_across = swap(late_att, "head", 2)
     parts = pair_up([early_att, late_att, early_across, late_across])
     cs = pair_up([cotangent, c_across], [top])
-    output, norm_grad, gz, dots, owg = call(
+    output, norm_grad, gz, dots, low = call(
         middle_kernel,
         "middle",
         [
@@ -604,7 +599,7 @@
             ((rows, D), F32),
             ((node_rows, BLOCK), BF16),
             ((BLK, 8, BLOCK), F32),
-            ((HD, D), F32),
+            ((node_rows, D), BF16),
         ],
         [smem()] + [vmem()] * 8,
         limit,
@@ -633,16 +628,16 @@
             pltpu.VMEM((PER * BLOCK, 2 * BLOCK), F32),
         ],
     )(place, key_slots, block_count, qz, gz, table, tablet, top, inv, dots)
-    returned = exchange_nodes(rest[4:])
-    query_wg, wkv, wq = call(
+    returned = exchange_nodes(rest[4:], step_masks(node_count))
+    query_wg, owg, wkv, wq = call(
         query_weight_kernel,
         "query_weight",
-        [((HD, D), F32), ((D, 2 * D), BF16), ((2 * D, 2 * D), BF16)],
-        [smem()] + [vmem()] * 4,
+        [((HD, D), F32)] * 2 + [((D, 2 * D), BF16), ((2 * D, 2 * D), BF16)],
+        [smem()] + [vmem()] * 6,
         limit,
         flops=2 * node_rows * D * HD,
         scratch=[pltpu.VMEM((HEADS, D, BLOCK), BF16), pltpu.VMEM((HEADS, 2 * D, BLOCK), BF16)],
-    )(place, dqt, *xs, in_weight)
+    )(place, dqt, *xs, in_weight, attt, low)
     sent = ((rows * 3 // 2, BLOCK), BF16)
     collected = call(
         functools.partial(collect_kernel, node_count),

time: 107 us -> 107 us (level)
    ppermute x14 -> x20, starting transfers between devices: 22.4 us -> 31.2 us  [exchange_nodes(): moved[step] = lax.ppermute(pieces[step], ('node', 'head'), perm)]
    ppermute x16 -> x10, starting transfers between devices: 17 us -> 8.4 us  [swap(): return lax.ppermute(value, axis, [(i, i ^ mask) for i in range(size)])]
    ppermute x14 -> x20, waiting for transfers between devices: 7.07 us -> 11.3 us  [exchange_nodes(): moved[step] = lax.ppermute(pieces[step], ('node', 'head'), perm)]
    ppermute x16 -> x10, waiting for transfers between devices: 14.3 us -> 10.4 us  [swap(): return lax.ppermute(value, axis, [(i, i ^ mask) for i in range(size)])]
  transfers between devices with their start and end apart: 30 -> 30, of which waited for: 15 -> 13; matrix products, arithmetic and copies ran while one was open for 0% -> 0% of each run, Pallas kernels for 9% -> 9%
where the time goes in v5:
time: 107 us
  starting transfers between devices  39.6 us (37%)
  Pallas kernels  31.8 us (30%)
  waiting for transfers between devices  21.8 us (20%)
  blocking collectives  12.1 us (11%)
  local copies, waits for them, and re-layouts  1.12 us (1%)
    ppermute x20, starting transfers between devices, exchange_nodes(): moved[step] = lax.ppermute(pieces[step], ('node', 'head'), perm)  31.2 us
    all_to_all x1, blocking collectives, on_device(): lax.all_to_all(wanted.reshape(node_count, 1, CAP), 'node', split_axis=0,...  12.1 us
    ppermute x20, waiting for transfers between devices, exchange_nodes(): moved[step] = lax.ppermute(pieces[step], ('node', 'head'), perm)  11.3 us
    pallas_call x1, Pallas kernels, on_device(): call(functools.partial(backward_kernel, node_count), 'backward', [((BLK,...  11 us
    ppermute x10, waiting for transfers between devices, swap(): return lax.ppermute(value, axis, [(i, i ^ mask) for i in range(size)])  10.4 us
    ppermute x10, starting transfers between devices, swap(): return lax.ppermute(value, axis, [(i, i ^ mask) for i in range(size)])  8.4 us
    pallas_call x1, Pallas kernels, on_device(): call(functools.partial(early_forward_kernel, node_count), 'early_forward'...  4.67 us
    pallas_call x1, Pallas kernels, on_device(): call(late_forward_kernel, 'late_forward', [half_att, ((HD, node_rows), BF...  4.49 us
  transfers between devices with their start and end apart: 30, of which 13 were waited for; matrix products, arithmetic and copies ran while one was open for 0% of the time, Pallas kernels for 9%

profile of v5, /device:TPU:0, one launch (start us, length us, event | category | flops | bytes accessed | tf_op | source)
XLA Modules:
  0.0 107.3 jit_solution(17583260987548182376)
XLA Ops:
  0.6 3.0 %collective-permute-start = (bf16[512,256]{1,0:T(8,128)(2,1)}, bf16[512,256]{1,0:T(8,128)(2,1)S(1)}, u32[]{:S(2)}, u32[]{:S(2)}) collective-permute-start(bf16[512,256]{1,0:T(8,128)(2,1)} %refs_0_.2), channel_id=1, source_target_pairs={{0,2},{1,3},{2,0},{3,1},{4,6},{5,7},{6,4},{7,5},{8,10},{9,11},{10,... | collective-permute-start | bytes 786440 | tf_op jit(solution)/shard_map/ppermute | solution.py:480
  3.7 12.1 %all_to_all.5.refs_2_.wanted_ref = s32[8,1,2]{2,1,0:T(1,128)S(1)} all-to-all(s32[8,1,2]{2,1,0:T(1,128)S(1)} %copy.11), channel_id=1, replica_groups=mesh['node'=8,'head'=4] {'node'}, dimensions={0} | all-to-all | bytes 128 | tf_op jit(solution)/shard_map/all_to_all | solution.py:536
  20.7 3.2 %collective-permute-start.4 = (bf16[2,128,128]{2,1,0:T(8,128)(2,1)S(1)}, bf16[2,128,128]{2,1,0:T(8,128)(2,1)S(1)}, u32[]{:S(2)}, u32[]{:S(2)}) collective-permute-start(bf16[2,128,128]{2,1,0:T(8,128)(2,1)S(1)} %get-tuple-element.65), channel_id=1, source_target_pairs={{0,24},{1,9},{2,26},{3,11},{4,28},{5,13},{6,30},{7,15},{8,16},{9,1... | collective-permute-start | bytes 196616 | tf_op jit(solution)/shard_map/ppermute | solution.py:501
  24.0 3.8 %collective-permute-start.6 = (bf16[2,128,128]{2,1,0:T(8,128)(2,1)S(1)}, bf16[2,128,128]{2,1,0:T(8,128)(2,1)S(1)}, u32[]{:S(2)}, u32[]{:S(2)}) collective-permute-start(bf16[2,128,128]{2,1,0:T(8,128)(2,1)S(1)} %get-tuple-element.67), channel_id=1, source_target_pairs={{0,16},{1,29},{2,18},{3,31},{4,20},{5,25},{6,22},{7,27},{8,24},{9,... | collective-permute-start | bytes 196616 | tf_op jit(solution)/shard_map/ppermute | solution.py:501
  27.8 2.0 %collective-permute-start.8 = (bf16[2,128,128]{2,1,0:T(8,128)(2,1)S(1)}, bf16[2,128,128]{2,1,0:T(8,128)(2,1)S(1)}, u32[]{:S(2)}, u32[]{:S(2)}) collective-permute-start(bf16[2,128,128]{2,1,0:T(8,128)(2,1)S(1)} %get-tuple-element.69), channel_id=1, source_target_pairs={{0,8},{1,21},{2,10},{3,23},{4,12},{5,17},{6,14},{7,19},{8,0},{9,29... | collective-permute-start | bytes 196616 | tf_op jit(solution)/shard_map/ppermute | solution.py:501
  32.8 2.2 %collective-permute-done.6.refs_4_ = bf16[2,128,128]{2,1,0:T(8,128)(2,1)S(1)} collective-permute-done((bf16[2,128,128]{2,1,0:T(8,128)(2,1)S(1)}, bf16[2,128,128]{2,1,0:T(8,128)(2,1)S(1)}, u32[]{:S(2)}, u32[]{:S(2)}) %collective-permute-start.6) | collective-permute-done | bytes 65568 | tf_op jit(solution)/shard_map/ppermute | solution.py:501
  35.1 4.7 %early_forward.1 = (bf16[512,128]{1,0:T(8,128)(2,1)S(1)}, bf16[64,1024]{1,0:T(8,128)(2,1)S(1)}, bf16[32,128,128]{2,1,0:T(8,128)(2,1)S(1)}, bf16[32,128,128]{2,1,...) custom-call(s32[2]{0:T(128)S(1)} %pad_add_fusion.place_ref, s32[16,12]{1,0:T(8,128)S(1)} %copy-done.3, ...), custom_call_target="tpu_custom_call" | custom-call | flops 805306368 | bytes 4194304 | tf_op jit(solution)/shard_map/early_forward/pallas_call | solution.py:560
  40.4 4.5 %late_forward.1 = (bf16[512,128]{1,0:T(8,128)(2,1)S(1)}, bf16[64,2048]{1,0:T(8,128)(2,1)S(1)}, f32[16,8,128]{2,1,0:T(8,128)S(1)}, f32[16,8,128]{2,1,0:T(8,128)S(1)}) custom-call(s32[16,12]{1,0:T(8,128)S(1)} %copy-done.3, s32[16]{0:T(128)S(1)} %copy-done.4, bf16[2048,128]{1,0:T(8,128)(2,1)S(1)} %get-tuple-element.60.qz_ref, ...), custom_call_target="tpu_custom_call" | custom-call | flops 805306368 | bytes 4194304 | tf_op jit(solution)/shard_map/late_forward/pallas_call | solution.py:577
  44.9 1.5 %collective-permute-start.12 = (bf16[512,128]{1,0:T(8,128)(2,1)S(1)}, bf16[512,128]{1,0:T(8,128)(2,1)S(1)}, u32[]{:S(2)}, u32[]{:S(2)}) collective-permute-start(bf16[512,128]{1,0:T(8,128)(2,1)S(1)} %get-tuple-element.78.refs_1_), channel_id=1, source_target_pairs={{0,2},{1,3},{2,0},{3,1},{4,6},{5,7},{6,4},{7,5},{8,10},{9,11},{10,... | collective-permute-start | bytes 393224 | tf_op jit(solution)/shard_map/ppermute | solution.py:480
  46.5 3.8 %collective-permute-done.12.refs_3_ = bf16[512,128]{1,0:T(8,128)(2,1)S(1)} collective-permute-done((bf16[512,128]{1,0:T(8,128)(2,1)S(1)}, bf16[512,128]{1,0:T(8,128)(2,1)S(1)}, u32[]{:S(2)}, u32[]{:S(2)}) %collective-permute-start.12) | collective-permute-done | bytes 131104 | tf_op jit(solution)/shard_map/ppermute | solution.py:480
  50.5 1.9 %collective-permute-done.13.a_other = bf16[2048,128]{1,0:T(8,128)(2,1)S(1)} collective-permute-done((bf16[2048,128]{1,0:T(8,128)(2,1)S(1)}, bf16[2048,128]{1,0:T(8,128)(2,1)S(1)}, u32[]{:S(2)}, u32[]{:S(2)}) %collective-permute-start.13) | collective-permute-done | bytes 524320 | tf_op jit(solution)/shard_map/ppermute | solution.py:480
  52.4 4.0 %middle.1 = (bf16[512,256]{1,0:T(8,128)(2,1)}, f32[512,256]{1,0:T(8,128)S(1)}, bf16[2048,128]{1,0:T(8,128)(2,1)S(1)}, f32[16,8,128]{2,1,0:T(8,128)S(1)}, bf16[2048,256]{1,0:T(8,128)(2,1)S(1)}) custom-call(s32[2]{0:T(128)S(1)} %pad_add_fusion.place_ref, bf16[1024,256]{1,0:T(8,128)(2,1)S(1)} %pair.3.pair_ref.x_pair, ...), custom_call_target="tpu_custom_call" | custom-call | flops 1073741824 | bytes 4194304 | tf_op jit(solution)/shard_map/middle/pallas_call | solution.py:594
  56.4 11.0 %backward.1 = (f32[16,128,128]{2,1,0:T(8,128)S(1)}, bf16[64,2048]{1,0:T(8,128)(2,1)S(1)}, bf16[256,128]{1,0:T(8,128)(2,1)S(1)}, bf16[256,128]{1,0:T(8,128)(2,1)S...) custom-call(s32[2]{0:T(128)S(1)} %pad_add_fusion.place_ref, ...), custom_call_target="tpu_custom_call" | custom-call | flops 4026531840 | bytes 4194304 | tf_op jit(solution)/shard_map/backward/pallas_call | solution.py:615
  67.4 2.2 %collective-permute-start.14 = (bf16[2,128,128]{2,1,0:T(8,128)(2,1)S(1)}, bf16[2,128,128]{2,1,0:T(8,128)(2,1)S(1)}, u32[]{:S(2)}, u32[]{:S(2)}) collective-permute-start(bf16[2,128,128]{2,1,0:T(8,128)(2,1)S(1)} %get-tuple-element.87), channel_id=1, source_target_pairs={{0,28},{1,13},{2,30},{3,15},{4,24},{5,9},{6,26},{7,11},{8,20},{9,5... | collective-permute-start | bytes 196616 | tf_op jit(solution)/shard_map/ppermute | solution.py:501
  69.6 2.4 %collective-permute-start.15 = (bf16[2,128,128]{2,1,0:T(8,128)(2,1)S(1)}, bf16[2,128,128]{2,1,0:T(8,128)(2,1)S(1)}, u32[]{:S(2)}, u32[]{:S(2)}) collective-permute-start(bf16[2,128,128]{2,1,0:T(8,128)(2,1)S(1)} %get-tuple-element.88), channel_id=1, source_target_pairs={{0,24},{1,9},{2,26},{3,11},{4,28},{5,13},{6,30},{7,15},{8,16},{9,1... | collective-permute-start | bytes 196616 | tf_op jit(solution)/shard_map/ppermute | solution.py:501
  72.0 3.1 %collective-permute-start.17 = (bf16[2,128,128]{2,1,0:T(8,128)(2,1)S(1)}, bf16[2,128,128]{2,1,0:T(8,128)(2,1)S(1)}, u32[]{:S(2)}, u32[]{:S(2)}) collective-permute-start(bf16[2,128,128]{2,1,0:T(8,128)(2,1)S(1)} %get-tuple-element.90), channel_id=1, source_target_pairs={{0,16},{1,29},{2,18},{3,31},{4,20},{5,25},{6,22},{7,27},{8,24},{9,... | collective-permute-start | bytes 196616 | tf_op jit(solution)/shard_map/ppermute | solution.py:501
  75.1 2.7 %collective-permute-start.19 = (bf16[2,128,128]{2,1,0:T(8,128)(2,1)S(1)}, bf16[2,128,128]{2,1,0:T(8,128)(2,1)S(1)}, u32[]{:S(2)}, u32[]{:S(2)}) collective-permute-start(bf16[2,128,128]{2,1,0:T(8,128)(2,1)S(1)} %get-tuple-element.92), channel_id=1, source_target_pairs={{0,8},{1,21},{2,10},{3,23},{4,12},{5,17},{6,14},{7,19},{8,0},{9,29... | collective-permute-start | bytes 196616 | tf_op jit(solution)/shard_map/ppermute | solution.py:501
  79.7 2.2 %collective-permute-done.16.refs_3_ = bf16[2,128,128]{2,1,0:T(8,128)(2,1)S(1)} collective-permute-done((bf16[2,128,128]{2,1,0:T(8,128)(2,1)S(1)}, bf16[2,128,128]{2,1,0:T(8,128)(2,1)S(1)}, u32[]{:S(2)}, u32[]{:S(2)}) %collective-permute-start.16) | collective-permute-done | bytes 65568 | tf_op jit(solution)/shard_map/ppermute | solution.py:501
  85.0 1.5 %collective-permute-start.21 = (bf16[1536,128]{1,0:T(8,128)(2,1)S(1)}, bf16[1536,128]{1,0:T(8,128)(2,1)S(1)}, u32[]{:S(2)}, u32[]{:S(2)}) collective-permute-start(bf16[1536,128]{1,0:T(8,128)(2,1)S(1)} %get-tuple-element.105), channel_id=1, source_target_pairs={{0,2},{1,3},{2,0},{3,1},{4,6},{5,7},{6,4},{7,5},{8,10},{9,11},{10,... | collective-permute-start | bytes 1179656 | tf_op jit(solution)/shard_map/ppermute | solution.py:480
  87.8 3.1 %collective-permute-start.24 = (bf16[64,256]{1,0:T(8,128)(2,1)S(1)}, bf16[64,256]{1,0:T(8,128)(2,1)S(1)}, u32[]{:S(2)}, u32[]{:S(2)}) collective-permute-start(bf16[64,256]{1,0:T(8,128)(2,1)S(1)} %get-tuple-element.109), channel_id=1, source_target_pairs={{0,8},{1,25},{2,10},{3,27},{4,12},{5,29},{6,14},{7,31},{8,0},{9,17... | collective-permute-start | bytes 98312 | tf_op jit(solution)/shard_map/ppermute | solution.py:501
  94.0 3.5 %collective-permute-done.25 = f32[64,256]{1,0:T(8,128)S(1)} collective-permute-done((f32[64,256]{1,0:T(8,128)S(1)}, f32[64,256]{1,0:T(8,128)S(1)}, u32[]{:S(2)}, u32[]{:S(2)}) %collective-permute-start.25) | collective-permute-done | bytes 65568 | tf_op jit(solution)/shard_map/ppermute | solution.py:480
  97.6 1.8 %collective-permute-start.29 = (bf16[64,256]{1,0:T(8,128)(2,1)S(1)}, bf16[64,256]{1,0:T(8,128)(2,1)S(1)}, u32[]{:S(2)}, u32[]{:S(2)}) collective-permute-start(bf16[64,256]{1,0:T(8,128)(2,1)S(1)} %add_convert_fusion.after_ref.l0), channel_id=1, source_target_pairs={{0,8},{1,25},{2,10},{3,27},{4,12},{5,29},{6,14},{7,31},{8,0},{9,17... | collective-permute-start | bytes 98312 | tf_op jit(solution)/shard_map/ppermute | solution.py:501
  100.3 1.8 %collective-permute-start.27 = (bf16[64,256]{1,0:T(8,128)(2,1)S(1)}, bf16[64,256]{1,0:T(8,128)(2,1)S(1)}, u32[]{:S(2)}, u32[]{:S(2)}) collective-permute-start(bf16[64,256]{1,0:T(8,128)(2,1)S(1)} %add_convert_fusion.after_ref.l0), channel_id=1, source_target_pairs={{0,24},{1,9},{2,26},{3,11},{4,28},{5,13},{6,30},{7,15},{8,16},{9,1... | collective-permute-start | bytes 98312 | tf_op jit(solution)/shard_map/ppermute | solution.py:501
  104.4 1.6 %collective-permute-done.27.l1 = bf16[64,256]{1,0:T(8,128)(2,1)S(1)} collective-permute-done((bf16[64,256]{1,0:T(8,128)(2,1)S(1)}, bf16[64,256]{1,0:T(8,128)(2,1)S(1)}, u32[]{:S(2)}, u32[]{:S(2)}) %collective-permute-start.27) | collective-permute-done | bytes 32800 | tf_op jit(solution)/shard_map/ppermute | solution.py:501
  (69 shorter events, 22.8 us)
Async XLA Ops:
  0.6 15.2 %collective-permute-start = (bf16[512,256]{1,0:T(8,128)(2,1)}, bf16[512,256]{1,0:T(8,128)(2,1)S(1)}, u32[]{:S(2)}, u32[]{:S(2)}) collective-permute-start(bf16[512,256]{1,0:T(8,128)(2,1)} %refs_0_.2), channel_id=1, source_target_pairs={{0,2},{1,3},{2,0},{3,1},{4,6},{5,7},{6,4},{7,5},{8,10},{9,11},{10,... | collective-permute-start | bytes 786440 | tf_op jit(solution)/shard_map/ppermute | solution.py:480
  17.0 10.8 %collective-permute-start.2 = (bf16[512,256]{1,0:T(8,128)(2,1)S(1)}, bf16[512,256]{1,0:T(8,128)(2,1)S(1)}, u32[]{:S(2)}, u32[]{:S(2)}) collective-permute-start(bf16[512,256]{1,0:T(8,128)(2,1)S(1)} %copy-done.1), channel_id=1, source_target_pairs={{0,2},{1,3},{2,0},{3,1},{4,6},{5,7},{6,4},{7,5},{8,10},{9,11},{10,... | collective-permute-start | bytes 786440 | tf_op jit(solution)/shard_map/ppermute | solution.py:480
  20.1 7.7 %collective-permute-start.3 = (bf16[2,128,128]{2,1,0:T(8,128)(2,1)S(1)}, bf16[2,128,128]{2,1,0:T(8,128)(2,1)S(1)}, u32[]{:S(2)}, u32[]{:S(2)}) collective-permute-start(bf16[2,128,128]{2,1,0:T(8,128)(2,1)S(1)} %get-tuple-element.64), channel_id=1, source_target_pairs={{0,28},{1,13},{2,30},{3,15},{4,24},{5,9},{6,26},{7,11},{8,20},{9,5... | collective-permute-start | bytes 196616 | tf_op jit(solution)/shard_map/ppermute | solution.py:501
  20.7 9.1 %collective-permute-start.4 = (bf16[2,128,128]{2,1,0:T(8,128)(2,1)S(1)}, bf16[2,128,128]{2,1,0:T(8,128)(2,1)S(1)}, u32[]{:S(2)}, u32[]{:S(2)}) collective-permute-start(bf16[2,128,128]{2,1,0:T(8,128)(2,1)S(1)} %get-tuple-element.65), channel_id=1, source_target_pairs={{0,24},{1,9},{2,26},{3,11},{4,28},{5,13},{6,30},{7,15},{8,16},{9,1... | collective-permute-start | bytes 196616 | tf_op jit(solution)/shard_map/ppermute | solution.py:501
  24.0 8.9 %collective-permute-start.5 = (bf16[2,128,128]{2,1,0:T(8,128)(2,1)S(1)}, bf16[2,128,128]{2,1,0:T(8,128)(2,1)S(1)}, u32[]{:S(2)}, u32[]{:S(2)}) collective-permute-start(bf16[2,128,128]{2,1,0:T(8,128)(2,1)S(1)} %get-tuple-element.66), channel_id=1, source_target_pairs={{0,20},{1,5},{2,22},{3,7},{4,16},{5,1},{6,18},{7,3},{8,28},{9,13},... | collective-permute-start | bytes 196616 | tf_op jit(solution)/shard_map/ppermute | solution.py:501
  24.0 11.1 %collective-permute-start.6 = (bf16[2,128,128]{2,1,0:T(8,128)(2,1)S(1)}, bf16[2,128,128]{2,1,0:T(8,128)(2,1)S(1)}, u32[]{:S(2)}, u32[]{:S(2)}) collective-permute-start(bf16[2,128,128]{2,1,0:T(8,128)(2,1)S(1)} %get-tuple-element.67), channel_id=1, source_target_pairs={{0,16},{1,29},{2,18},{3,31},{4,20},{5,25},{6,22},{7,27},{8,24},{9,... | collective-permute-start | bytes 196616 | tf_op jit(solution)/shard_map/ppermute | solution.py:501
  27.8 7.3 %collective-permute-start.7 = (bf16[2,128,128]{2,1,0:T(8,128)(2,1)S(1)}, bf16[2,128,128]{2,1,0:T(8,128)(2,1)S(1)}, u32[]{:S(2)}, u32[]{:S(2)}) collective-permute-start(bf16[2,128,128]{2,1,0:T(8,128)(2,1)S(1)} %get-tuple-element.68), channel_id=1, source_target_pairs={{0,12},{1,25},{2,14},{3,27},{4,8},{5,29},{6,10},{7,31},{8,4},{9,17... | collective-permute-start | bytes 196616 | tf_op jit(solution)/shard_map/ppermute | solution.py:501
  27.8 7.2 %collective-permute-start.8 = (bf16[2,128,128]{2,1,0:T(8,128)(2,1)S(1)}, bf16[2,128,128]{2,1,0:T(8,128)(2,1)S(1)}, u32[]{:S(2)}, u32[]{:S(2)}) collective-permute-start(bf16[2,128,128]{2,1,0:T(8,128)(2,1)S(1)} %get-tuple-element.69), channel_id=1, source_target_pairs={{0,8},{1,21},{2,10},{3,23},{4,12},{5,17},{6,14},{7,19},{8,0},{9,29... | collective-permute-start | bytes 196616 | tf_op jit(solution)/shard_map/ppermute | solution.py:501
  29.8 5.2 %collective-permute-start.9 = (bf16[2,128,128]{2,1,0:T(8,128)(2,1)S(1)}, bf16[2,128,128]{2,1,0:T(8,128)(2,1)S(1)}, u32[]{:S(2)}, u32[]{:S(2)}) collective-permute-start(bf16[2,128,128]{2,1,0:T(8,128)(2,1)S(1)} %get-tuple-element.70), channel_id=1, source_target_pairs={{0,4},{1,17},{2,6},{3,19},{4,0},{5,21},{6,2},{7,23},{8,12},{9,25},... | collective-permute-start | bytes 196616 | tf_op jit(solution)/shard_map/ppermute | solution.py:501
  39.8 6.8 %collective-permute-start.11 = (bf16[512,128]{1,0:T(8,128)(2,1)S(1)}, bf16[512,128]{1,0:T(8,128)(2,1)S(1)}, u32[]{:S(2)}, u32[]{:S(2)}) collective-permute-start(bf16[512,128]{1,0:T(8,128)(2,1)S(1)} %get-tuple-element.77.refs_0_), channel_id=1, source_target_pairs={{0,2},{1,3},{2,0},{3,1},{4,6},{5,7},{6,4},{7,5},{8,10},{9,11},{10,... | collective-permute-start | bytes 393224 | tf_op jit(solution)/shard_map/ppermute | solution.py:480
  44.9 5.5 %collective-permute-start.12 = (bf16[512,128]{1,0:T(8,128)(2,1)S(1)}, bf16[512,128]{1,0:T(8,128)(2,1)S(1)}, u32[]{:S(2)}, u32[]{:S(2)}) collective-permute-start(bf16[512,128]{1,0:T(8,128)(2,1)S(1)} %get-tuple-element.78.refs_1_), channel_id=1, source_target_pairs={{0,2},{1,3},{2,0},{3,1},{4,6},{5,7},{6,4},{7,5},{8,10},{9,11},{10,... | collective-permute-start | bytes 393224 | tf_op jit(solution)/shard_map/ppermute | solution.py:480
  67.4 7.7 %collective-permute-start.14 = (bf16[2,128,128]{2,1,0:T(8,128)(2,1)S(1)}, bf16[2,128,128]{2,1,0:T(8,128)(2,1)S(1)}, u32[]{:S(2)}, u32[]{:S(2)}) collective-permute-start(bf16[2,128,128]{2,1,0:T(8,128)(2,1)S(1)} %get-tuple-element.87), channel_id=1, source_target_pairs={{0,28},{1,13},{2,30},{3,15},{4,24},{5,9},{6,26},{7,11},{8,20},{9,5... | collective-permute-start | bytes 196616 | tf_op jit(solution)/shard_map/ppermute | solution.py:501
  69.6 8.3 %collective-permute-start.15 = (bf16[2,128,128]{2,1,0:T(8,128)(2,1)S(1)}, bf16[2,128,128]{2,1,0:T(8,128)(2,1)S(1)}, u32[]{:S(2)}, u32[]{:S(2)}) collective-permute-start(bf16[2,128,128]{2,1,0:T(8,128)(2,1)S(1)} %get-tuple-element.88), channel_id=1, source_target_pairs={{0,24},{1,9},{2,26},{3,11},{4,28},{5,13},{6,30},{7,15},{8,16},{9,1... | collective-permute-start | bytes 196616 | tf_op jit(solution)/shard_map/ppermute | solution.py:501
  72.0 9.9 %collective-permute-start.16 = (bf16[2,128,128]{2,1,0:T(8,128)(2,1)S(1)}, bf16[2,128,128]{2,1,0:T(8,128)(2,1)S(1)}, u32[]{:S(2)}, u32[]{:S(2)}) collective-permute-start(bf16[2,128,128]{2,1,0:T(8,128)(2,1)S(1)} %get-tuple-element.89), channel_id=1, source_target_pairs={{0,20},{1,5},{2,22},{3,7},{4,16},{5,1},{6,18},{7,3},{8,28},{9,13},... | collective-permute-start | bytes 196616 | tf_op jit(solution)/shard_map/ppermute | solution.py:501
  72.0 10.9 %collective-permute-start.17 = (bf16[2,128,128]{2,1,0:T(8,128)(2,1)S(1)}, bf16[2,128,128]{2,1,0:T(8,128)(2,1)S(1)}, u32[]{:S(2)}, u32[]{:S(2)}) collective-permute-start(bf16[2,128,128]{2,1,0:T(8,128)(2,1)S(1)} %get-tuple-element.90), channel_id=1, source_target_pairs={{0,16},{1,29},{2,18},{3,31},{4,20},{5,25},{6,22},{7,27},{8,24},{9,... | collective-permute-start | bytes 196616 | tf_op jit(solution)/shard_map/ppermute | solution.py:501
  75.1 7.8 %collective-permute-start.18 = (bf16[2,128,128]{2,1,0:T(8,128)(2,1)S(1)}, bf16[2,128,128]{2,1,0:T(8,128)(2,1)S(1)}, u32[]{:S(2)}, u32[]{:S(2)}) collective-permute-start(bf16[2,128,128]{2,1,0:T(8,128)(2,1)S(1)} %get-tuple-element.91), channel_id=1, source_target_pairs={{0,12},{1,25},{2,14},{3,27},{4,8},{5,29},{6,10},{7,31},{8,4},{9,17... | collective-permute-start | bytes 196616 | tf_op jit(solution)/shard_map/ppermute | solution.py:501
  75.1 8.5 %collective-permute-start.19 = (bf16[2,128,128]{2,1,0:T(8,128)(2,1)S(1)}, bf16[2,128,128]{2,1,0:T(8,128)(2,1)S(1)}, u32[]{:S(2)}, u32[]{:S(2)}) collective-permute-start(bf16[2,128,128]{2,1,0:T(8,128)(2,1)S(1)} %get-tuple-element.92), channel_id=1, source_target_pairs={{0,8},{1,21},{2,10},{3,23},{4,12},{5,17},{6,14},{7,19},{8,0},{9,29... | collective-permute-start | bytes 196616 | tf_op jit(solution)/shard_map/ppermute | solution.py:501
  77.9 5.7 %collective-permute-start.20 = (bf16[2,128,128]{2,1,0:T(8,128)(2,1)S(1)}, bf16[2,128,128]{2,1,0:T(8,128)(2,1)S(1)}, u32[]{:S(2)}, u32[]{:S(2)}) collective-permute-start(bf16[2,128,128]{2,1,0:T(8,128)(2,1)S(1)} %get-tuple-element.93), channel_id=1, source_target_pairs={{0,4},{1,17},{2,6},{3,19},{4,0},{5,21},{6,2},{7,23},{8,12},{9,25},... | collective-permute-start | bytes 196616 | tf_op jit(solution)/shard_map/ppermute | solution.py:501
  85.0 12.5 %collective-permute-start.21 = (bf16[1536,128]{1,0:T(8,128)(2,1)S(1)}, bf16[1536,128]{1,0:T(8,128)(2,1)S(1)}, u32[]{:S(2)}, u32[]{:S(2)}) collective-permute-start(bf16[1536,128]{1,0:T(8,128)(2,1)S(1)} %get-tuple-element.105), channel_id=1, source_target_pairs={{0,2},{1,3},{2,0},{3,1},{4,6},{5,7},{6,4},{7,5},{8,10},{9,11},{10,... | collective-permute-start | bytes 1179656 | tf_op jit(solution)/shard_map/ppermute | solution.py:480
  86.5 5.8 %collective-permute-start.22 = (bf16[64,256]{1,0:T(8,128)(2,1)S(1)}, bf16[64,256]{1,0:T(8,128)(2,1)S(1)}, u32[]{:S(2)}, u32[]{:S(2)}) collective-permute-start(bf16[64,256]{1,0:T(8,128)(2,1)S(1)} %get-tuple-element.107), channel_id=1, source_target_pairs={{0,24},{1,9},{2,26},{3,11},{4,28},{5,13},{6,30},{7,15},{8,16},{9,1... | collective-permute-start | bytes 98312 | tf_op jit(solution)/shard_map/ppermute | solution.py:501
  87.8 5.3 %collective-permute-start.23 = (bf16[64,256]{1,0:T(8,128)(2,1)S(1)}, bf16[64,256]{1,0:T(8,128)(2,1)S(1)}, u32[]{:S(2)}, u32[]{:S(2)}) collective-permute-start(bf16[64,256]{1,0:T(8,128)(2,1)S(1)} %get-tuple-element.108), channel_id=1, source_target_pairs={{0,16},{1,17},{2,18},{3,19},{4,20},{5,21},{6,22},{7,23},{8,24},{9,... | collective-permute-start | bytes 98312 | tf_op jit(solution)/shard_map/ppermute | solution.py:501
  87.8 5.4 %collective-permute-start.24 = (bf16[64,256]{1,0:T(8,128)(2,1)S(1)}, bf16[64,256]{1,0:T(8,128)(2,1)S(1)}, u32[]{:S(2)}, u32[]{:S(2)}) collective-permute-start(bf16[64,256]{1,0:T(8,128)(2,1)S(1)} %get-tuple-element.109), channel_id=1, source_target_pairs={{0,8},{1,25},{2,10},{3,27},{4,12},{5,29},{6,14},{7,31},{8,0},{9,17... | collective-permute-start | bytes 98312 | tf_op jit(solution)/shard_map/ppermute | solution.py:501
  97.6 5.7 %collective-permute-start.29 = (bf16[64,256]{1,0:T(8,128)(2,1)S(1)}, bf16[64,256]{1,0:T(8,128)(2,1)S(1)}, u32[]{:S(2)}, u32[]{:S(2)}) collective-permute-start(bf16[64,256]{1,0:T(8,128)(2,1)S(1)} %add_convert_fusion.after_ref.l0), channel_id=1, source_target_pairs={{0,8},{1,25},{2,10},{3,27},{4,12},{5,29},{6,14},{7,31},{8,0},{9,17... | collective-permute-start | bytes 98312 | tf_op jit(solution)/shard_map/ppermute | solution.py:501
  100.3 5.7 %collective-permute-start.27 = (bf16[64,256]{1,0:T(8,128)(2,1)S(1)}, bf16[64,256]{1,0:T(8,128)(2,1)S(1)}, u32[]{:S(2)}, u32[]{:S(2)}) collective-permute-start(bf16[64,256]{1,0:T(8,128)(2,1)S(1)} %add_convert_fusion.after_ref.l0), channel_id=1, source_target_pairs={{0,24},{1,9},{2,26},{3,11},{4,28},{5,13},{6,30},{7,15},{8,16},{9,1... | collective-permute-start | bytes 98312 | tf_op jit(solution)/shard_map/ppermute | solution.py:501
  (13 other events, 48.8 us)

commit v6 on v5

--- a/solution.py
+++ b/solution.py
@@ -69,7 +69,7 @@
     return (node >> shift) & 3
 
 
-PIECE_STEPS = ((0, 3, 2, 1), (0, 1, 2, 3))
+PIECE_STEPS = ((0, 3, 2, 1), (0, 3, 2, 1))
 
 
 def piece_at(group, step, head):

time: 107 us -> 107 us (level)
  no operation moved by 1% of the time
where the time goes in v6:
time: 107 us
  starting transfers between devices  39.5 us (37%)
  Pallas kernels  31.8 us (30%)
  waiting for transfers between devices  21.9 us (20%)
  blocking collectives  12.1 us (11%)
  local copies, waits for them, and re-layouts  1.12 us (1%)
    ppermute x20, starting transfers between devices, exchange_nodes(): moved[step] = lax.ppermute(pieces[step], ('node', 'head'), perm)  31.2 us
    all_to_all x1, blocking collectives, on_device(): lax.all_to_all(wanted.reshape(node_count, 1, CAP), 'node', split_axis=0,...  12.1 us
    ppermute x20, waiting for transfers between devices, exchange_nodes(): moved[step] = lax.ppermute(pieces[step], ('node', 'head'), perm)  11.3 us
    pallas_call x1, Pallas kernels, on_device(): call(functools.partial(backward_kernel, node_count), 'backward', [((BLK,...  11 us
    ppermute x10, waiting for transfers between devices, swap(): return lax.ppermute(value, axis, [(i, i ^ mask) for i in range(size)])  10.6 us
    ppermute x10, starting transfers between devices, swap(): return lax.ppermute(value, axis, [(i, i ^ mask) for i in range(size)])  8.25 us
    pallas_call x1, Pallas kernels, on_device(): call(functools.partial(early_forward_kernel, node_count), 'early_forward'...  4.67 us
    pallas_call x1, Pallas kernels, on_device(): call(late_forward_kernel, 'late_forward', [half_att, ((HD, node_rows), BF...  4.49 us
  transfers between devices with their start and end apart: 30, of which 13 were waited for; matrix products, arithmetic and copies ran while one was open for 0% of the time, Pallas kernels for 9%

profile of v6, /device:TPU:0, one launch (start us, length us, event | category | flops | bytes accessed | tf_op | source)
XLA Modules:
  0.0 107.3 jit_solution(10988797649329569506)
XLA Ops:
  0.6 3.0 %collective-permute-start = (bf16[512,256]{1,0:T(8,128)(2,1)}, bf16[512,256]{1,0:T(8,128)(2,1)S(1)}, u32[]{:S(2)}, u32[]{:S(2)}) collective-permute-start(bf16[512,256]{1,0:T(8,128)(2,1)} %refs_0_.2), channel_id=1, source_target_pairs={{0,2},{1,3},{2,0},{3,1},{4,6},{5,7},{6,4},{7,5},{8,10},{9,11},{10,... | collective-permute-start | bytes 786440 | tf_op jit(solution)/shard_map/ppermute | solution.py:480
  3.7 12.1 %all_to_all.5.refs_2_.wanted_ref = s32[8,1,2]{2,1,0:T(1,128)S(1)} all-to-all(s32[8,1,2]{2,1,0:T(1,128)S(1)} %copy.11), channel_id=1, replica_groups=mesh['node'=8,'head'=4] {'node'}, dimensions={0} | all-to-all | bytes 128 | tf_op jit(solution)/shard_map/all_to_all | solution.py:536
  20.7 3.2 %collective-permute-start.4 = (bf16[2,128,128]{2,1,0:T(8,128)(2,1)S(1)}, bf16[2,128,128]{2,1,0:T(8,128)(2,1)S(1)}, u32[]{:S(2)}, u32[]{:S(2)}) collective-permute-start(bf16[2,128,128]{2,1,0:T(8,128)(2,1)S(1)} %get-tuple-element.65), channel_id=1, source_target_pairs={{0,24},{1,9},{2,26},{3,11},{4,28},{5,13},{6,30},{7,15},{8,16},{9,1... | collective-permute-start | bytes 196616 | tf_op jit(solution)/shard_map/ppermute | solution.py:501
  24.0 3.8 %collective-permute-start.6 = (bf16[2,128,128]{2,1,0:T(8,128)(2,1)S(1)}, bf16[2,128,128]{2,1,0:T(8,128)(2,1)S(1)}, u32[]{:S(2)}, u32[]{:S(2)}) collective-permute-start(bf16[2,128,128]{2,1,0:T(8,128)(2,1)S(1)} %get-tuple-element.67), channel_id=1, source_target_pairs={{0,16},{1,29},{2,18},{3,31},{4,20},{5,25},{6,22},{7,27},{8,24},{9,... | collective-permute-start | bytes 196616 | tf_op jit(solution)/shard_map/ppermute | solution.py:501
  27.8 2.0 %collective-permute-start.8 = (bf16[2,128,128]{2,1,0:T(8,128)(2,1)S(1)}, bf16[2,128,128]{2,1,0:T(8,128)(2,1)S(1)}, u32[]{:S(2)}, u32[]{:S(2)}) collective-permute-start(bf16[2,128,128]{2,1,0:T(8,128)(2,1)S(1)} %get-tuple-element.69), channel_id=1, source_target_pairs={{0,8},{1,21},{2,10},{3,23},{4,12},{5,17},{6,14},{7,19},{8,0},{9,29... | collective-permute-start | bytes 196616 | tf_op jit(solution)/shard_map/ppermute | solution.py:501
  29.8 1.5 %collective-permute-start.9 = (bf16[2,128,128]{2,1,0:T(8,128)(2,1)S(1)}, bf16[2,128,128]{2,1,0:T(8,128)(2,1)S(1)}, u32[]{:S(2)}, u32[]{:S(2)}) collective-permute-start(bf16[2,128,128]{2,1,0:T(8,128)(2,1)S(1)} %get-tuple-element.70), channel_id=1, source_target_pairs={{0,4},{1,17},{2,6},{3,19},{4,0},{5,21},{6,2},{7,23},{8,12},{9,25},... | collective-permute-start | bytes 196616 | tf_op jit(solution)/shard_map/ppermute | solution.py:501
  32.8 2.2 %collective-permute-done.6.refs_4_ = bf16[2,128,128]{2,1,0:T(8,128)(2,1)S(1)} collective-permute-done((bf16[2,128,128]{2,1,0:T(8,128)(2,1)S(1)}, bf16[2,128,128]{2,1,0:T(8,128)(2,1)S(1)}, u32[]{:S(2)}, u32[]{:S(2)}) %collective-permute-start.6) | collective-permute-done | bytes 65568 | tf_op jit(solution)/shard_map/ppermute | solution.py:501
  35.1 4.7 %early_forward.1 = (bf16[512,128]{1,0:T(8,128)(2,1)S(1)}, bf16[64,1024]{1,0:T(8,128)(2,1)S(1)}, bf16[32,128,128]{2,1,0:T(8,128)(2,1)S(1)}, bf16[32,128,128]{2,1,...) custom-call(s32[2]{0:T(128)S(1)} %pad_add_fusion.place_ref, s32[16,12]{1,0:T(8,128)S(1)} %copy-done.3, ...), custom_call_target="tpu_custom_call" | custom-call | flops 805306368 | bytes 4194304 | tf_op jit(solution)/shard_map/early_forward/pallas_call | solution.py:560
  40.4 4.5 %late_forward.1 = (bf16[512,128]{1,0:T(8,128)(2,1)S(1)}, bf16[64,2048]{1,0:T(8,128)(2,1)S(1)}, f32[16,8,128]{2,1,0:T(8,128)S(1)}, f32[16,8,128]{2,1,0:T(8,128)S(1)}) custom-call(s32[16,12]{1,0:T(8,128)S(1)} %copy-done.3, s32[16]{0:T(128)S(1)} %copy-done.4, bf16[2048,128]{1,0:T(8,128)(2,1)S(1)} %get-tuple-element.60.qz_ref, ...), custom_call_target="tpu_custom_call" | custom-call | flops 805306368 | bytes 4194304 | tf_op jit(solution)/shard_map/late_forward/pallas_call | solution.py:577
  44.9 1.5 %collective-permute-start.12 = (bf16[512,128]{1,0:T(8,128)(2,1)S(1)}, bf16[512,128]{1,0:T(8,128)(2,1)S(1)}, u32[]{:S(2)}, u32[]{:S(2)}) collective-permute-start(bf16[512,128]{1,0:T(8,128)(2,1)S(1)} %get-tuple-element.78.refs_1_), channel_id=1, source_target_pairs={{0,2},{1,3},{2,0},{3,1},{4,6},{5,7},{6,4},{7,5},{8,10},{9,11},{10,... | collective-permute-start | bytes 393224 | tf_op jit(solution)/shard_map/ppermute | solution.py:480
  46.5 3.8 %collective-permute-done.12.refs_3_ = bf16[512,128]{1,0:T(8,128)(2,1)S(1)} collective-permute-done((bf16[512,128]{1,0:T(8,128)(2,1)S(1)}, bf16[512,128]{1,0:T(8,128)(2,1)S(1)}, u32[]{:S(2)}, u32[]{:S(2)}) %collective-permute-start.12) | collective-permute-done | bytes 131104 | tf_op jit(solution)/shard_map/ppermute | solution.py:480
  50.5 1.9 %collective-permute-done.13.a_other = bf16[2048,128]{1,0:T(8,128)(2,1)S(1)} collective-permute-done((bf16[2048,128]{1,0:T(8,128)(2,1)S(1)}, bf16[2048,128]{1,0:T(8,128)(2,1)S(1)}, u32[]{:S(2)}, u32[]{:S(2)}) %collective-permute-start.13) | collective-permute-done | bytes 524320 | tf_op jit(solution)/shard_map/ppermute | solution.py:480
  52.4 4.0 %middle.1 = (bf16[512,256]{1,0:T(8,128)(2,1)}, f32[512,256]{1,0:T(8,128)S(1)}, bf16[2048,128]{1,0:T(8,128)(2,1)S(1)}, f32[16,8,128]{2,1,0:T(8,128)S(1)}, bf16[2048,256]{1,0:T(8,128)(2,1)S(1)}) custom-call(s32[2]{0:T(128)S(1)} %pad_add_fusion.place_ref, bf16[1024,256]{1,0:T(8,128)(2,1)S(1)} %pair.3.pair_ref.x_pair, ...), custom_call_target="tpu_custom_call" | custom-call | flops 1073741824 | bytes 4194304 | tf_op jit(solution)/shard_map/middle/pallas_call | solution.py:594
  56.4 11.0 %backward.1 = (f32[16,128,128]{2,1,0:T(8,128)S(1)}, bf16[64,2048]{1,0:T(8,128)(2,1)S(1)}, bf16[256,128]{1,0:T(8,128)(2,1)S(1)}, bf16[256,128]{1,0:T(8,128)(2,1)S...) custom-call(s32[2]{0:T(128)S(1)} %pad_add_fusion.place_ref, ...), custom_call_target="tpu_custom_call" | custom-call | flops 4026531840 | bytes 4194304 | tf_op jit(solution)/shard_map/backward/pallas_call | solution.py:615
  67.4 2.2 %collective-permute-start.14 = (bf16[2,128,128]{2,1,0:T(8,128)(2,1)S(1)}, bf16[2,128,128]{2,1,0:T(8,128)(2,1)S(1)}, u32[]{:S(2)}, u32[]{:S(2)}) collective-permute-start(bf16[2,128,128]{2,1,0:T(8,128)(2,1)S(1)} %get-tuple-element.87), channel_id=1, source_target_pairs={{0,28},{1,13},{2,30},{3,15},{4,24},{5,9},{6,26},{7,11},{8,20},{9,5... | collective-permute-start | bytes 196616 | tf_op jit(solution)/shard_map/ppermute | solution.py:501
  69.6 2.4 %collective-permute-start.15 = (bf16[2,128,128]{2,1,0:T(8,128)(2,1)S(1)}, bf16[2,128,128]{2,1,0:T(8,128)(2,1)S(1)}, u32[]{:S(2)}, u32[]{:S(2)}) collective-permute-start(bf16[2,128,128]{2,1,0:T(8,128)(2,1)S(1)} %get-tuple-element.88), channel_id=1, source_target_pairs={{0,24},{1,9},{2,26},{3,11},{4,28},{5,13},{6,30},{7,15},{8,16},{9,1... | collective-permute-start | bytes 196616 | tf_op jit(solution)/shard_map/ppermute | solution.py:501
  72.0 3.1 %collective-permute-start.17 = (bf16[2,128,128]{2,1,0:T(8,128)(2,1)S(1)}, bf16[2,128,128]{2,1,0:T(8,128)(2,1)S(1)}, u32[]{:S(2)}, u32[]{:S(2)}) collective-permute-start(bf16[2,128,128]{2,1,0:T(8,128)(2,1)S(1)} %get-tuple-element.90), channel_id=1, source_target_pairs={{0,16},{1,29},{2,18},{3,31},{4,20},{5,25},{6,22},{7,27},{8,24},{9,... | collective-permute-start | bytes 196616 | tf_op jit(solution)/shard_map/ppermute | solution.py:501
  75.1 2.7 %collective-permute-start.19 = (bf16[2,128,128]{2,1,0:T(8,128)(2,1)S(1)}, bf16[2,128,128]{2,1,0:T(8,128)(2,1)S(1)}, u32[]{:S(2)}, u32[]{:S(2)}) collective-permute-start(bf16[2,128,128]{2,1,0:T(8,128)(2,1)S(1)} %get-tuple-element.92), channel_id=1, source_target_pairs={{0,8},{1,21},{2,10},{3,23},{4,12},{5,17},{6,14},{7,19},{8,0},{9,29... | collective-permute-start | bytes 196616 | tf_op jit(solution)/shard_map/ppermute | solution.py:501
  79.7 2.2 %collective-permute-done.16.refs_3_ = bf16[2,128,128]{2,1,0:T(8,128)(2,1)S(1)} collective-permute-done((bf16[2,128,128]{2,1,0:T(8,128)(2,1)S(1)}, bf16[2,128,128]{2,1,0:T(8,128)(2,1)S(1)}, u32[]{:S(2)}, u32[]{:S(2)}) %collective-permute-start.16) | collective-permute-done | bytes 65568 | tf_op jit(solution)/shard_map/ppermute | solution.py:501
  85.0 1.5 %collective-permute-start.21 = (bf16[1536,128]{1,0:T(8,128)(2,1)S(1)}, bf16[1536,128]{1,0:T(8,128)(2,1)S(1)}, u32[]{:S(2)}, u32[]{:S(2)}) collective-permute-start(bf16[1536,128]{1,0:T(8,128)(2,1)S(1)} %get-tuple-element.105), channel_id=1, source_target_pairs={{0,2},{1,3},{2,0},{3,1},{4,6},{5,7},{6,4},{7,5},{8,10},{9,11},{10,... | collective-permute-start | bytes 1179656 | tf_op jit(solution)/shard_map/ppermute | solution.py:480
  87.8 3.1 %collective-permute-start.24 = (bf16[64,256]{1,0:T(8,128)(2,1)S(1)}, bf16[64,256]{1,0:T(8,128)(2,1)S(1)}, u32[]{:S(2)}, u32[]{:S(2)}) collective-permute-start(bf16[64,256]{1,0:T(8,128)(2,1)S(1)} %get-tuple-element.109), channel_id=1, source_target_pairs={{0,8},{1,9},{2,10},{3,11},{4,12},{5,13},{6,14},{7,15},{8,0},{9,1},... | collective-permute-start | bytes 98312 | tf_op jit(solution)/shard_map/ppermute | solution.py:501
  93.8 3.7 %collective-permute-done.25 = f32[64,256]{1,0:T(8,128)S(1)} collective-permute-done((f32[64,256]{1,0:T(8,128)S(1)}, f32[64,256]{1,0:T(8,128)S(1)}, u32[]{:S(2)}, u32[]{:S(2)}) %collective-permute-start.25) | collective-permute-done | bytes 65568 | tf_op jit(solution)/shard_map/ppermute | solution.py:480
  97.6 1.8 %collective-permute-start.29 = (bf16[64,256]{1,0:T(8,128)(2,1)S(1)}, bf16[64,256]{1,0:T(8,128)(2,1)S(1)}, u32[]{:S(2)}, u32[]{:S(2)}) collective-permute-start(bf16[64,256]{1,0:T(8,128)(2,1)S(1)} %add_convert_fusion.after_ref.l0), channel_id=1, source_target_pairs={{0,8},{1,9},{2,10},{3,11},{4,12},{5,13},{6,14},{7,15},{8,0},{9,1},... | collective-permute-start | bytes 98312 | tf_op jit(solution)/shard_map/ppermute | solution.py:501
  100.3 1.8 %collective-permute-start.27 = (bf16[64,256]{1,0:T(8,128)(2,1)S(1)}, bf16[64,256]{1,0:T(8,128)(2,1)S(1)}, u32[]{:S(2)}, u32[]{:S(2)}) collective-permute-start(bf16[64,256]{1,0:T(8,128)(2,1)S(1)} %add_convert_fusion.after_ref.l0), channel_id=1, source_target_pairs={{0,24},{1,25},{2,26},{3,27},{4,28},{5,29},{6,30},{7,31},{8,16},{9,... | collective-permute-start | bytes 98312 | tf_op jit(solution)/shard_map/ppermute | solution.py:501
  (69 shorter events, 22.8 us)
Async XLA Ops:
  0.6 15.2 %collective-permute-start = (bf16[512,256]{1,0:T(8,128)(2,1)}, bf16[512,256]{1,0:T(8,128)(2,1)S(1)}, u32[]{:S(2)}, u32[]{:S(2)}) collective-permute-start(bf16[512,256]{1,0:T(8,128)(2,1)} %refs_0_.2), channel_id=1, source_target_pairs={{0,2},{1,3},{2,0},{3,1},{4,6},{5,7},{6,4},{7,5},{8,10},{9,11},{10,... | collective-permute-start | bytes 786440 | tf_op jit(solution)/shard_map/ppermute | solution.py:480
  17.0 10.8 %collective-permute-start.2 = (bf16[512,256]{1,0:T(8,128)(2,1)S(1)}, bf16[512,256]{1,0:T(8,128)(2,1)S(1)}, u32[]{:S(2)}, u32[]{:S(2)}) collective-permute-start(bf16[512,256]{1,0:T(8,128)(2,1)S(1)} %copy-done.1), channel_id=1, source_target_pairs={{0,2},{1,3},{2,0},{3,1},{4,6},{5,7},{6,4},{7,5},{8,10},{9,11},{10,... | collective-permute-start | bytes 786440 | tf_op jit(solution)/shard_map/ppermute | solution.py:480
  20.1 7.7 %collective-permute-start.3 = (bf16[2,128,128]{2,1,0:T(8,128)(2,1)S(1)}, bf16[2,128,128]{2,1,0:T(8,128)(2,1)S(1)}, u32[]{:S(2)}, u32[]{:S(2)}) collective-permute-start(bf16[2,128,128]{2,1,0:T(8,128)(2,1)S(1)} %get-tuple-element.64), channel_id=1, source_target_pairs={{0,28},{1,13},{2,30},{3,15},{4,24},{5,9},{6,26},{7,11},{8,20},{9,5... | collective-permute-start | bytes 196616 | tf_op jit(solution)/shard_map/ppermute | solution.py:501
  20.7 9.1 %collective-permute-start.4 = (bf16[2,128,128]{2,1,0:T(8,128)(2,1)S(1)}, bf16[2,128,128]{2,1,0:T(8,128)(2,1)S(1)}, u32[]{:S(2)}, u32[]{:S(2)}) collective-permute-start(bf16[2,128,128]{2,1,0:T(8,128)(2,1)S(1)} %get-tuple-element.65), channel_id=1, source_target_pairs={{0,24},{1,9},{2,26},{3,11},{4,28},{5,13},{6,30},{7,15},{8,16},{9,1... | collective-permute-start | bytes 196616 | tf_op jit(solution)/shard_map/ppermute | solution.py:501
  24.0 8.9 %collective-permute-start.5 = (bf16[2,128,128]{2,1,0:T(8,128)(2,1)S(1)}, bf16[2,128,128]{2,1,0:T(8,128)(2,1)S(1)}, u32[]{:S(2)}, u32[]{:S(2)}) collective-permute-start(bf16[2,128,128]{2,1,0:T(8,128)(2,1)S(1)} %get-tuple-element.66), channel_id=1, source_target_pairs={{0,20},{1,5},{2,22},{3,7},{4,16},{5,1},{6,18},{7,3},{8,28},{9,13},... | collective-permute-start | bytes 196616 | tf_op jit(solution)/shard_map/ppermute | solution.py:501
  24.0 11.1 %collective-permute-start.6 = (bf16[2,128,128]{2,1,0:T(8,128)(2,1)S(1)}, bf16[2,128,128]{2,1,0:T(8,128)(2,1)S(1)}, u32[]{:S(2)}, u32[]{:S(2)}) collective-permute-start(bf16[2,128,128]{2,1,0:T(8,128)(2,1)S(1)} %get-tuple-element.67), channel_id=1, source_target_pairs={{0,16},{1,29},{2,18},{3,31},{4,20},{5,25},{6,22},{7,27},{8,24},{9,... | collective-permute-start | bytes 196616 | tf_op jit(solution)/shard_map/ppermute | solution.py:501
  27.8 7.3 %collective-permute-start.7 = (bf16[2,128,128]{2,1,0:T(8,128)(2,1)S(1)}, bf16[2,128,128]{2,1,0:T(8,128)(2,1)S(1)}, u32[]{:S(2)}, u32[]{:S(2)}) collective-permute-start(bf16[2,128,128]{2,1,0:T(8,128)(2,1)S(1)} %get-tuple-element.68), channel_id=1, source_target_pairs={{0,12},{1,25},{2,14},{3,27},{4,8},{5,29},{6,10},{7,31},{8,4},{9,17... | collective-permute-start | bytes 196616 | tf_op jit(solution)/shard_map/ppermute | solution.py:501
  27.8 7.2 %collective-permute-start.8 = (bf16[2,128,128]{2,1,0:T(8,128)(2,1)S(1)}, bf16[2,128,128]{2,1,0:T(8,128)(2,1)S(1)}, u32[]{:S(2)}, u32[]{:S(2)}) collective-permute-start(bf16[2,128,128]{2,1,0:T(8,128)(2,1)S(1)} %get-tuple-element.69), channel_id=1, source_target_pairs={{0,8},{1,21},{2,10},{3,23},{4,12},{5,17},{6,14},{7,19},{8,0},{9,29... | collective-permute-start | bytes 196616 | tf_op jit(solution)/shard_map/ppermute | solution.py:501
  29.8 5.2 %collective-permute-start.9 = (bf16[2,128,128]{2,1,0:T(8,128)(2,1)S(1)}, bf16[2,128,128]{2,1,0:T(8,128)(2,1)S(1)}, u32[]{:S(2)}, u32[]{:S(2)}) collective-permute-start(bf16[2,128,128]{2,1,0:T(8,128)(2,1)S(1)} %get-tuple-element.70), channel_id=1, source_target_pairs={{0,4},{1,17},{2,6},{3,19},{4,0},{5,21},{6,2},{7,23},{8,12},{9,25},... | collective-permute-start | bytes 196616 | tf_op jit(solution)/shard_map/ppermute | solution.py:501
  39.8 6.8 %collective-permute-start.11 = (bf16[512,128]{1,0:T(8,128)(2,1)S(1)}, bf16[512,128]{1,0:T(8,128)(2,1)S(1)}, u32[]{:S(2)}, u32[]{:S(2)}) collective-permute-start(bf16[512,128]{1,0:T(8,128)(2,1)S(1)} %get-tuple-element.77.refs_0_), channel_id=1, source_target_pairs={{0,2},{1,3},{2,0},{3,1},{4,6},{5,7},{6,4},{7,5},{8,10},{9,11},{10,... | collective-permute-start | bytes 393224 | tf_op jit(solution)/shard_map/ppermute | solution.py:480
  44.9 5.5 %collective-permute-start.12 = (bf16[512,128]{1,0:T(8,128)(2,1)S(1)}, bf16[512,128]{1,0:T(8,128)(2,1)S(1)}, u32[]{:S(2)}, u32[]{:S(2)}) collective-permute-start(bf16[512,128]{1,0:T(8,128)(2,1)S(1)} %get-tuple-element.78.refs_1_), channel_id=1, source_target_pairs={{0,2},{1,3},{2,0},{3,1},{4,6},{5,7},{6,4},{7,5},{8,10},{9,11},{10,... | collective-permute-start | bytes 393224 | tf_op jit(solution)/shard_map/ppermute | solution.py:480
  67.4 7.7 %collective-permute-start.14 = (bf16[2,128,128]{2,1,0:T(8,128)(2,1)S(1)}, bf16[2,128,128]{2,1,0:T(8,128)(2,1)S(1)}, u32[]{:S(2)}, u32[]{:S(2)}) collective-permute-start(bf16[2,128,128]{2,1,0:T(8,128)(2,1)S(1)} %get-tuple-element.87), channel_id=1, source_target_pairs={{0,28},{1,13},{2,30},{3,15},{4,24},{5,9},{6,26},{7,11},{8,20},{9,5... | collective-permute-start | bytes 196616 | tf_op jit(solution)/shard_map/ppermute | solution.py:501
  69.6 8.3 %collective-permute-start.15 = (bf16[2,128,128]{2,1,0:T(8,128)(2,1)S(1)}, bf16[2,128,128]{2,1,0:T(8,128)(2,1)S(1)}, u32[]{:S(2)}, u32[]{:S(2)}) collective-permute-start(bf16[2,128,128]{2,1,0:T(8,128)(2,1)S(1)} %get-tuple-element.88), channel_id=1, source_target_pairs={{0,24},{1,9},{2,26},{3,11},{4,28},{5,13},{6,30},{7,15},{8,16},{9,1... | collective-permute-start | bytes 196616 | tf_op jit(solution)/shard_map/ppermute | solution.py:501
  72.0 9.9 %collective-permute-start.16 = (bf16[2,128,128]{2,1,0:T(8,128)(2,1)S(1)}, bf16[2,128,128]{2,1,0:T(8,128)(2,1)S(1)}, u32[]{:S(2)}, u32[]{:S(2)}) collective-permute-start(bf16[2,128,128]{2,1,0:T(8,128)(2,1)S(1)} %get-tuple-element.89), channel_id=1, source_target_pairs={{0,20},{1,5},{2,22},{3,7},{4,16},{5,1},{6,18},{7,3},{8,28},{9,13},... | collective-permute-start | bytes 196616 | tf_op jit(solution)/shard_map/ppermute | solution.py:501
  72.0 10.9 %collective-permute-start.17 = (bf16[2,128,128]{2,1,0:T(8,128)(2,1)S(1)}, bf16[2,128,128]{2,1,0:T(8,128)(2,1)S(1)}, u32[]{:S(2)}, u32[]{:S(2)}) collective-permute-start(bf16[2,128,128]{2,1,0:T(8,128)(2,1)S(1)} %get-tuple-element.90), channel_id=1, source_target_pairs={{0,16},{1,29},{2,18},{3,31},{4,20},{5,25},{6,22},{7,27},{8,24},{9,... | collective-permute-start | bytes 196616 | tf_op jit(solution)/shard_map/ppermute | solution.py:501
  75.1 7.8 %collective-permute-start.18 = (bf16[2,128,128]{2,1,0:T(8,128)(2,1)S(1)}, bf16[2,128,128]{2,1,0:T(8,128)(2,1)S(1)}, u32[]{:S(2)}, u32[]{:S(2)}) collective-permute-start(bf16[2,128,128]{2,1,0:T(8,128)(2,1)S(1)} %get-tuple-element.91), channel_id=1, source_target_pairs={{0,12},{1,25},{2,14},{3,27},{4,8},{5,29},{6,10},{7,31},{8,4},{9,17... | collective-permute-start | bytes 196616 | tf_op jit(solution)/shard_map/ppermute | solution.py:501
  75.1 8.5 %collective-permute-start.19 = (bf16[2,128,128]{2,1,0:T(8,128)(2,1)S(1)}, bf16[2,128,128]{2,1,0:T(8,128)(2,1)S(1)}, u32[]{:S(2)}, u32[]{:S(2)}) collective-permute-start(bf16[2,128,128]{2,1,0:T(8,128)(2,1)S(1)} %get-tuple-element.92), channel_id=1, source_target_pairs={{0,8},{1,21},{2,10},{3,23},{4,12},{5,17},{6,14},{7,19},{8,0},{9,29... | collective-permute-start | bytes 196616 | tf_op jit(solution)/shard_map/ppermute | solution.py:501
  77.9 5.7 %collective-permute-start.20 = (bf16[2,128,128]{2,1,0:T(8,128)(2,1)S(1)}, bf16[2,128,128]{2,1,0:T(8,128)(2,1)S(1)}, u32[]{:S(2)}, u32[]{:S(2)}) collective-permute-start(bf16[2,128,128]{2,1,0:T(8,128)(2,1)S(1)} %get-tuple-element.93), channel_id=1, source_target_pairs={{0,4},{1,17},{2,6},{3,19},{4,0},{5,21},{6,2},{7,23},{8,12},{9,25},... | collective-permute-start | bytes 196616 | tf_op jit(solution)/shard_map/ppermute | solution.py:501
  85.0 12.5 %collective-permute-start.21 = (bf16[1536,128]{1,0:T(8,128)(2,1)S(1)}, bf16[1536,128]{1,0:T(8,128)(2,1)S(1)}, u32[]{:S(2)}, u32[]{:S(2)}) collective-permute-start(bf16[1536,128]{1,0:T(8,128)(2,1)S(1)} %get-tuple-element.105), channel_id=1, source_target_pairs={{0,2},{1,3},{2,0},{3,1},{4,6},{5,7},{6,4},{7,5},{8,10},{9,11},{10,... | collective-permute-start | bytes 1179656 | tf_op jit(solution)/shard_map/ppermute | solution.py:480
  86.5 5.8 %collective-permute-start.22 = (bf16[64,256]{1,0:T(8,128)(2,1)S(1)}, bf16[64,256]{1,0:T(8,128)(2,1)S(1)}, u32[]{:S(2)}, u32[]{:S(2)}) collective-permute-start(bf16[64,256]{1,0:T(8,128)(2,1)S(1)} %get-tuple-element.107), channel_id=1, source_target_pairs={{0,24},{1,25},{2,26},{3,27},{4,28},{5,29},{6,30},{7,31},{8,16},{9,... | collective-permute-start | bytes 98312 | tf_op jit(solution)/shard_map/ppermute | solution.py:501
  87.8 5.3 %collective-permute-start.23 = (bf16[64,256]{1,0:T(8,128)(2,1)S(1)}, bf16[64,256]{1,0:T(8,128)(2,1)S(1)}, u32[]{:S(2)}, u32[]{:S(2)}) collective-permute-start(bf16[64,256]{1,0:T(8,128)(2,1)S(1)} %get-tuple-element.108), channel_id=1, source_target_pairs={{0,16},{1,17},{2,18},{3,19},{4,20},{5,21},{6,22},{7,23},{8,24},{9,... | collective-permute-start | bytes 98312 | tf_op jit(solution)/shard_map/ppermute | solution.py:501
  87.8 5.4 %collective-permute-start.24 = (bf16[64,256]{1,0:T(8,128)(2,1)S(1)}, bf16[64,256]{1,0:T(8,128)(2,1)S(1)}, u32[]{:S(2)}, u32[]{:S(2)}) collective-permute-start(bf16[64,256]{1,0:T(8,128)(2,1)S(1)} %get-tuple-element.109), channel_id=1, source_target_pairs={{0,8},{1,9},{2,10},{3,11},{4,12},{5,13},{6,14},{7,15},{8,0},{9,1},... | collective-permute-start | bytes 98312 | tf_op jit(solution)/shard_map/ppermute | solution.py:501
  97.6 5.7 %collective-permute-start.29 = (bf16[64,256]{1,0:T(8,128)(2,1)S(1)}, bf16[64,256]{1,0:T(8,128)(2,1)S(1)}, u32[]{:S(2)}, u32[]{:S(2)}) collective-permute-start(bf16[64,256]{1,0:T(8,128)(2,1)S(1)} %add_convert_fusion.after_ref.l0), channel_id=1, source_target_pairs={{0,8},{1,9},{2,10},{3,11},{4,12},{5,13},{6,14},{7,15},{8,0},{9,1},... | collective-permute-start | bytes 98312 | tf_op jit(solution)/shard_map/ppermute | solution.py:501
  100.3 5.7 %collective-permute-start.27 = (bf16[64,256]{1,0:T(8,128)(2,1)S(1)}, bf16[64,256]{1,0:T(8,128)(2,1)S(1)}, u32[]{:S(2)}, u32[]{:S(2)}) collective-permute-start(bf16[64,256]{1,0:T(8,128)(2,1)S(1)} %add_convert_fusion.after_ref.l0), channel_id=1, source_target_pairs={{0,24},{1,25},{2,26},{3,27},{4,28},{5,29},{6,30},{7,31},{8,16},{9,... | collective-permute-start | bytes 98312 | tf_op jit(solution)/shard_map/ppermute | solution.py:501
  (13 other events, 49.0 us)

commit v7 on v6

--- a/solution.py
+++ b/solution.py
@@ -108,7 +108,7 @@
     out_ref[...] = ((values[0] + values[1]) + (values[2] + values[3])) * factor
 
 
-def result_kernel(shift, place_ref, l0, l1, l2, l3, after_ref, in_ref, out_ref):
+def result_kernel(shift, place_ref, l0, l3, l2, l1, after_ref, in_ref, out_ref):
     head, group = place_ref[0], group_of(place_ref[1], shift)
     for step, piece_ref in enumerate((l0, l1, l2, l3)):
         at = piece_at(group, step, head)
@@ -672,7 +672,7 @@
         [((3 * HD, D), F32), ((HD, D), F32)],
         [smem()] + [vmem()] * 5,
         limit,
-    )(place, *late, finished)
+    )(place, late[0], *late[:0:-1], finished)
     return (output, feature_grad, in_grad.T, out_grad)
 
 

time: 107 us -> 107 us (level)
  transfers between devices with their start and end apart: 30 -> 30, of which waited for: 13 -> 14; matrix products, arithmetic and copies ran while one was open for 0% -> 0% of each run, Pallas kernels for 9% -> 9%
where the time goes in v7:
time: 107 us; the launch traced here: 106 us
  starting transfers between devices  39.5 us (37%)
  Pallas kernels  31.7 us (30%)
  waiting for transfers between devices  21.1 us (20%)
  blocking collectives  12.1 us (11%)
  local copies, waits for them, and re-layouts  1.12 us (1%)
    ppermute x20, starting transfers between devices, exchange_nodes(): moved[step] = lax.ppermute(pieces[step], ('node', 'head'), perm)  31.2 us
    all_to_all x1, blocking collectives, on_device(): lax.all_to_all(wanted.reshape(node_count, 1, CAP), 'node', split_axis=0,...  12.1 us
    pallas_call x1, Pallas kernels, on_device(): call(functools.partial(backward_kernel, node_count), 'backward', [((BLK,...  11 us
    ppermute x10, waiting for transfers between devices, swap(): return lax.ppermute(value, axis, [(i, i ^ mask) for i in range(size)])  10.6 us
    ppermute x20, waiting for transfers between devices, exchange_nodes(): moved[step] = lax.ppermute(pieces[step], ('node', 'head'), perm)  10.5 us
    ppermute x10, starting transfers between devices, swap(): return lax.ppermute(value, axis, [(i, i ^ mask) for i in range(size)])  8.26 us
    pallas_call x1, Pallas kernels, on_device(): call(functools.partial(early_forward_kernel, node_count), 'early_forward'...  4.67 us
    pallas_call x1, Pallas kernels, on_device(): call(late_forward_kernel, 'late_forward', [half_att, ((HD, node_rows), BF...  4.49 us
  transfers between devices with their start and end apart: 30, of which 14 were waited for; matrix products, arithmetic and copies ran while one was open for 0% of the time, Pallas kernels for 9%

profile of v7, /device:TPU:0, one launch (start us, length us, event | category | flops | bytes accessed | tf_op | source)
XLA Modules:
  0.0 106.5 jit_solution(7719843456460257453)
XLA Ops:
  0.6 3.0 %collective-permute-start = (bf16[512,256]{1,0:T(8,128)(2,1)}, bf16[512,256]{1,0:T(8,128)(2,1)S(1)}, u32[]{:S(2)}, u32[]{:S(2)}) collective-permute-start(bf16[512,256]{1,0:T(8,128)(2,1)} %refs_0_.2), channel_id=1, source_target_pairs={{0,2},{1,3},{2,0},{3,1},{4,6},{5,7},{6,4},{7,5},{8,10},{9,11},{10,... | collective-permute-start | bytes 786440 | tf_op jit(solution)/shard_map/ppermute | solution.py:480
  3.7 12.1 %all_to_all.5.refs_2_.wanted_ref = s32[8,1,2]{2,1,0:T(1,128)S(1)} all-to-all(s32[8,1,2]{2,1,0:T(1,128)S(1)} %copy.11), channel_id=1, replica_groups=mesh['node'=8,'head'=4] {'node'}, dimensions={0} | all-to-all | bytes 128 | tf_op jit(solution)/shard_map/all_to_all | solution.py:536
  20.7 3.2 %collective-permute-start.4 = (bf16[2,128,128]{2,1,0:T(8,128)(2,1)S(1)}, bf16[2,128,128]{2,1,0:T(8,128)(2,1)S(1)}, u32[]{:S(2)}, u32[]{:S(2)}) collective-permute-start(bf16[2,128,128]{2,1,0:T(8,128)(2,1)S(1)} %get-tuple-element.65), channel_id=1, source_target_pairs={{0,24},{1,9},{2,26},{3,11},{4,28},{5,13},{6,30},{7,15},{8,16},{9,1... | collective-permute-start | bytes 196616 | tf_op jit(solution)/shard_map/ppermute | solution.py:501
  24.0 3.8 %collective-permute-start.6 = (bf16[2,128,128]{2,1,0:T(8,128)(2,1)S(1)}, bf16[2,128,128]{2,1,0:T(8,128)(2,1)S(1)}, u32[]{:S(2)}, u32[]{:S(2)}) collective-permute-start(bf16[2,128,128]{2,1,0:T(8,128)(2,1)S(1)} %get-tuple-element.67), channel_id=1, source_target_pairs={{0,16},{1,29},{2,18},{3,31},{4,20},{5,25},{6,22},{7,27},{8,24},{9,... | collective-permute-start | bytes 196616 | tf_op jit(solution)/shard_map/ppermute | solution.py:501
  27.8 2.0 %collective-permute-start.8 = (bf16[2,128,128]{2,1,0:T(8,128)(2,1)S(1)}, bf16[2,128,128]{2,1,0:T(8,128)(2,1)S(1)}, u32[]{:S(2)}, u32[]{:S(2)}) collective-permute-start(bf16[2,128,128]{2,1,0:T(8,128)(2,1)S(1)} %get-tuple-element.69), channel_id=1, source_target_pairs={{0,8},{1,21},{2,10},{3,23},{4,12},{5,17},{6,14},{7,19},{8,0},{9,29... | collective-permute-start | bytes 196616 | tf_op jit(solution)/shard_map/ppermute | solution.py:501
  29.8 1.5 %collective-permute-start.9 = (bf16[2,128,128]{2,1,0:T(8,128)(2,1)S(1)}, bf16[2,128,128]{2,1,0:T(8,128)(2,1)S(1)}, u32[]{:S(2)}, u32[]{:S(2)}) collective-permute-start(bf16[2,128,128]{2,1,0:T(8,128)(2,1)S(1)} %get-tuple-element.70), channel_id=1, source_target_pairs={{0,4},{1,17},{2,6},{3,19},{4,0},{5,21},{6,2},{7,23},{8,12},{9,25},... | collective-permute-start | bytes 196616 | tf_op jit(solution)/shard_map/ppermute | solution.py:501
  32.8 2.2 %collective-permute-done.6.refs_4_ = bf16[2,128,128]{2,1,0:T(8,128)(2,1)S(1)} collective-permute-done((bf16[2,128,128]{2,1,0:T(8,128)(2,1)S(1)}, bf16[2,128,128]{2,1,0:T(8,128)(2,1)S(1)}, u32[]{:S(2)}, u32[]{:S(2)}) %collective-permute-start.6) | collective-permute-done | bytes 65568 | tf_op jit(solution)/shard_map/ppermute | solution.py:501
  35.1 4.7 %early_forward.1 = (bf16[512,128]{1,0:T(8,128)(2,1)S(1)}, bf16[64,1024]{1,0:T(8,128)(2,1)S(1)}, bf16[32,128,128]{2,1,0:T(8,128)(2,1)S(1)}, bf16[32,128,128]{2,1,...) custom-call(s32[2]{0:T(128)S(1)} %pad_add_fusion.place_ref, s32[16,12]{1,0:T(8,128)S(1)} %copy-done.3, ...), custom_call_target="tpu_custom_call" | custom-call | flops 805306368 | bytes 4194304 | tf_op jit(solution)/shard_map/early_forward/pallas_call | solution.py:560
  40.4 4.5 %late_forward.1 = (bf16[512,128]{1,0:T(8,128)(2,1)S(1)}, bf16[64,2048]{1,0:T(8,128)(2,1)S(1)}, f32[16,8,128]{2,1,0:T(8,128)S(1)}, f32[16,8,128]{2,1,0:T(8,128)S(1)}) custom-call(s32[16,12]{1,0:T(8,128)S(1)} %copy-done.3, s32[16]{0:T(128)S(1)} %copy-done.4, bf16[2048,128]{1,0:T(8,128)(2,1)S(1)} %get-tuple-element.60.qz_ref, ...), custom_call_target="tpu_custom_call" | custom-call | flops 805306368 | bytes 4194304 | tf_op jit(solution)/shard_map/late_forward/pallas_call | solution.py:577
  44.9 1.5 %collective-permute-start.12 = (bf16[512,128]{1,0:T(8,128)(2,1)S(1)}, bf16[512,128]{1,0:T(8,128)(2,1)S(1)}, u32[]{:S(2)}, u32[]{:S(2)}) collective-permute-start(bf16[512,128]{1,0:T(8,128)(2,1)S(1)} %get-tuple-element.78.refs_1_), channel_id=1, source_target_pairs={{0,2},{1,3},{2,0},{3,1},{4,6},{5,7},{6,4},{7,5},{8,10},{9,11},{10,... | collective-permute-start | bytes 393224 | tf_op jit(solution)/shard_map/ppermute | solution.py:480
  46.5 3.8 %collective-permute-done.12.refs_3_ = bf16[512,128]{1,0:T(8,128)(2,1)S(1)} collective-permute-done((bf16[512,128]{1,0:T(8,128)(2,1)S(1)}, bf16[512,128]{1,0:T(8,128)(2,1)S(1)}, u32[]{:S(2)}, u32[]{:S(2)}) %collective-permute-start.12) | collective-permute-done | bytes 131104 | tf_op jit(solution)/shard_map/ppermute | solution.py:480
  50.5 1.9 %collective-permute-done.13.a_other = bf16[2048,128]{1,0:T(8,128)(2,1)S(1)} collective-permute-done((bf16[2048,128]{1,0:T(8,128)(2,1)S(1)}, bf16[2048,128]{1,0:T(8,128)(2,1)S(1)}, u32[]{:S(2)}, u32[]{:S(2)}) %collective-permute-start.13) | collective-permute-done | bytes 524320 | tf_op jit(solution)/shard_map/ppermute | solution.py:480
  52.4 4.0 %middle.1 = (bf16[512,256]{1,0:T(8,128)(2,1)}, f32[512,256]{1,0:T(8,128)S(1)}, bf16[2048,128]{1,0:T(8,128)(2,1)S(1)}, f32[16,8,128]{2,1,0:T(8,128)S(1)}, bf16[2048,256]{1,0:T(8,128)(2,1)S(1)}) custom-call(s32[2]{0:T(128)S(1)} %pad_add_fusion.place_ref, bf16[1024,256]{1,0:T(8,128)(2,1)S(1)} %pair.3.pair_ref.x_pair, ...), custom_call_target="tpu_custom_call" | custom-call | flops 1073741824 | bytes 4194304 | tf_op jit(solution)/shard_map/middle/pallas_call | solution.py:594
  56.4 11.0 %backward.1 = (f32[16,128,128]{2,1,0:T(8,128)S(1)}, bf16[64,2048]{1,0:T(8,128)(2,1)S(1)}, bf16[256,128]{1,0:T(8,128)(2,1)S(1)}, bf16[256,128]{1,0:T(8,128)(2,1)S...) custom-call(s32[2]{0:T(128)S(1)} %pad_add_fusion.place_ref, ...), custom_call_target="tpu_custom_call" | custom-call | flops 4026531840 | bytes 4194304 | tf_op jit(solution)/shard_map/backward/pallas_call | solution.py:615
  67.4 2.2 %collective-permute-start.14 = (bf16[2,128,128]{2,1,0:T(8,128)(2,1)S(1)}, bf16[2,128,128]{2,1,0:T(8,128)(2,1)S(1)}, u32[]{:S(2)}, u32[]{:S(2)}) collective-permute-start(bf16[2,128,128]{2,1,0:T(8,128)(2,1)S(1)} %get-tuple-element.87), channel_id=1, source_target_pairs={{0,28},{1,13},{2,30},{3,15},{4,24},{5,9},{6,26},{7,11},{8,20},{9,5... | collective-permute-start | bytes 196616 | tf_op jit(solution)/shard_map/ppermute | solution.py:501
  69.6 2.4 %collective-permute-start.15 = (bf16[2,128,128]{2,1,0:T(8,128)(2,1)S(1)}, bf16[2,128,128]{2,1,0:T(8,128)(2,1)S(1)}, u32[]{:S(2)}, u32[]{:S(2)}) collective-permute-start(bf16[2,128,128]{2,1,0:T(8,128)(2,1)S(1)} %get-tuple-element.88), channel_id=1, source_target_pairs={{0,24},{1,9},{2,26},{3,11},{4,28},{5,13},{6,30},{7,15},{8,16},{9,1... | collective-permute-start | bytes 196616 | tf_op jit(solution)/shard_map/ppermute | solution.py:501
  72.0 3.1 %collective-permute-start.17 = (bf16[2,128,128]{2,1,0:T(8,128)(2,1)S(1)}, bf16[2,128,128]{2,1,0:T(8,128)(2,1)S(1)}, u32[]{:S(2)}, u32[]{:S(2)}) collective-permute-start(bf16[2,128,128]{2,1,0:T(8,128)(2,1)S(1)} %get-tuple-element.90), channel_id=1, source_target_pairs={{0,16},{1,29},{2,18},{3,31},{4,20},{5,25},{6,22},{7,27},{8,24},{9,... | collective-permute-start | bytes 196616 | tf_op jit(solution)/shard_map/ppermute | solution.py:501
  75.1 2.7 %collective-permute-start.19 = (bf16[2,128,128]{2,1,0:T(8,128)(2,1)S(1)}, bf16[2,128,128]{2,1,0:T(8,128)(2,1)S(1)}, u32[]{:S(2)}, u32[]{:S(2)}) collective-permute-start(bf16[2,128,128]{2,1,0:T(8,128)(2,1)S(1)} %get-tuple-element.92), channel_id=1, source_target_pairs={{0,8},{1,21},{2,10},{3,23},{4,12},{5,17},{6,14},{7,19},{8,0},{9,29... | collective-permute-start | bytes 196616 | tf_op jit(solution)/shard_map/ppermute | solution.py:501
  79.7 2.2 %collective-permute-done.16.refs_3_ = bf16[2,128,128]{2,1,0:T(8,128)(2,1)S(1)} collective-permute-done((bf16[2,128,128]{2,1,0:T(8,128)(2,1)S(1)}, bf16[2,128,128]{2,1,0:T(8,128)(2,1)S(1)}, u32[]{:S(2)}, u32[]{:S(2)}) %collective-permute-start.16) | collective-permute-done | bytes 65568 | tf_op jit(solution)/shard_map/ppermute | solution.py:501
  83.6 1.4 %collect.1 = (bf16[768,128]{1,0:T(8,128)(2,1)S(1)}, bf16[768,128]{1,0:T(8,128)(2,1)S(1)}, bf16[1536,128]{1,0:T(8,128)(2,1)S(1)}, bf16[64,256]{1,0:T(8,128)(2,1)S...) custom-call(s32[2]{0:T(128)S(1)} %pad_add_fusion.place_ref, ...), custom_call_target="tpu_custom_call" | custom-call | flops 134217728 | bytes 4194304 | tf_op jit(solution)/shard_map/collect/pallas_call | solution.py:642
  85.0 1.5 %collective-permute-start.21 = (bf16[1536,128]{1,0:T(8,128)(2,1)S(1)}, bf16[1536,128]{1,0:T(8,128)(2,1)S(1)}, u32[]{:S(2)}, u32[]{:S(2)}) collective-permute-start(bf16[1536,128]{1,0:T(8,128)(2,1)S(1)} %get-tuple-element.105), channel_id=1, source_target_pairs={{0,2},{1,3},{2,0},{3,1},{4,6},{5,7},{6,4},{7,5},{8,10},{9,11},{10,... | collective-permute-start | bytes 1179656 | tf_op jit(solution)/shard_map/ppermute | solution.py:480
  87.8 3.1 %collective-permute-start.24 = (bf16[64,256]{1,0:T(8,128)(2,1)S(1)}, bf16[64,256]{1,0:T(8,128)(2,1)S(1)}, u32[]{:S(2)}, u32[]{:S(2)}) collective-permute-start(bf16[64,256]{1,0:T(8,128)(2,1)S(1)} %get-tuple-element.109), channel_id=1, source_target_pairs={{0,8},{1,9},{2,10},{3,11},{4,12},{5,13},{6,14},{7,15},{8,0},{9,1},... | collective-permute-start | bytes 98312 | tf_op jit(solution)/shard_map/ppermute | solution.py:501
  93.8 3.7 %collective-permute-done.25 = f32[64,256]{1,0:T(8,128)S(1)} collective-permute-done((f32[64,256]{1,0:T(8,128)S(1)}, f32[64,256]{1,0:T(8,128)S(1)}, u32[]{:S(2)}, u32[]{:S(2)}) %collective-permute-start.25) | collective-permute-done | bytes 65568 | tf_op jit(solution)/shard_map/ppermute | solution.py:480
  97.6 2.1 %collective-permute-start.29 = (bf16[64,256]{1,0:T(8,128)(2,1)S(1)}, bf16[64,256]{1,0:T(8,128)(2,1)S(1)}, u32[]{:S(2)}, u32[]{:S(2)}) collective-permute-start(bf16[64,256]{1,0:T(8,128)(2,1)S(1)} %add_convert_fusion.after_ref.l0), channel_id=1, source_target_pairs={{0,24},{1,25},{2,26},{3,27},{4,28},{5,29},{6,30},{7,31},{8,16},{9,... | collective-permute-start | bytes 98312 | tf_op jit(solution)/shard_map/ppermute | solution.py:501
  (69 shorter events, 22.0 us)
Async XLA Ops:
  0.6 15.2 %collective-permute-start = (bf16[512,256]{1,0:T(8,128)(2,1)}, bf16[512,256]{1,0:T(8,128)(2,1)S(1)}, u32[]{:S(2)}, u32[]{:S(2)}) collective-permute-start(bf16[512,256]{1,0:T(8,128)(2,1)} %refs_0_.2), channel_id=1, source_target_pairs={{0,2},{1,3},{2,0},{3,1},{4,6},{5,7},{6,4},{7,5},{8,10},{9,11},{10,... | collective-permute-start | bytes 786440 | tf_op jit(solution)/shard_map/ppermute | solution.py:480
  17.0 10.8 %collective-permute-start.2 = (bf16[512,256]{1,0:T(8,128)(2,1)S(1)}, bf16[512,256]{1,0:T(8,128)(2,1)S(1)}, u32[]{:S(2)}, u32[]{:S(2)}) collective-permute-start(bf16[512,256]{1,0:T(8,128)(2,1)S(1)} %copy-done.1), channel_id=1, source_target_pairs={{0,2},{1,3},{2,0},{3,1},{4,6},{5,7},{6,4},{7,5},{8,10},{9,11},{10,... | collective-permute-start | bytes 786440 | tf_op jit(solution)/shard_map/ppermute | solution.py:480
  20.1 7.7 %collective-permute-start.3 = (bf16[2,128,128]{2,1,0:T(8,128)(2,1)S(1)}, bf16[2,128,128]{2,1,0:T(8,128)(2,1)S(1)}, u32[]{:S(2)}, u32[]{:S(2)}) collective-permute-start(bf16[2,128,128]{2,1,0:T(8,128)(2,1)S(1)} %get-tuple-element.64), channel_id=1, source_target_pairs={{0,28},{1,13},{2,30},{3,15},{4,24},{5,9},{6,26},{7,11},{8,20},{9,5... | collective-permute-start | bytes 196616 | tf_op jit(solution)/shard_map/ppermute | solution.py:501
  20.7 9.1 %collective-permute-start.4 = (bf16[2,128,128]{2,1,0:T(8,128)(2,1)S(1)}, bf16[2,128,128]{2,1,0:T(8,128)(2,1)S(1)}, u32[]{:S(2)}, u32[]{:S(2)}) collective-permute-start(bf16[2,128,128]{2,1,0:T(8,128)(2,1)S(1)} %get-tuple-element.65), channel_id=1, source_target_pairs={{0,24},{1,9},{2,26},{3,11},{4,28},{5,13},{6,30},{7,15},{8,16},{9,1... | collective-permute-start | bytes 196616 | tf_op jit(solution)/shard_map/ppermute | solution.py:501
  24.0 8.9 %collective-permute-start.5 = (bf16[2,128,128]{2,1,0:T(8,128)(2,1)S(1)}, bf16[2,128,128]{2,1,0:T(8,128)(2,1)S(1)}, u32[]{:S(2)}, u32[]{:S(2)}) collective-permute-start(bf16[2,128,128]{2,1,0:T(8,128)(2,1)S(1)} %get-tuple-element.66), channel_id=1, source_target_pairs={{0,20},{1,5},{2,22},{3,7},{4,16},{5,1},{6,18},{7,3},{8,28},{9,13},... | collective-permute-start | bytes 196616 | tf_op jit(solution)/shard_map/ppermute | solution.py:501
  24.0 11.1 %collective-permute-start.6 = (bf16[2,128,128]{2,1,0:T(8,128)(2,1)S(1)}, bf16[2,128,128]{2,1,0:T(8,128)(2,1)S(1)}, u32[]{:S(2)}, u32[]{:S(2)}) collective-permute-start(bf16[2,128,128]{2,1,0:T(8,128)(2,1)S(1)} %get-tuple-element.67), channel_id=1, source_target_pairs={{0,16},{1,29},{2,18},{3,31},{4,20},{5,25},{6,22},{7,27},{8,24},{9,... | collective-permute-start | bytes 196616 | tf_op jit(solution)/shard_map/ppermute | solution.py:501
  27.8 7.3 %collective-permute-start.7 = (bf16[2,128,128]{2,1,0:T(8,128)(2,1)S(1)}, bf16[2,128,128]{2,1,0:T(8,128)(2,1)S(1)}, u32[]{:S(2)}, u32[]{:S(2)}) collective-permute-start(bf16[2,128,128]{2,1,0:T(8,128)(2,1)S(1)} %get-tuple-element.68), channel_id=1, source_target_pairs={{0,12},{1,25},{2,14},{3,27},{4,8},{5,29},{6,10},{7,31},{8,4},{9,17... | collective-permute-start | bytes 196616 | tf_op jit(solution)/shard_map/ppermute | solution.py:501
  27.8 7.2 %collective-permute-start.8 = (bf16[2,128,128]{2,1,0:T(8,128)(2,1)S(1)}, bf16[2,128,128]{2,1,0:T(8,128)(2,1)S(1)}, u32[]{:S(2)}, u32[]{:S(2)}) collective-permute-start(bf16[2,128,128]{2,1,0:T(8,128)(2,1)S(1)} %get-tuple-element.69), channel_id=1, source_target_pairs={{0,8},{1,21},{2,10},{3,23},{4,12},{5,17},{6,14},{7,19},{8,0},{9,29... | collective-permute-start | bytes 196616 | tf_op jit(solution)/shard_map/ppermute | solution.py:501
  29.8 5.2 %collective-permute-start.9 = (bf16[2,128,128]{2,1,0:T(8,128)(2,1)S(1)}, bf16[2,128,128]{2,1,0:T(8,128)(2,1)S(1)}, u32[]{:S(2)}, u32[]{:S(2)}) collective-permute-start(bf16[2,128,128]{2,1,0:T(8,128)(2,1)S(1)} %get-tuple-element.70), channel_id=1, source_target_pairs={{0,4},{1,17},{2,6},{3,19},{4,0},{5,21},{6,2},{7,23},{8,12},{9,25},... | collective-permute-start | bytes 196616 | tf_op jit(solution)/shard_map/ppermute | solution.py:501
  39.8 6.8 %collective-permute-start.11 = (bf16[512,128]{1,0:T(8,128)(2,1)S(1)}, bf16[512,128]{1,0:T(8,128)(2,1)S(1)}, u32[]{:S(2)}, u32[]{:S(2)}) collective-permute-start(bf16[512,128]{1,0:T(8,128)(2,1)S(1)} %get-tuple-element.77.refs_0_), channel_id=1, source_target_pairs={{0,2},{1,3},{2,0},{3,1},{4,6},{5,7},{6,4},{7,5},{8,10},{9,11},{10,... | collective-permute-start | bytes 393224 | tf_op jit(solution)/shard_map/ppermute | solution.py:480
  44.9 5.5 %collective-permute-start.12 = (bf16[512,128]{1,0:T(8,128)(2,1)S(1)}, bf16[512,128]{1,0:T(8,128)(2,1)S(1)}, u32[]{:S(2)}, u32[]{:S(2)}) collective-permute-start(bf16[512,128]{1,0:T(8,128)(2,1)S(1)} %get-tuple-element.78.refs_1_), channel_id=1, source_target_pairs={{0,2},{1,3},{2,0},{3,1},{4,6},{5,7},{6,4},{7,5},{8,10},{9,11},{10,... | collective-permute-start | bytes 393224 | tf_op jit(solution)/shard_map/ppermute | solution.py:480
  67.4 7.7 %collective-permute-start.14 = (bf16[2,128,128]{2,1,0:T(8,128)(2,1)S(1)}, bf16[2,128,128]{2,1,0:T(8,128)(2,1)S(1)}, u32[]{:S(2)}, u32[]{:S(2)}) collective-permute-start(bf16[2,128,128]{2,1,0:T(8,128)(2,1)S(1)} %get-tuple-element.87), channel_id=1, source_target_pairs={{0,28},{1,13},{2,30},{3,15},{4,24},{5,9},{6,26},{7,11},{8,20},{9,5... | collective-permute-start | bytes 196616 | tf_op jit(solution)/shard_map/ppermute | solution.py:501
  69.6 8.3 %collective-permute-start.15 = (bf16[2,128,128]{2,1,0:T(8,128)(2,1)S(1)}, bf16[2,128,128]{2,1,0:T(8,128)(2,1)S(1)}, u32[]{:S(2)}, u32[]{:S(2)}) collective-permute-start(bf16[2,128,128]{2,1,0:T(8,128)(2,1)S(1)} %get-tuple-element.88), channel_id=1, source_target_pairs={{0,24},{1,9},{2,26},{3,11},{4,28},{5,13},{6,30},{7,15},{8,16},{9,1... | collective-permute-start | bytes 196616 | tf_op jit(solution)/shard_map/ppermute | solution.py:501
  72.0 9.9 %collective-permute-start.16 = (bf16[2,128,128]{2,1,0:T(8,128)(2,1)S(1)}, bf16[2,128,128]{2,1,0:T(8,128)(2,1)S(1)}, u32[]{:S(2)}, u32[]{:S(2)}) collective-permute-start(bf16[2,128,128]{2,1,0:T(8,128)(2,1)S(1)} %get-tuple-element.89), channel_id=1, source_target_pairs={{0,20},{1,5},{2,22},{3,7},{4,16},{5,1},{6,18},{7,3},{8,28},{9,13},... | collective-permute-start | bytes 196616 | tf_op jit(solution)/shard_map/ppermute | solution.py:501
  72.0 10.9 %collective-permute-start.17 = (bf16[2,128,128]{2,1,0:T(8,128)(2,1)S(1)}, bf16[2,128,128]{2,1,0:T(8,128)(2,1)S(1)}, u32[]{:S(2)}, u32[]{:S(2)}) collective-permute-start(bf16[2,128,128]{2,1,0:T(8,128)(2,1)S(1)} %get-tuple-element.90), channel_id=1, source_target_pairs={{0,16},{1,29},{2,18},{3,31},{4,20},{5,25},{6,22},{7,27},{8,24},{9,... | collective-permute-start | bytes 196616 | tf_op jit(solution)/shard_map/ppermute | solution.py:501
  75.1 7.8 %collective-permute-start.18 = (bf16[2,128,128]{2,1,0:T(8,128)(2,1)S(1)}, bf16[2,128,128]{2,1,0:T(8,128)(2,1)S(1)}, u32[]{:S(2)}, u32[]{:S(2)}) collective-permute-start(bf16[2,128,128]{2,1,0:T(8,128)(2,1)S(1)} %get-tuple-element.91), channel_id=1, source_target_pairs={{0,12},{1,25},{2,14},{3,27},{4,8},{5,29},{6,10},{7,31},{8,4},{9,17... | collective-permute-start | bytes 196616 | tf_op jit(solution)/shard_map/ppermute | solution.py:501
  75.1 8.5 %collective-permute-start.19 = (bf16[2,128,128]{2,1,0:T(8,128)(2,1)S(1)}, bf16[2,128,128]{2,1,0:T(8,128)(2,1)S(1)}, u32[]{:S(2)}, u32[]{:S(2)}) collective-permute-start(bf16[2,128,128]{2,1,0:T(8,128)(2,1)S(1)} %get-tuple-element.92), channel_id=1, source_target_pairs={{0,8},{1,21},{2,10},{3,23},{4,12},{5,17},{6,14},{7,19},{8,0},{9,29... | collective-permute-start | bytes 196616 | tf_op jit(solution)/shard_map/ppermute | solution.py:501
  77.9 5.7 %collective-permute-start.20 = (bf16[2,128,128]{2,1,0:T(8,128)(2,1)S(1)}, bf16[2,128,128]{2,1,0:T(8,128)(2,1)S(1)}, u32[]{:S(2)}, u32[]{:S(2)}) collective-permute-start(bf16[2,128,128]{2,1,0:T(8,128)(2,1)S(1)} %get-tuple-element.93), channel_id=1, source_target_pairs={{0,4},{1,17},{2,6},{3,19},{4,0},{5,21},{6,2},{7,23},{8,12},{9,25},... | collective-permute-start | bytes 196616 | tf_op jit(solution)/shard_map/ppermute | solution.py:501
  85.0 12.5 %collective-permute-start.21 = (bf16[1536,128]{1,0:T(8,128)(2,1)S(1)}, bf16[1536,128]{1,0:T(8,128)(2,1)S(1)}, u32[]{:S(2)}, u32[]{:S(2)}) collective-permute-start(bf16[1536,128]{1,0:T(8,128)(2,1)S(1)} %get-tuple-element.105), channel_id=1, source_target_pairs={{0,2},{1,3},{2,0},{3,1},{4,6},{5,7},{6,4},{7,5},{8,10},{9,11},{10,... | collective-permute-start | bytes 1179656 | tf_op jit(solution)/shard_map/ppermute | solution.py:480
  86.5 5.8 %collective-permute-start.22 = (bf16[64,256]{1,0:T(8,128)(2,1)S(1)}, bf16[64,256]{1,0:T(8,128)(2,1)S(1)}, u32[]{:S(2)}, u32[]{:S(2)}) collective-permute-start(bf16[64,256]{1,0:T(8,128)(2,1)S(1)} %get-tuple-element.107), channel_id=1, source_target_pairs={{0,24},{1,25},{2,26},{3,27},{4,28},{5,29},{6,30},{7,31},{8,16},{9,... | collective-permute-start | bytes 98312 | tf_op jit(solution)/shard_map/ppermute | solution.py:501
  87.8 5.3 %collective-permute-start.23 = (bf16[64,256]{1,0:T(8,128)(2,1)S(1)}, bf16[64,256]{1,0:T(8,128)(2,1)S(1)}, u32[]{:S(2)}, u32[]{:S(2)}) collective-permute-start(bf16[64,256]{1,0:T(8,128)(2,1)S(1)} %get-tuple-element.108), channel_id=1, source_target_pairs={{0,16},{1,17},{2,18},{3,19},{4,20},{5,21},{6,22},{7,23},{8,24},{9,... | collective-permute-start | bytes 98312 | tf_op jit(solution)/shard_map/ppermute | solution.py:501
  87.8 5.4 %collective-permute-start.24 = (bf16[64,256]{1,0:T(8,128)(2,1)S(1)}, bf16[64,256]{1,0:T(8,128)(2,1)S(1)}, u32[]{:S(2)}, u32[]{:S(2)}) collective-permute-start(bf16[64,256]{1,0:T(8,128)(2,1)S(1)} %get-tuple-element.109), channel_id=1, source_target_pairs={{0,8},{1,9},{2,10},{3,11},{4,12},{5,13},{6,14},{7,15},{8,0},{9,1},... | collective-permute-start | bytes 98312 | tf_op jit(solution)/shard_map/ppermute | solution.py:501
  97.6 6.2 %collective-permute-start.29 = (bf16[64,256]{1,0:T(8,128)(2,1)S(1)}, bf16[64,256]{1,0:T(8,128)(2,1)S(1)}, u32[]{:S(2)}, u32[]{:S(2)}) collective-permute-start(bf16[64,256]{1,0:T(8,128)(2,1)S(1)} %add_convert_fusion.after_ref.l0), channel_id=1, source_target_pairs={{0,24},{1,25},{2,26},{3,27},{4,28},{5,29},{6,30},{7,31},{8,16},{9,... | collective-permute-start | bytes 98312 | tf_op jit(solution)/shard_map/ppermute | solution.py:501
  99.7 5.2 %collective-permute-start.28 = (bf16[64,256]{1,0:T(8,128)(2,1)S(1)}, bf16[64,256]{1,0:T(8,128)(2,1)S(1)}, u32[]{:S(2)}, u32[]{:S(2)}) collective-permute-start(bf16[64,256]{1,0:T(8,128)(2,1)S(1)} %add_convert_fusion.after_ref.l0), channel_id=1, source_target_pairs={{0,16},{1,17},{2,18},{3,19},{4,20},{5,21},{6,22},{7,23},{8,24},{9,... | collective-permute-start | bytes 98312 | tf_op jit(solution)/shard_map/ppermute | solution.py:501
  (13 other events, 48.1 us)
